TPU v7x, 512 devices: a whole 4x4x16 slice. The times are simulated.
512 devices in a mesh: row: 16 (over x_lo, y, core), col: 32 (over z, x_hi).
Axes of the slice: x: 4 (x_hi: 2, x_lo: 2; x = x_hi * 2 + x_lo), y: 4, z: 16, core: 2. Of those that a mesh axis runs over, the one named last changes fastest.
Arguments:
- pair: bfloat16 [384, 384, 128], P('row', 'col'), may hold values from -6 to 6
- crop: int32 [384], replicated, may hold values from 0 to 3, never falling along the last dimension, each value on 1 to 192 neighbouring positions
- in_gain: float32 [128], replicated, may hold values from 0.25 to 1.75
- in_bias: float32 [128], replicated, may hold values from -2 to 2
- in_weights: bfloat16 [128, 640], replicated, may hold values from -0.5 to 0.5
- out_gain: float32 [128], replicated, may hold values from 0.25 to 1.75
- out_bias: float32 [128], replicated, may hold values from -2 to 2
- out_weights: bfloat16 [128, 128], replicated, may hold values from -0.5 to 0.5
- cotangent: bfloat16 [384, 384, 128], P('row', 'col'), may hold values from -6 to 6
Outputs:
- update: bfloat16 [384, 384, 128], P('row', 'col')
- pair_grad: bfloat16 [384, 384, 128], P('row', 'col')
Inputs may be any that keep to these rules, and one draw needn't show every extreme that they name: crop numbers never fall along the row; every crop is 1 to 192 residues long, and one crop is exactly 192 long.
All inputs are finite; a program needn't handle non-finite values.
Results may differ from a plain program's by a relative error of at most 0.0076.
Values may be sent and summed in bfloat16 or wider, within the bound.
No kernel may reach another device: no remote copies, remote signals or barrier semaphores. Data moves between devices by JAX's collectives and lax.ppermute only.
A program may use at most 128 MiB of HBM per device.

v0:
```python
import jax
import jax.numpy as jnp
from jax import lax
from jax.sharding import PartitionSpec as P

norm_eps = 1e-05


def from_root(value, axis, source):
    kept = jnp.where(lax.axis_index(axis) == source, value, 0).astype(value.dtype)
    return lax.psum(kept, axis)


def normalize(values):
    average = jnp.mean(values, axis=-1, keepdims=True)
    centered = values - average
    inv_std = lax.rsqrt(jnp.mean(centered * centered, axis=-1, keepdims=True) + norm_eps)
    return (centered * inv_std, inv_std)


def norm_back(upstream_grad, normalized, inv_std):
    first_mean = jnp.mean(upstream_grad, axis=-1, keepdims=True)
    second_mean = jnp.mean(upstream_grad * normalized, axis=-1, keepdims=True)
    return inv_std * (upstream_grad - first_mean - normalized * second_mean)


def contract(einsum_form, first_op, second_op):
    return jnp.einsum(einsum_form, first_op, second_op, preferred_element_type=jnp.float32)


def body(pair, crop, in_gain, in_bias, in_weights, out_gain, out_bias, out_weights, cotangent):
    tile_rows, tile_cols, pair_width = pair.shape
    hidden_width = out_weights.shape[0]
    col_per_row = lax.axis_size("col") // lax.axis_size("row")
    row_pos = lax.axis_index("row")
    col_pos = lax.axis_index("col")
    crop_rows = lax.dynamic_slice_in_dim(crop, row_pos * tile_rows, tile_rows)
    crop_cols = lax.dynamic_slice_in_dim(crop, col_pos * tile_cols, tile_cols)
    same_crop = crop_rows[:, None] == crop_cols[None, :]
    inside = same_crop.astype(jnp.float32)[:, :, None]
    pair_hat, inv_in = normalize(pair.astype(jnp.float32))
    normed = (pair_hat * in_gain + in_bias).astype(jnp.bfloat16)
    projected = jnp.dot(
        normed.reshape(tile_rows * tile_cols, pair_width),
        in_weights,
        preferred_element_type=jnp.float32,
    )
    projected = projected.reshape(tile_rows, tile_cols, -1)
    left_val = projected[:, :, :hidden_width]
    right_val = projected[:, :, hidden_width : 2 * hidden_width]
    left_sig = jax.nn.sigmoid(projected[:, :, 2 * hidden_width : 3 * hidden_width])
    right_sig = jax.nn.sigmoid(projected[:, :, 3 * hidden_width : 4 * hidden_width])
    gate = jax.nn.sigmoid(projected[:, :, 4 * hidden_width :])
    left_gated = (inside * left_sig * left_val).astype(jnp.bfloat16)
    right_gated = (inside * right_sig * right_val).astype(jnp.bfloat16)
    left_cols, right_cols = (
        lax.all_gather(left_gated, "row", axis=0, tiled=True),
        lax.all_gather(right_gated, "row", axis=0, tiled=True),
    )
    mirror_parts = []
    for piece_index in range(col_per_row):
        mirror_parts.append(from_root(left_cols, "col", row_pos * col_per_row + piece_index))
    mirrored = jnp.concatenate(mirror_parts, axis=1)
    tri = contract("kih,kjh->ijh", mirrored, right_cols)
    tri_hat, inv_out = normalize(tri)
    normed_out = (tri_hat * out_gain + out_bias).astype(jnp.bfloat16)
    gated_value = jnp.dot(
        normed_out.reshape(-1, hidden_width), out_weights, preferred_element_type=jnp.float32
    )
    gated_value = gated_value.reshape(tile_rows, tile_cols, pair_width)
    update = (gate * gated_value).astype(jnp.bfloat16)
    upstream = cotangent.astype(jnp.float32)
    d_value = (upstream * gate).astype(jnp.bfloat16)
    d_outpre = upstream * gated_value * gate * (1.0 - gate)
    d_normed = jnp.dot(
        d_value.reshape(-1, pair_width), out_weights.T, preferred_element_type=jnp.float32
    )
    d_normed = d_normed.reshape(tile_rows, tile_cols, hidden_width)
    d_tri = norm_back(d_normed * out_gain, tri_hat, inv_out).astype(jnp.bfloat16)
    left_rows, right_rows, grad_rows = (
        lax.all_gather(left_gated, "col", axis=1, tiled=True),
        lax.all_gather(right_gated, "col", axis=1, tiled=True),
        lax.all_gather(d_tri, "col", axis=1, tiled=True),
    )
    grad_cols = lax.all_gather(d_tri, "row", axis=0, tiled=True)
    d_right = contract("kih,ijh->kjh", left_rows, grad_cols)
    own_rows = lax.dynamic_slice_in_dim(grad_rows, col_pos % col_per_row * tile_cols, tile_cols, 0)
    grad_mirror = from_root(own_rows, "row", col_pos // col_per_row)
    d_left = contract("kjh,ijh->kih", right_rows, grad_mirror)
    d_proj = jnp.concatenate(
        [
            d_left * inside * left_sig,
            d_right * inside * right_sig,
            d_left * inside * left_val * left_sig * (1.0 - left_sig),
            d_right * inside * right_val * right_sig * (1.0 - right_sig),
            d_outpre,
        ],
        axis=-1,
    ).astype(jnp.bfloat16)
    d_normed_in = jnp.dot(
        d_proj.reshape(tile_rows * tile_cols, -1), in_weights.T, preferred_element_type=jnp.float32
    )
    d_normed_in = d_normed_in.reshape(tile_rows, tile_cols, pair_width)
    pair_grad = norm_back(d_normed_in * in_gain, pair_hat, inv_in).astype(jnp.bfloat16)
    return (update, pair_grad)


def solution(mesh):
    in_specs = (P("row", "col", None), P(), P(), P(), P(), P(), P(), P(), P("row", "col", None))
    out_specs = (P("row", "col", None), P("row", "col", None))
    return jax.shard_map(body, mesh=mesh, in_specs=in_specs, out_specs=out_specs, check_vma=False)
```

profile of v0, /device:TPU:1, one launch (start us, length us, event | category | flops | bytes accessed | tf_op | source)
XLA Modules:
  0.0 1073.1 jit_solution(18351010488392321802)
XLA Ops:
  7.2 0.8 dynamic_slice.10
  8.0 0.8 dynamic_slice.9
  8.8 1.0 convert_reduce_fusion
  9.8 1.1 fusion.14
  11.0 1.3 fusion.6
  12.2 0.8 multiply_convert_fusion.6
  13.1 0.7 all-gather.7.cloned.1.call-update
  13.8 45.4 %all-gather.9.cloned.1.call-done = bf16[384,12,128]{2,0,1:T(8,128)(2,1)} async-done(((bf16[24,12,128]{2,0,1:T(8,128)(2,1)}), bf16[384,12,128]{2,0,1:T(8,128)(2,1)}) %all-gather.9.cloned.1.call-update) | async-done | bytes 1179664 | tf_op jit(solution)/shard_map/all_gather | solution.py:57
  59.2 2.9 broadcast_select_fusion.2
  62.2 40.3 %all-gather.7.cloned.1.call-done = bf16[384,12,128]{2,0,1:T(8,128)(2,1)} async-done(((bf16[24,12,128]{2,0,1:T(8,128)(2,1)}), bf16[384,12,128]{2,0,1:T(8,128)(2,1)}) %all-gather.7.cloned.1.call-update) | async-done | bytes 1179664 | tf_op jit(solution)/shard_map/all_gather | solution.py:58
  102.4 3.0 copy.32
  105.4 296.4 %all-reduce.6.cloned.1.call-done = (bf16[384,12,128]{2,0,1:T(8,128)(2,1)}, bf16[384,12,128]{2,0,1:T(8,128)(2,1)}) async-done(((bf16[384,12,128]{2,0,1:T(8,128)(2,1)}, bf16[384,12,128]{2,0,1:T(8,128)(2,1)}), (bf16[384,12,128]{2,0,1:T(8,128)(2,1)}, bf16[384,12,128]{2,0,1:T(8,128)(2,1)})) %all-reduce.6.cloned.1.call-update) | async-done | bytes 2359312 | tf_op jit(solution)/shard_map/psum | solution.py:11
  401.8 1.8 pad_maximum_fusion
  403.7 2.9 copy.33
  406.5 3.2 fusion.50
  410.7 0.9 multiply_convert_fusion.4
  412.8 0.7 all-gather.15.cloned.1.call-update
  413.8 156.7 %all-gather.11.cloned.1.call-done = bf16[24,384,128]{2,0,1:T(8,128)(2,1)} async-done(((bf16[24,12,128]{2,0,1:T(8,128)(2,1)}), bf16[24,384,128]{2,0,1:T(8,128)(2,1)}) %all-gather.11.cloned.1.call-update) | async-done | bytes 2359312 | tf_op jit(solution)/shard_map/all_gather | solution.py:83
  570.5 2.4 constant_dynamic-slice_fusion
  573.0 2.5 copy.41
  575.4 1.4 broadcast_select_fusion
  576.8 143.9 %all-gather.13.cloned.1.call-done = bf16[24,384,128]{2,0,1:T(8,128)(2,1)} async-done(((bf16[24,12,128]{2,0,1:T(8,128)(2,1)}), bf16[24,384,128]{2,0,1:T(8,128)(2,1)}) %all-gather.13.cloned.1.call-update) | async-done | bytes 2359312 | tf_op jit(solution)/shard_map/all_gather | solution.py:82
  720.7 10.9 %copy.36 = bf16[24,384,128]{0,1,2:T(8,128)(2,1)} copy(bf16[24,384,128]{2,0,1:T(8,128)(2,1)} %all-gather.13.cloned.1.call-done) | data formatting | bytes 4718592 | tf_op jit(solution)/shard_map/all_gather | solution.py:82
  731.6 139.3 %all-gather.17.cloned.1.call-done = bf16[24,384,128]{2,0,1:T(8,128)(2,1)} async-done(((bf16[24,12,128]{2,0,1:T(8,128)(2,1)}), bf16[24,384,128]{2,0,1:T(8,128)(2,1)}) %all-gather.17.cloned.1.call-update) | async-done | bytes 2359312 | tf_op jit(solution)/shard_map/all_gather | solution.py:81
  870.8 10.8 %copy.39 = bf16[24,384,128]{0,1,2:T(8,128)(2,1)} copy(bf16[24,384,128]{2,0,1:T(8,128)(2,1)} %all-gather.17.cloned.1.call-done) | data formatting | bytes 4718592 | tf_op jit(solution)/shard_map/all_gather | solution.py:81
  881.7 1.0 multiply_convert_fusion.5
  882.6 34.9 %all-gather.15.cloned.1.call-done = bf16[384,12,128]{2,0,1:T(8,128)(2,1)} async-done(((bf16[24,12,128]{2,0,1:T(8,128)(2,1)}), bf16[384,12,128]{2,0,1:T(8,128)(2,1)}) %all-gather.15.cloned.1.call-update) | async-done | bytes 1179664 | tf_op jit(solution)/shard_map/all_gather | solution.py:85
  917.5 2.2 copy.38
  919.7 5.8 fusion.52
  925.9 130.7 %all-reduce.4.cloned.1.call-done = bf16[12,384,128]{1,0,2:T(8,128)(2,1)} async-done(((bf16[12,384,128]{1,0,2:T(8,128)(2,1)}), bf16[12,384,128]{1,0,2:T(8,128)(2,1)}) %all-reduce.4.cloned.1.call-update) | async-done | bytes 1179664 | tf_op jit(solution)/shard_map/psum | solution.py:11
  1056.5 7.3 fusion.51
  1065.4 0.9 fusion.13
  (52 shorter events, 4.4 us)
Async XLA Ops:
  7.2 3.8 copy-start
  7.2 52.0 %all-gather.9.cloned.1.call-start = ((), (), s32[]{:S(2)}) async-start(), calls=%async_computation.1 | async-start | bytes 1253376 | tf_op jit(solution)/shard_map/all_gather | solution.py:57
  13.0 89.4 %all-gather.7.cloned.1.call-start = ((), (), s32[]{:S(2)}) async-start(), calls=%async_computation | async-start | bytes 1253376 | tf_op jit(solution)/shard_map/all_gather | solution.py:58
  13.8 388.1 %all-reduce.6.cloned.1.call-start = ((), (), s32[]{:S(2)}) async-start(), calls=%async_computation.7 | async-start | bytes 4718592 | tf_op jit(solution)/shard_map/psum | solution.py:11
  62.1 508.4 %all-gather.11.cloned.1.call-start = ((), (), s32[]{:S(2)}) async-start(), calls=%async_computation.2 | async-start | bytes 2433024 | tf_op jit(solution)/shard_map/all_gather | solution.py:83
  406.5 3.9 copy-start.3
  406.5 3.9 copy-start.6
  406.5 3.9 copy-start.8
  411.6 309.1 %all-gather.13.cloned.1.call-start = ((), (), s32[]{:S(2)}) async-start(), calls=%async_computation.4 | async-start | bytes 2433024 | tf_op jit(solution)/shard_map/all_gather | solution.py:82
  412.2 458.6 %all-gather.17.cloned.1.call-start = ((), (), s32[]{:S(2)}) async-start(), calls=%async_computation.6 | async-start | bytes 2433024 | tf_op jit(solution)/shard_map/all_gather | solution.py:81
  412.8 504.7 %all-gather.15.cloned.1.call-start = ((), (), s32[]{:S(2)}) async-start(), calls=%async_computation.5 | async-start | bytes 1253376 | tf_op jit(solution)/shard_map/all_gather | solution.py:85
  413.5 643.0 %all-reduce.4.cloned.1.call-start = ((), (), s32[]{:S(2)}) async-start(), calls=%async_computation.3 | async-start | bytes 3145728 | tf_op jit(solution)/shard_map/psum | solution.py:11
  731.6 150.1 %copy-start.7 = (f32[128]{0:T(128)S(1)}, f32[128]{0:T(128)}, u32[]{:S(2)}) copy-start(f32[128]{0:T(128)} %param.15) | copy-start | bytes 1540
  1063.9 0.9 copy-start.2
  1063.9 1.0 copy-start.4
  1063.9 1.0 copy-start.1
  1063.9 1.0 copy-start.5
Sparse Core Ops, SparseCore 0:
  13.1 46.0 all-gather.8
  61.9 40.5 all-gather.6
  105.4 296.3 all-reduce.5
  411.7 158.7 all-gather.10
  574.1 146.5 all-gather.12
  724.2 146.5 all-gather.16
  872.9 44.5 all-gather.14
  920.5 136.0 all-reduce.3
where the time goes:
time: 1070 us
  waiting for transfers between devices  990 us (93%)
  local copies, waits for them, and re-layouts  37.3 us (3%)
  matrix products  19.2 us (2%)
  between operations  14.4 us (1%)
  other arithmetic  11.6 us (1%)
    psum x2, waiting for transfers between devices, from_root(): return lax.psum(kept, axis)  427 us
    all_gather x1, waiting for transfers between devices, body(): lax.all_gather(d_tri, 'col', axis=1, tiled=True)  157 us
    all_gather x1, waiting for transfers between devices, body(): lax.all_gather(right_gated, 'col', axis=1, tiled=True)  144 us
    all_gather x1, waiting for transfers between devices, body(): lax.all_gather(left_gated, 'col', axis=1, tiled=True)  139 us
    all_gather x1, waiting for transfers between devices, body(): lax.all_gather(left_gated, 'row', axis=0, tiled=True)  45.4 us
    all_gather x1, waiting for transfers between devices, body(): lax.all_gather(right_gated, 'row', axis=0, tiled=True)  40.3 us
    all_gather x1, waiting for transfers between devices, body(): grad_cols = lax.all_gather(d_tri, 'row', axis=0, tiled=True)  34.9 us
  transfers between devices with their start and end apart: 8, of which 8 were waited for; matrix products, arithmetic and copies ran while one was open for 4% of the time, Pallas kernels for 0%

commit v1 on v0

v1 whole, which is shorter than its diff:
```python
import jax
import jax.numpy as jnp
from jax import lax
from jax.experimental import pallas as pl
from jax.experimental.pallas import tpu as pltpu
from jax.sharding import Mesh, PartitionSpec as P

norm_eps = 1e-05
f32 = jnp.float32
bf16 = jnp.bfloat16
ROWS = ("xlo", "y", "core")
COLS = ("zhi", "zlo", "xhi")
OWNERS = ("zlo", "xhi", "xlo", "y", "core")
TK, TI, PAD = 24, 12, 16
LANES = TK * PAD
E, R, Q = 8, 16, 4
C = 128
N = 384
FOLD = N // 2
RF = R // 2


def dot(first_op, second_op, dims):
    return lax.dot_general(first_op, second_op, (dims, ((), ())), preferred_element_type=f32)


def swap_blocks(parts):
    parts = list(parts)
    block = lax.broadcasted_iota(jnp.int32, parts[0].shape, 1) // PAD
    for step in (4, 2, 1):
        upper = (block & step) != 0
        for a in range(8):
            if a & step:
                continue
            b = a | step
            low, high = parts[a], parts[b]
            parts[a] = jnp.where(upper, pltpu.roll(high, step * PAD, 1), low)
            parts[b] = jnp.where(upper, high, pltpu.roll(low, 128 - step * PAD, 1))
    return parts


def as_column(row):
    return jnp.broadcast_to(row, (C, C)).T[:, :1]


def padded_rows(tile, scratch):
    scratch[...] = jnp.zeros_like(scratch)
    scratch[:, :TI, :] = tile.astype(f32)
    return scratch[...].reshape(LANES, C)


def norm_rows(values):
    centered = values - jnp.mean(values, axis=1, keepdims=True)
    inv_std = lax.rsqrt(jnp.mean(centered * centered, axis=1, keepdims=True) + norm_eps)
    return centered * inv_std, inv_std


def put_channels(scratch, values, slot, stride):
    for t in range(3):
        scratch[pl.ds(slot + t, C, stride=stride), :] = values[:, 128 * t : 128 * (t + 1)]
    scratch[pl.ds(slot + 3, C, stride=stride), :] = jnp.zeros((C, 128), f32)


def get_channels(scratch, slot, stride):
    return jnp.concatenate(
        [scratch[pl.ds(slot + t, C, stride=stride), :] for t in range(3)], axis=1
    )


def project_kernel(pair, crop, gain, bias, weights, send, projected, inside, padded, slots):
    row_pos = lax.axis_index(ROWS)
    col_pos = lax.axis_index(COLS)
    lane = lax.broadcasted_iota(jnp.int32, (N, LANES), 1)
    residue = lax.broadcasted_iota(jnp.int32, (N, LANES), 0)
    crops = jnp.broadcast_to(crop[...].astype(f32), (8, N)).astype(bf16)
    pick_row = (residue == row_pos * TK + lane // PAD).astype(f32).astype(bf16)
    pick_col = (residue == col_pos * TI + lane % PAD).astype(f32).astype(bf16)
    crop_rows = dot(crops, pick_row, ((1,), (0,)))
    crop_cols = dot(crops, pick_col, ((1,), (0,)))
    lane8 = lax.broadcasted_iota(jnp.int32, (8, LANES), 1)
    same = (crop_rows == crop_cols) & (lane8 % PAD < TI)
    inside[...] = same.astype(f32)
    mask = same.astype(f32)[:1, :]

    hat, _ = norm_rows(padded_rows(pair[...], padded))
    normed = (hat * gain[...] + bias[...]).astype(bf16)
    proj = dot(weights[...].T, normed, ((1,), (1,)))
    projected[...] = proj
    left = mask * jax.nn.sigmoid(proj[2 * C : 3 * C]) * proj[:C]
    right = mask * jax.nn.sigmoid(proj[3 * C : 4 * C]) * proj[C : 2 * C]
    put_channels(slots, left, 0, 8)
    put_channels(slots, right, 4, 8)
    send[...] = slots[...].astype(bf16)


def collect_kernel(received, left, right, slots):
    slots[...] = received[...].astype(f32)
    parts = [
        jnp.concatenate(
            [
                slots[pl.ds(8 * R * e + 4 * side + t, R, stride=8), :]
                for side in range(2)
                for t in range(3)
            ],
            axis=0,
        )
        for e in range(E)
    ]
    parts = swap_blocks(parts)
    for side, out in enumerate((left, right)):
        pieces = []
        for t in range(3):
            for k in range(8):
                at = (3 * side + t) * R
                pieces.append(parts[k][at : at + RF] + parts[k][at + RF : at + R])
        out[...] = jnp.concatenate(pieces, axis=0).astype(bf16)


def reorder(transposed):
    shape = (N, Q * 128) if transposed else (Q * 128, N)
    wide = lax.broadcasted_iota(jnp.int32, shape, 1 if transposed else 0)
    target = lax.broadcasted_iota(jnp.int32, shape, 0 if transposed else 1)
    e = (wide // PAD) % E
    within = (e % 2) * TI + wide % PAD
    position = (wide // 128) * 4 + e // 2
    hit = (target == within * R + position) & (wide % PAD < TI)
    return hit.astype(f32).astype(bf16)


def triangle_kernel(left_all, right, send, slots):
    tri = jnp.concatenate(
        [dot(left_all[q], right[...], ((0,), (0,))) for q in range(Q)], axis=0
    ).astype(bf16)
    tri = dot(reorder(True), tri, ((1,), (0,)))
    parts = [
        jnp.concatenate([tri[(8 * t + i) * R : (8 * t + i + 1) * R] for t in range(3)], axis=0)
        for i in range(8)
    ]
    parts = swap_blocks(parts)
    for e in range(E):
        for t in range(3):
            slots[pl.ds(4 * R * e + t, R, stride=4), :] = parts[e][t * R : (t + 1) * R]
        slots[pl.ds(4 * R * e + 3, R, stride=4), :] = jnp.zeros((R, 128), f32)
    send[...] = slots[...].astype(bf16)


def output_kernel(
    received, out_pre, inside, cotangent, gain, bias, weights, update, d_outpre, send, padded, slots
):
    mask = inside[:1, :]
    slots[...] = received[...].astype(f32)
    tri = jnp.where(mask > 0, get_channels(slots, 0, 4), 0.0)
    centered = tri - jnp.mean(tri, axis=0, keepdims=True)
    inv_out = lax.rsqrt(jnp.mean(centered * centered, axis=0, keepdims=True) + norm_eps)
    tri_hat = centered * inv_out
    gain_col = as_column(gain[...])
    normed_out = (tri_hat * gain_col + as_column(bias[...])).astype(bf16)
    gated_value = dot(weights[...].T, normed_out, ((1,), (0,)))
    gate = jax.nn.sigmoid(out_pre[...])
    new = (gate * gated_value).T.reshape(TK, PAD, C)
    update[...] = new[:, :TI, :].astype(bf16)
    upstream = padded_rows(cotangent[...], padded).T
    d_value = (upstream * gate).astype(bf16)
    d_outpre[...] = (upstream * gated_value * gate * (1.0 - gate)).astype(bf16)
    grad = dot(weights[...], d_value, ((1,), (0,))) * gain_col
    first_mean = jnp.mean(grad, axis=0, keepdims=True)
    second_mean = jnp.mean(grad * tri_hat, axis=0, keepdims=True)
    d_tri = inv_out * (grad - first_mean - tri_hat * second_mean)
    put_channels(slots, jnp.where(mask > 0, d_tri, 0.0), 0, 4)
    send[...] = slots[...].astype(bf16)


def back_kernel(received, left_all, right, d_right, send, slots):
    slots[...] = received[...].astype(f32)
    parts = [
        jnp.concatenate(
            [slots[pl.ds(4 * R * e + t, R, stride=4), :] for t in range(3)], axis=0
        )
        for e in range(E)
    ]
    parts = swap_blocks(parts)
    d_tri = jnp.concatenate(
        [parts[i][t * R : (t + 1) * R] for t in range(3) for i in range(8)], axis=0
    ).astype(bf16)
    d_tri = dot(reorder(False), d_tri, ((1,), (0,))).astype(bf16)
    total = jnp.zeros((FOLD, 128), f32)
    for q in range(Q):
        block = d_tri[128 * q : 128 * (q + 1)]
        total = total + dot(left_all[q], block, ((1,), (0,)))
        send[q] = dot(right[...], block, ((1,), (1,))).astype(bf16)
    d_right[...] = total


def spread_kernel(received, d_right, send, slots):
    d_left = received[0].astype(f32)
    for q in range(1, Q):
        d_left = d_left + received[q].astype(f32)
    sides = (d_left, d_right[...])
    parts = [
        jnp.concatenate(
            [
                sides[side][(8 * t + k) * RF : (8 * t + k + 1) * RF]
                for side in range(2)
                for t in range(3)
            ],
            axis=0,
        )
        for k in range(8)
    ]
    parts = swap_blocks(parts)
    for e in range(E):
        for side in range(2):
            for t in range(3):
                piece = parts[e][(3 * side + t) * RF : (3 * side + t + 1) * RF]
                for half in range(2):
                    start = 8 * (R * e + RF * half) + 4 * side + t
                    slots[pl.ds(start, RF, stride=8), :] = piece
            slots[pl.ds(8 * R * e + 4 * side + 3, R, stride=8), :] = jnp.zeros((R, 128), f32)
    send[...] = slots[...].astype(bf16)


def input_kernel(
    received, projected, inside, d_outpre, pair, gain, weights, pair_grad, padded, slots
):
    slots[...] = received[...].astype(f32)
    mask = inside[:1, :]
    d_left = get_channels(slots, 0, 8) * mask
    d_right = get_channels(slots, 4, 8) * mask
    left_val, right_val = projected[:C], projected[C : 2 * C]
    left_sig = jax.nn.sigmoid(projected[2 * C : 3 * C])
    right_sig = jax.nn.sigmoid(projected[3 * C : 4 * C])
    d_proj = jnp.concatenate(
        [
            (d_left * left_sig).astype(bf16),
            (d_right * right_sig).astype(bf16),
            (d_left * left_val * left_sig * (1.0 - left_sig)).astype(bf16),
            (d_right * right_val * right_sig * (1.0 - right_sig)).astype(bf16),
            d_outpre[...],
        ],
        axis=0,
    )
    grad = dot(weights[...], d_proj, ((1,), (0,))).T * gain[...]
    hat, inv_in = norm_rows(padded_rows(pair[...], padded))
    first_mean = jnp.mean(grad, axis=1, keepdims=True)
    second_mean = jnp.mean(grad * hat, axis=1, keepdims=True)
    result = (inv_in * (grad - first_mean - hat * second_mean)).reshape(TK, PAD, C)
    pair_grad[...] = result[:, :TI, :].astype(bf16)


def call(kernel, outs, scratch, *operands):
    return pl.pallas_call(
        kernel,
        out_shape=[jax.ShapeDtypeStruct(shape, dtype) for shape, dtype in outs],
        in_specs=[pl.BlockSpec(memory_space=pltpu.VMEM)] * len(operands),
        out_specs=[pl.BlockSpec(memory_space=pltpu.VMEM)] * len(outs),
        scratch_shapes=[pltpu.VMEM(shape, f32) for shape in scratch],
        compiler_params=pltpu.CompilerParams(vmem_limit_bytes=40 * 1024 * 1024),
        name=kernel.__name__,
    )(*operands)


def exchange(values, height):
    moved = lax.all_to_all(values.reshape(C, height, 128), OWNERS, 0, 0, tiled=True)
    return moved.reshape(C * height, 128)


def body(pair, crop, in_gain, in_bias, in_weights, out_gain, out_bias, out_weights, cotangent):
    tile = (TK, PAD, C)
    in_gain, in_bias, out_gain, out_bias = (
        v.reshape(1, C) for v in (in_gain, in_bias, out_gain, out_bias)
    )
    send, projected, inside = call(
        project_kernel,
        [((8 * C, 128), bf16), ((5 * C, LANES), f32), ((8, LANES), f32)],
        [tile, (8 * C, 128)],
        pair, crop.reshape(1, N), in_gain, in_bias, in_weights,
    )
    left, right = call(
        collect_kernel,
        [((FOLD, 128), bf16)] * 2,
        [(8 * C, 128)],
        exchange(send, 8),
    )
    left_all = lax.all_gather(left, "zhi", axis=0)
    (send,) = call(
        triangle_kernel, [((4 * C, 128), bf16)], [(4 * C, 128)], left_all, right
    )
    update, d_outpre, send = call(
        output_kernel,
        [((TK, TI, C), bf16), ((C, LANES), bf16), ((4 * C, 128), bf16)],
        [tile, (4 * C, 128)],
        exchange(send, 4), projected[4 * C :], inside, cotangent, out_gain, out_bias, out_weights,
    )
    d_right, send = call(
        back_kernel,
        [((FOLD, 128), f32), ((Q, FOLD, 128), bf16)],
        [(4 * C, 128)],
        exchange(send, 4), left_all, right,
    )
    partial = lax.all_to_all(send, "zhi", 0, 0, tiled=True)
    (send,) = call(
        spread_kernel, [((8 * C, 128), bf16)], [(8 * C, 128)], partial, d_right
    )
    (pair_grad,) = call(
        input_kernel,
        [((TK, TI, C), bf16)],
        [tile, (8 * C, 128)],
        exchange(send, 8), projected, inside, d_outpre, pair, in_gain, in_weights,
    )
    return update, pair_grad


def solution(mesh):
    split = Mesh(mesh.devices.reshape(2, 4, 2, 4, 4, 2), ROWS + COLS)
    tiles = P(ROWS, COLS, None)
    in_specs = (tiles, P(), P(), P(), P(), P(), P(), P(), tiles)
    return jax.shard_map(
        body, mesh=split, in_specs=in_specs, out_specs=(tiles, tiles), check_vma=False
    )
```

time: 1070 us -> 138 us (0.13)
  waiting for transfers between devices: 990 us -> 22.8 us
  blocking collectives: 0 us -> 82.6 us
  local copies, waits for them, and re-layouts: 37.3 us -> 4.29 us
  starting transfers between devices: 0.5 us -> 21.4 us
  matrix products: 19.2 us -> 0 us
  between operations: 14.4 us -> 0.76 us
  other arithmetic: 11.6 us -> 0 us
    all_gather x6 -> x0, waiting for transfers between devices: 560 us -> none  [the longest x1 157 us: body(): lax.all_gather(d_tri, 'col', axis=1, tiled=True)]
    psum x2 -> x0, waiting for transfers between devices: 427 us -> none  [from_root(): return lax.psum(kept, axis)]
    all_to_all x0 -> x3, blocking collectives: none -> 61.6 us  [the longest x2 42.4 us: exchange(): lax.all_to_all(values.reshape(C, height, 128), OWNERS, 0, 0, tiled=True)]
    all_gather x4 -> x0, local copies, waits for them, and re-layouts: 26.9 us -> none  [the longest x1 10.9 us: body(): lax.all_gather(right_gated, 'col', axis=1, tiled=True)]
    all_to_all x0 -> x2, waiting for transfers between devices: none -> 22.8 us  [exchange(): lax.all_to_all(values.reshape(C, height, 128), OWNERS, 0, 0, tiled=True)]
    all_to_all x0 -> x2, starting transfers between devices: none -> 21.4 us  [exchange(): lax.all_to_all(values.reshape(C, height, 128), OWNERS, 0, 0, tiled=True)]
    all_gather x0 -> x1, blocking collectives: none -> 21 us  [body(): left_all = lax.all_gather(left, 'zhi', axis=0)]
    dot_general x7 -> x0, matrix products: 19.2 us -> none  [the longest x3 16.3 us: contract(): jnp.einsum(einsum_form, first_op, second_op, preferred_element_type=jnp.f...]
  transfers between devices with their start and end apart: 8 -> 2, of which waited for: 8 -> 2; matrix products, arithmetic and copies ran while one was open for 4% -> 1% of each run, Pallas kernels for 0% -> 0%
where the time goes in v1:
time: 138 us; the launch traced here: 137 us
  blocking collectives  82.6 us (60%)
  waiting for transfers between devices  22.8 us (17%)
  starting transfers between devices  21.4 us (16%)
  Pallas kernels  5.38 us (4%)
  local copies, waits for them, and re-layouts  4.29 us (3%)
    all_to_all x2, blocking collectives, exchange(): lax.all_to_all(values.reshape(C, height, 128), OWNERS, 0, 0, tiled=True)  42.4 us
    all_to_all x2, waiting for transfers between devices, exchange(): lax.all_to_all(values.reshape(C, height, 128), OWNERS, 0, 0, tiled=True)  22.8 us
    all_to_all x2, starting transfers between devices, exchange(): lax.all_to_all(values.reshape(C, height, 128), OWNERS, 0, 0, tiled=True)  21.4 us
    all_gather x1, blocking collectives, body(): left_all = lax.all_gather(left, 'zhi', axis=0)  21 us
    all_to_all x1, blocking collectives, body(): partial = lax.all_to_all(send, 'zhi', 0, 0, tiled=True)  19.2 us
    pallas_call x7, Pallas kernels, call(): pl.pallas_call(kernel, out_shape=[jax.ShapeDtypeStruct(shape, dtype) for...  5.38 us
    unnamed x18, local copies, waits for them, and re-layouts  3.56 us
  transfers between devices with their start and end apart: 2, of which 2 were waited for; matrix products, arithmetic and copies ran while one was open for 1% of the time, Pallas kernels for 0%

profile of v1, /device:TPU:1, one launch (start us, length us, event | category | flops | bytes accessed | tf_op | source)
XLA Modules:
  0.0 137.2 jit_solution(10815053197724531981)
XLA Ops:
  0.6 0.0 copy-start
  0.6 0.7 reshape.43.crop
  1.4 0.9 copy.11.pair
  2.3 0.0 copy-start.2
  2.3 0.0 copy-start.3
  2.3 0.0 copy-done
  2.3 0.6 copy-done.2
  2.9 0.0 copy-done.3
  2.9 0.7 project_kernel.1
  3.6 26.2 %all_to_all.25 = bf16[128,8,128]{2,1,0:T(8,128)(2,1)S(1)} all-to-all(bf16[128,8,128]{2,1,0:T(8,128)(2,1)S(1)} %bitcast.19), channel_id=1, replica_groups=mesh['xlo'=2,'y'=4,'core'=2,'zhi'=4,'zlo'=4,'xhi'=2] {'zlo','xhi','xlo',..., dimensions={0} | all-to-all | bytes 524288 | tf_op jit(solution)/shard_map/all_to_all | solution.py:263
  29.8 0.4 collect_kernel.1
  30.2 21.0 %all-gather = bf16[768,128]{1,0:T(8,128)(2,1)S(1)} all-gather(bf16[192,128]{1,0:T(8,128)(2,1)S(1)} %get-tuple-element.13), channel_id=2, replica_groups=mesh['xlo'=2,'y'=4,'core'=2,'zhi'=4,'zlo'=4,'xhi'=2] {'zhi'}, dimensions={0}, use_global_device_ids=true | all-gather | bytes 245760 | tf_op jit(solution)/shard_map/all_gather | solution.py:284
  51.3 1.4 %triangle_kernel.1 = bf16[512,128]{1,0:T(8,128)(2,1)} custom-call(bf16[4,192,128]{2,1,0:T(8,128)(2,1)S(1)} %bitcast.13, bf16[192,128]{1,0:T(8,128)(2,1)S(1)} %get-tuple-element.14.right), custom_call_target="tpu_custom_call" | custom-call | tf_op jit(solution)/shard_map/triangle_kernel/pallas_call | solution.py:251
  52.7 0.0 copy-start.6
  52.7 10.2 %all-to-all-start.1 = ((bf16[128,4,128]{2,1,0:T(4,128)(2,1)}), bf16[128,4,128]{2,1,0:T(4,128)(2,1)S(1)}, u32[]{:S(2)}, u32[]{:S(2)}) async-start(bf16[128,4,128]{2,1,0:T(4,128)(2,1)} %bitcast.5), calls=%async_computation.1 | async-start | bytes 262144 | tf_op jit(solution)/shard_map/all_to_all | solution.py:263
  62.8 0.0 copy-done.6
  62.9 0.0 copy-start.1
  62.9 10.9 %all-to-all-done.1 = bf16[128,4,128]{2,1,0:T(4,128)(2,1)S(1)} async-done(((bf16[128,4,128]{2,1,0:T(4,128)(2,1)}), bf16[128,4,128]{2,1,0:T(4,128)(2,1)S(1)}, u32[]{:S(2)}, u32[]{:S(2)}) %all-to-all-start.1) | async-done | bytes 131104 | tf_op jit(solution)/shard_map/all_to_all | solution.py:263
  73.8 0.0 copy-start.4
  73.8 0.0 copy-done.1
  73.8 0.6 copy-done.4
  74.4 0.0 copy-done.5
  74.5 0.5 output_kernel.1
  74.9 16.1 %all_to_all.26 = bf16[128,4,128]{2,1,0:T(4,128)(2,1)S(1)} all-to-all(bf16[128,4,128]{2,1,0:T(4,128)(2,1)S(1)} %bitcast.20), channel_id=1, replica_groups=mesh['xlo'=2,'y'=4,'core'=2,'zhi'=4,'zlo'=4,'xhi'=2] {'zlo','xhi','xlo',..., dimensions={0} | all-to-all | bytes 262144 | tf_op jit(solution)/shard_map/all_to_all | solution.py:263
  91.1 0.7 back_kernel.1
  91.8 19.2 %all_to_all.27.received = bf16[4,192,128]{2,1,0:T(8,128)(2,1)S(1)} all-to-all(bf16[4,192,128]{2,1,0:T(8,128)(2,1)S(1)} %get-tuple-element.19), channel_id=1, replica_groups=mesh['xlo'=2,'y'=4,'core'=2,'zhi'=4,'zlo'=4,'xhi'=2] {'zhi'}, dimensions={0} | all-to-all | bytes 393216 | tf_op jit(solution)/shard_map/all_to_all | solution.py:300
  111.1 1.1 spread_kernel.1
  112.1 11.2 %all-to-all-start.4 = ((bf16[128,8,128]{2,1,0:T(8,128)(2,1)}), bf16[128,8,128]{2,1,0:T(8,128)(2,1)S(1)}, u32[]{:S(2)}, u32[]{:S(2)}) async-start(bf16[128,8,128]{2,1,0:T(8,128)(2,1)} %bitcast.11), calls=%async_computation.4 | async-start | bytes 524288 | tf_op jit(solution)/shard_map/all_to_all | solution.py:263
  123.3 0.7 copy.14
  124.0 11.9 %all-to-all-done.4 = bf16[128,8,128]{2,1,0:T(8,128)(2,1)S(1)} async-done(((bf16[128,8,128]{2,1,0:T(8,128)(2,1)}), bf16[128,8,128]{2,1,0:T(8,128)(2,1)S(1)}, u32[]{:S(2)}, u32[]{:S(2)}) %all-to-all-start.4) | async-done | bytes 262176 | tf_op jit(solution)/shard_map/all_to_all | solution.py:263
  135.9 0.7 input_kernel.1
  136.6 0.7 copy.15
  (3 shorter events, 0.0 us)
Async XLA Ops:
  0.6 1.7 %copy-start = (bf16[128,640]{1,0:T(8,128)(2,1)S(1)}, bf16[128,640]{1,0:T(8,128)(2,1)}, u32[]{:S(2)}) copy-start(bf16[128,640]{1,0:T(8,128)(2,1)} %weights.5) | copy-start | bytes 491524
  2.3 0.7 copy-start.2
  2.3 0.7 copy-start.3
  52.7 10.2 %copy-start.6 = (bf16[24,12,128]{2,0,1:T(8,128)(2,1)S(1)}, bf16[24,12,128]{2,0,1:T(8,128)(2,1)}, u32[]{:S(2)}) copy-start(bf16[24,12,128]{2,0,1:T(8,128)(2,1)} %param.17) | copy-start | bytes 221188
  52.7 21.1 %all-to-all-start.1 = ((bf16[128,4,128]{2,1,0:T(4,128)(2,1)}), bf16[128,4,128]{2,1,0:T(4,128)(2,1)S(1)}, u32[]{:S(2)}, u32[]{:S(2)}) async-start(bf16[128,4,128]{2,1,0:T(4,128)(2,1)} %bitcast.5), calls=%async_computation.1 | async-start | bytes 262144 | tf_op jit(solution)/shard_map/all_to_all | solution.py:263
  62.9 10.9 %copy-start.1 = (bf16[128,128]{1,0:T(8,128)(2,1)S(1)}, bf16[128,128]{1,0:T(8,128)(2,1)}, u32[]{:S(2)}) copy-start(bf16[128,128]{1,0:T(8,128)(2,1)} %weights.4) | copy-start | bytes 98308
  73.8 0.7 copy-start.4
  73.8 0.7 copy-start.5
  112.1 23.8 %all-to-all-start.4 = ((bf16[128,8,128]{2,1,0:T(8,128)(2,1)}), bf16[128,8,128]{2,1,0:T(8,128)(2,1)S(1)}, u32[]{:S(2)}, u32[]{:S(2)}) async-start(bf16[128,8,128]{2,1,0:T(8,128)(2,1)} %bitcast.11), calls=%async_computation.4 | async-start | bytes 524288 | tf_op jit(solution)/shard_map/all_to_all | solution.py:263

commit v2 on v1

v2 whole, which is shorter than its diff:
```python
import jax
import jax.numpy as jnp
from jax import lax
from jax.experimental import pallas as pl
from jax.experimental.pallas import tpu as pltpu
from jax.sharding import Mesh, PartitionSpec as P

norm_eps = 1e-05
f32 = jnp.float32
bf16 = jnp.bfloat16
ROWS = ("xlo", "y", "core")
COLS = ("zhi", "zlo", "xhi")
OWNERS = ("zlo", "xhi", "xlo", "y", "core")
TK, TI, PAD = 24, 12, 16
LANES = TK * PAD
E, R, Q = 4, 16, 8
HELD = 8 // E
WIDTH = 128 // HELD
C = 128
N = 384
FOLD = N // 2
PACK = FOLD * TI // PAD
GROUP = FOLD - PACK
RF = R // 2
BOTH = (C // HELD, 2 * HELD, LANES)
ONE = (C // HELD, HELD, LANES)


def dot(first_op, second_op, dims):
    return lax.dot_general(first_op, second_op, (dims, ((), ())), preferred_element_type=f32)


def swap_blocks(parts):
    parts = list(parts)
    block = lax.broadcasted_iota(jnp.int32, parts[0].shape, 1) // PAD
    for step in (4, 2, 1):
        upper = (block & step) != 0
        for a in range(8):
            if a & step:
                continue
            b = a | step
            low, high = parts[a], parts[b]
            parts[a] = jnp.where(upper, pltpu.roll(high, step * PAD, 1), low)
            parts[b] = jnp.where(upper, high, pltpu.roll(low, 128 - step * PAD, 1))
    return parts


def as_column(row):
    return jnp.broadcast_to(row, (C, C)).T[:, :1]


def padded_rows(tile, scratch):
    tile = tile.astype(f32)
    for i in range(PAD):
        part = tile[i] if i < TI else jnp.zeros((TK, C), f32)
        scratch[pl.ds(i, TK, stride=PAD), :] = part
    return scratch[...]


def unpadded_rows(values, scratch):
    scratch[...] = values
    return jnp.stack([scratch[pl.ds(i, TK, stride=PAD), :] for i in range(TI)]).astype(bf16)


def parts_of(slots):
    kinds = slots.shape[1] // C
    step = HELD * kinds
    return [
        jnp.concatenate(
            [
                slots[t, pl.ds(step * R * e + kinds * held + kind, R, stride=step), :]
                for kind in range(kinds)
                for t in range(3)
            ],
            axis=0,
        )
        for held in range(HELD)
        for e in range(E)
    ]


def pack_rows(values):
    spare = lax.broadcasted_iota(jnp.int32, (PACK, 128), 1) % PAD >= TI
    last = values[PACK:]
    moved = [pltpu.roll(last, TI - (PAD - TI) * g, 1) for g in range(3)]
    return jnp.where(spare, jnp.concatenate(moved, axis=0), values[:PACK])


def unpack_rows(packed):
    lane = lax.broadcasted_iota(jnp.int32, (GROUP, 128), 1) % PAD
    last = jnp.zeros((GROUP, 128), f32)
    for g in range(3):
        back = pltpu.roll(packed[GROUP * g : GROUP * (g + 1)], 128 - TI + (PAD - TI) * g, 1)
        last = jnp.where(lane // (PAD - TI) == g, back, last)
    spare = lax.broadcasted_iota(jnp.int32, (PACK, 128), 1) % PAD >= TI
    return jnp.concatenate([jnp.where(spare, 0.0, packed), last], axis=0)


def own_block(shape):
    return lax.broadcasted_iota(jnp.int32, shape, 1) // WIDTH


def norm_rows(values):
    centered = values - jnp.mean(values, axis=1, keepdims=True)
    inv_std = lax.rsqrt(jnp.mean(centered * centered, axis=1, keepdims=True) + norm_eps)
    return centered * inv_std, inv_std


def put_rows(slots, rows, values):
    for t in range(3):
        slots[t, rows, :] = values[:, 128 * t : 128 * (t + 1)]


def get_rows(slots, rows):
    return jnp.concatenate([slots[t, rows, :] for t in range(3)], axis=1)


def message_rows(slots):
    rows = get_rows(slots, slice(None))
    return rows.reshape(C // HELD, rows.shape[0] * HELD // C, LANES).astype(bf16)


def own_rows(slots, received):
    put_rows(slots, slice(None), received[...].astype(f32).reshape(-1, LANES))


def project_kernel(
    crop, pair_hbm, gain_hbm, bias_hbm, weights_hbm, out_gain_hbm, out_bias_hbm,
    send, projected, inside, vectors,
    padded, slots, pair, weights, gain, bias, out_gain, out_bias, arrived,
):
    sources = (pair_hbm, gain_hbm, bias_hbm, weights_hbm, out_gain_hbm, out_bias_hbm)
    targets = (pair, gain, bias, weights, out_gain, out_bias)
    loads = [
        pltpu.make_async_copy(source, target, arrived.at[n])
        for n, (source, target) in enumerate(zip(sources, targets))
    ]
    for load in loads:
        load.start()
    row_pos = lax.axis_index(ROWS)
    col_pos = lax.axis_index(COLS)
    lane = lax.broadcasted_iota(jnp.int32, (8, LANES), 1)
    crop_rows = jnp.zeros((8, LANES), jnp.int32)
    crop_cols = jnp.full((8, LANES), -1, jnp.int32)
    for k in range(TK):
        crop_rows = jnp.where(lane // PAD == k, crop[row_pos * TK + k], crop_rows)
    for i in range(TI):
        crop_cols = jnp.where(lane % PAD == i, crop[col_pos * TI + i], crop_cols)
    same = (crop_rows == crop_cols).astype(f32)
    inside[...] = same
    mask = same[:1, :]

    for load in loads[:3]:
        load.wait()
    hat, _ = norm_rows(padded_rows(pair[...], padded))
    normed = (hat * gain[...] + bias[...]).astype(bf16)
    for load in loads[3:]:
        load.wait()
    vectors[...] = jnp.concatenate(
        [jnp.broadcast_to(v[...], (8, C)) for v in (gain, out_gain, out_bias)], axis=0
    )
    proj = dot(weights[...].T, normed, ((1,), (1,)))
    projected[...] = proj
    left = mask * jax.nn.sigmoid(proj[2 * C : 3 * C]) * proj[:C]
    right = mask * jax.nn.sigmoid(proj[3 * C : 4 * C]) * proj[C : 2 * C]
    put_rows(slots, pl.ds(0, C, stride=2), left)
    put_rows(slots, pl.ds(1, C, stride=2), right)
    send[...] = message_rows(slots)


def collect_kernel(received, left, right, slots):
    own_rows(slots, received)
    parts = parts_of(slots)
    parts = swap_blocks(parts)
    for side, out in enumerate((left, right)):
        pieces = []
        for t in range(3):
            for k in range(8):
                at = (3 * side + t) * R
                pieces.append(parts[k][at : at + RF] + parts[k][at + RF : at + R])
        whole = jnp.concatenate(pieces, axis=0)
        if side:
            out[...] = whole.astype(bf16)
        else:
            packed = pack_rows(whole).astype(bf16)
            for q in range(Q):
                out[q] = packed


def reorder(transposed):
    shape = (N, Q * WIDTH) if transposed else (Q * WIDTH, N)
    wide = lax.broadcasted_iota(jnp.int32, shape, 1 if transposed else 0)
    target = lax.broadcasted_iota(jnp.int32, shape, 0 if transposed else 1)
    within = (wide // PAD % 2) * TI + wide % PAD
    position = wide // (2 * PAD)
    hit = (target == within * R + position) & (wide % PAD < TI)
    return hit.astype(f32).astype(bf16)


def triangle_kernel(left_packed, right, left_all, send, slots):
    for q in range(Q):
        left_all[q] = unpack_rows(left_packed[q].astype(f32)).astype(bf16)
    rows = []
    block = own_block((WIDTH, 128))
    for q in range(Q):
        product = dot(left_all[q], right[...], ((0,), (0,)))
        own = product[:WIDTH]
        for held in range(1, HELD):
            own = jnp.where(block == held, product[WIDTH * held : WIDTH * (held + 1)], own)
        rows.append(own)
    tri = jnp.concatenate(rows, axis=0).astype(bf16)
    tri = dot(reorder(True), tri, ((1,), (0,)))
    parts = [
        jnp.concatenate([tri[(8 * t + i) * R : (8 * t + i + 1) * R] for t in range(3)], axis=0)
        for i in range(8)
    ]
    parts = swap_blocks(parts)
    for held in range(HELD):
        for e in range(E):
            rows = pl.ds(HELD * R * e + held, R, stride=HELD)
            part = parts[held * E + e]
            for t in range(3):
                slots[t, rows, :] = part[t * R : (t + 1) * R]
    send[...] = message_rows(slots)


def output_kernel(
    received, projected, inside, vectors, cotangent, weights, update, d_outpre, send, padded, slots
):
    mask = inside[:1, :]
    own_rows(slots, received)
    tri = jnp.where(mask > 0, get_rows(slots, slice(None)), 0.0)
    centered = tri - jnp.mean(tri, axis=0, keepdims=True)
    inv_out = lax.rsqrt(jnp.mean(centered * centered, axis=0, keepdims=True) + norm_eps)
    tri_hat = centered * inv_out
    gain_col = as_column(vectors[8:9])
    normed_out = (tri_hat * gain_col + as_column(vectors[16:17])).astype(bf16)
    gated_value = dot(weights[...].T, normed_out, ((1,), (0,)))
    gate = jax.nn.sigmoid(projected[4 * C :])
    update[...] = unpadded_rows((gate * gated_value).T, padded)
    upstream = padded_rows(cotangent[...], padded).T
    d_value = (upstream * gate).astype(bf16)
    d_outpre[...] = (upstream * gated_value * gate * (1.0 - gate)).astype(bf16)
    grad = dot(weights[...], d_value, ((1,), (0,))) * gain_col
    first_mean = jnp.mean(grad, axis=0, keepdims=True)
    second_mean = jnp.mean(grad * tri_hat, axis=0, keepdims=True)
    d_tri = inv_out * (grad - first_mean - tri_hat * second_mean)
    put_rows(slots, slice(None), jnp.where(mask > 0, d_tri, 0.0))
    send[...] = message_rows(slots)


def back_kernel(received, left_all, right, d_right, send, slots):
    own_rows(slots, received)
    parts = parts_of(slots)
    parts = swap_blocks(parts)
    d_tri = jnp.concatenate(
        [parts[i][t * R : (t + 1) * R] for t in range(3) for i in range(8)], axis=0
    ).astype(bf16)
    d_tri = dot(reorder(False), d_tri, ((1,), (0,))).astype(bf16)
    total = jnp.zeros((FOLD, 128), f32)
    own = own_block((WIDTH, 128))
    for q in range(Q):
        block = d_tri[WIDTH * q : WIDTH * (q + 1)]
        if HELD > 1:
            block = jnp.concatenate(
                [jnp.where(own == held, block, jnp.zeros_like(block)) for held in range(HELD)],
                axis=0,
            )
        total = total + dot(left_all[q], block, ((1,), (0,)))
        send[q] = pack_rows(dot(right[...], block, ((1,), (1,)))).astype(bf16)
    d_right[...] = total


def spread_kernel(received, d_right, send, slots):
    d_left = received[0].astype(f32)
    for q in range(1, Q):
        d_left = d_left + received[q].astype(f32)
    d_left = unpack_rows(d_left)
    sides = (d_left, d_right[...])
    parts = [
        jnp.concatenate(
            [
                sides[side][(8 * t + k) * RF : (8 * t + k + 1) * RF]
                for side in range(2)
                for t in range(3)
            ],
            axis=0,
        )
        for k in range(8)
    ]
    parts = swap_blocks(parts)
    step = HELD * 2
    for held in range(HELD):
        for e in range(E):
            part = parts[held * E + e]
            for side in range(2):
                for t in range(3):
                    piece = part[(3 * side + t) * RF : (3 * side + t + 1) * RF]
                    for half in range(2):
                        start = step * (R * e + RF * half) + 2 * held + side
                        slots[t, pl.ds(start, RF, stride=step), :] = piece
    send[...] = message_rows(slots)


def input_kernel(
    received, projected, inside, vectors, d_outpre, pair, weights, pair_grad, padded, slots
):
    own_rows(slots, received)
    mask = inside[:1, :]
    d_left = get_rows(slots, pl.ds(0, C, stride=2)) * mask
    d_right = get_rows(slots, pl.ds(1, C, stride=2)) * mask
    left_val, right_val = projected[:C], projected[C : 2 * C]
    left_sig = jax.nn.sigmoid(projected[2 * C : 3 * C])
    right_sig = jax.nn.sigmoid(projected[3 * C : 4 * C])
    d_proj = jnp.concatenate(
        [
            (d_left * left_sig).astype(bf16),
            (d_right * right_sig).astype(bf16),
            (d_left * left_val * left_sig * (1.0 - left_sig)).astype(bf16),
            (d_right * right_val * right_sig * (1.0 - right_sig)).astype(bf16),
            d_outpre[...],
        ],
        axis=0,
    )
    grad = dot(weights[...], d_proj, ((1,), (0,))).T * vectors[:1]
    hat, inv_in = norm_rows(padded_rows(pair[...], padded))
    first_mean = jnp.mean(grad, axis=1, keepdims=True)
    second_mean = jnp.mean(grad * hat, axis=1, keepdims=True)
    pair_grad[...] = unpadded_rows(inv_in * (grad - first_mean - hat * second_mean), padded)


def call(kernel, outs, scratch, *operands, spaces=None, vmem=40):
    spaces = spaces or [pltpu.VMEM] * len(operands)
    return pl.pallas_call(
        kernel,
        out_shape=[jax.ShapeDtypeStruct(shape, dtype) for shape, dtype in outs],
        in_specs=[pl.BlockSpec(memory_space=space) for space in spaces],
        out_specs=[pl.BlockSpec(memory_space=pltpu.VMEM)] * len(outs),
        scratch_shapes=[
            pltpu.VMEM(shape, f32) if isinstance(shape, tuple) else shape for shape in scratch
        ],
        compiler_params=pltpu.CompilerParams(vmem_limit_bytes=vmem * 1024 * 1024),
        name=kernel.__name__,
    )(*operands)


def exchange(messages):
    return lax.all_to_all(messages, OWNERS, 0, 0, tiled=True)


def body(pair, crop, in_gain, in_bias, in_weights, out_gain, out_bias, out_weights, cotangent):
    padded = (LANES, C)
    tile = ((TI, TK, C), bf16)
    pair = pair.transpose(1, 0, 2)
    cotangent = cotangent.transpose(1, 0, 2)
    in_gain, in_bias, out_gain, out_bias = (
        v.reshape(1, C) for v in (in_gain, in_bias, out_gain, out_bias)
    )
    send, projected, inside, vectors = call(
        project_kernel,
        [(BOTH, bf16), ((5 * C, LANES), f32), ((8, LANES), f32), ((24, C), f32)],
        [
            padded, (3, 2 * C, 128), pltpu.VMEM((TI, TK, C), bf16), pltpu.VMEM((C, 5 * C), bf16),
            (1, C), (1, C), (1, C), (1, C), pltpu.SemaphoreType.DMA((6,)),
        ],
        crop, pair, in_gain, in_bias, in_weights, out_gain, out_bias,
        spaces=[pltpu.SMEM] + [pl.ANY] * 6,
        vmem=58,
    )
    left, right = call(
        collect_kernel,
        [((Q, PACK, 128), bf16), ((FOLD, 128), bf16)],
        [(3, 2 * C, 128)],
        exchange(send),
    )
    left = lax.all_to_all(left, "zhi", 0, 0, tiled=True)
    left_all, send = call(
        triangle_kernel,
        [((Q, FOLD, 128), bf16), (ONE, bf16)],
        [(3, C, 128)],
        left, right,
    )
    update, d_outpre, send = call(
        output_kernel,
        [tile, ((C, LANES), bf16), (ONE, bf16)],
        [padded, (3, C, 128)],
        exchange(send), projected, inside, vectors, cotangent, out_weights,
    )
    d_right, send = call(
        back_kernel,
        [((FOLD, 128), f32), ((Q, PACK, 128), bf16)],
        [(3, C, 128)],
        exchange(send), left_all, right,
    )
    partial = lax.all_to_all(send, "zhi", 0, 0, tiled=True)
    (send,) = call(
        spread_kernel, [(BOTH, bf16)], [(3, 2 * C, 128)], partial, d_right
    )
    (pair_grad,) = call(
        input_kernel,
        [tile],
        [padded, (3, 2 * C, 128)],
        exchange(send), projected, inside, vectors, d_outpre, pair, in_weights,
    )
    return update.transpose(1, 0, 2), pair_grad.transpose(1, 0, 2)


def solution(mesh):
    split = Mesh(mesh.devices.reshape(2, 4, 2, Q, 16 // Q, 2), ROWS + COLS)
    tiles = P(ROWS, COLS, None)
    in_specs = (tiles, P(), P(), P(), P(), P(), P(), P(), tiles)
    return jax.shard_map(
        body, mesh=split, in_specs=in_specs, out_specs=(tiles, tiles), check_vma=False
    )
```

time: 138 us -> 131 us (0.949)
  blocking collectives: 82.6 us -> 121 us
  waiting for transfers between devices: 22.8 us -> 0 us
  starting transfers between devices: 21.4 us -> 0 us
  local copies, waits for them, and re-layouts: 4.29 us -> 0.04 us
  Pallas kernels: 5.38 us -> 8.68 us
    all_to_all x2 -> x5, blocking collectives: 42.4 us -> 96.5 us  [the longest x4 63.2 us: exchange(): return lax.all_to_all(messages, OWNERS, 0, 0, tiled=True)]
    all_to_all x2 -> x0, waiting for transfers between devices: 22.8 us -> none  [exchange(): lax.all_to_all(values.reshape(C, height, 128), OWNERS, 0, 0, tiled=True)]
    all_to_all x2 -> x0, starting transfers between devices: 21.4 us -> none  [exchange(): lax.all_to_all(values.reshape(C, height, 128), OWNERS, 0, 0, tiled=True)]
    all_gather x1 -> x0, blocking collectives: 21 us -> none  [body(): left_all = lax.all_gather(left, 'zhi', axis=0)]
    all_to_all x1, blocking collectives: 19.2 us -> 24.5 us  [body(): partial = lax.all_to_all(send, 'zhi', 0, 0, tiled=True)]
    unnamed x18 -> x14, local copies, waits for them, and re-layouts: 3.56 us -> 0.04 us
    pallas_call x7, Pallas kernels: 5.38 us -> 8.68 us  [call(): pl.pallas_call(kernel, out_shape=[jax.ShapeDtypeStruct(shape, dtype) for...]
  transfers between devices with their start and end apart: 2 -> 0, of which waited for: 2 -> 0; matrix products, arithmetic and copies ran while one was open for 1% -> 0% of each run, Pallas kernels for 0% -> 0%
where the time goes in v2:
time: 131 us; the launch traced here: 130 us
  blocking collectives  121 us (92%)
  Pallas kernels  8.68 us (7%)
    all_to_all x4, blocking collectives, exchange(): return lax.all_to_all(messages, OWNERS, 0, 0, tiled=True)  63.2 us
    all_to_all x1, blocking collectives, body(): left = lax.all_to_all(left, 'zhi', 0, 0, tiled=True)  33.3 us
    all_to_all x1, blocking collectives, body(): partial = lax.all_to_all(send, 'zhi', 0, 0, tiled=True)  24.5 us
    pallas_call x7, Pallas kernels, call(): pl.pallas_call(kernel, out_shape=[jax.ShapeDtypeStruct(shape, dtype) for...  8.68 us

profile of v2, /device:TPU:1, one launch (start us, length us, event | category | flops | bytes accessed | tf_op | source)
XLA Modules:
  0.0 130.4 jit_solution(12341906778473466870)
XLA Ops:
  0.6 3.2 %project_kernel.1 = (bf16[64,4,384]{2,1,0:T(4,128)(2,1)}, f32[640,384]{1,0:T(8,128)}, f32[8,384]{1,0:T(8,128)}, f32[24,128]{1,0:T(8,128)}) custom-call(s32[384]{0:T(512)} %crop.1, bf16[12,24,128]{2,1,0:T(8,128)(2,1)} %bitcast.8, f32[1,128]{1,0:T(1,128)} %bitcast.12, f32[1,128]{1,0:T(1,128)} %bitcast.13, bf16[128,640]{1,0:T(8,128)(2,1)} %weights.3, ...), custom_call_target="tpu_custom_call" | custom-call | tf_op jit(solution)/shard_map/project_kernel/pallas_call | solution.py:334
  3.9 0.0 copy-start
  3.9 20.3 %all_to_all.30.received = bf16[64,4,384]{2,1,0:T(4,128)(2,1)S(1)} all-to-all(bf16[64,4,384]{2,1,0:T(4,128)(2,1)} %get-tuple-element.15), channel_id=1, replica_groups=mesh['xlo'=2,'y'=4,'core'=2,'zhi'=8,'zlo'=2,'xhi'=2] {'zlo','xhi','xlo',..., dimensions={0} | all-to-all | bytes 393216 | tf_op jit(solution)/shard_map/all_to_all | solution.py:348
  24.2 0.4 collect_kernel.1
  24.6 33.3 %all_to_all.31.left_packed = bf16[8,144,128]{2,1,0:T(8,128)(2,1)S(1)} all-to-all(bf16[8,144,128]{2,1,0:T(8,128)(2,1)S(1)} %get-tuple-element.16), channel_id=1, replica_groups=mesh['xlo'=2,'y'=4,'core'=2,'zhi'=8,'zlo'=2,'xhi'=2] {'zhi'}, dimensions={0} | all-to-all | bytes 589824 | tf_op jit(solution)/shard_map/all_to_all | solution.py:376
  57.9 1.0 triangle_kernel.1
  59.0 0.0 copy-start.3
  59.0 0.0 copy-start.4
  59.0 0.0 copy-start.5
  59.0 0.0 copy-start.6
  59.0 15.5 %all_to_all.32.received = bf16[64,2,384]{2,1,0:T(2,128)(2,1)S(1)} all-to-all(bf16[64,2,384]{2,1,0:T(2,128)(2,1)S(1)} %get-tuple-element.18), channel_id=1, replica_groups=mesh['xlo'=2,'y'=4,'core'=2,'zhi'=8,'zlo'=2,'xhi'=2] {'zlo','xhi','xlo',..., dimensions={0} | all-to-all | bytes 196608 | tf_op jit(solution)/shard_map/all_to_all | solution.py:348
  74.5 0.0 copy-done
  74.5 0.0 copy-done.3
  74.5 0.0 copy-done.4
  74.5 0.0 copy-done.5
  74.5 0.0 copy-done.6
  74.5 1.2 output_kernel.1
  75.8 12.3 %all_to_all.33.received = bf16[64,2,384]{2,1,0:T(2,128)(2,1)S(1)} all-to-all(bf16[64,2,384]{2,1,0:T(2,128)(2,1)S(1)} %get-tuple-element.23), channel_id=1, replica_groups=mesh['xlo'=2,'y'=4,'core'=2,'zhi'=8,'zlo'=2,'xhi'=2] {'zlo','xhi','xlo',..., dimensions={0} | all-to-all | bytes 196608 | tf_op jit(solution)/shard_map/all_to_all | solution.py:348
  88.0 1.0 back_kernel.1
  89.0 24.5 %all_to_all.34.received = bf16[8,144,128]{2,1,0:T(8,128)(2,1)S(1)} all-to-all(bf16[8,144,128]{2,1,0:T(8,128)(2,1)S(1)} %get-tuple-element.25), channel_id=1, replica_groups=mesh['xlo'=2,'y'=4,'core'=2,'zhi'=8,'zlo'=2,'xhi'=2] {'zhi'}, dimensions={0} | all-to-all | bytes 589824 | tf_op jit(solution)/shard_map/all_to_all | solution.py:395
  113.4 0.4 spread_kernel.1
  113.9 0.0 copy-start.1
  113.9 0.0 copy-start.2
  113.9 15.1 %all_to_all.35.received = bf16[64,4,384]{2,1,0:T(4,128)(2,1)S(1)} all-to-all(bf16[64,4,384]{2,1,0:T(4,128)(2,1)S(1)} %spread_kernel.1), channel_id=1, replica_groups=mesh['xlo'=2,'y'=4,'core'=2,'zhi'=8,'zlo'=2,'xhi'=2] {'zlo','xhi','xlo',..., dimensions={0} | all-to-all | bytes 393216 | tf_op jit(solution)/shard_map/all_to_all | solution.py:348
  129.1 0.0 copy-done.1
  129.1 0.0 copy-done.2
  129.1 1.4 %input_kernel.1 = bf16[12,24,128]{2,1,0:T(8,128)(2,1)} custom-call(bf16[64,4,384]{2,1,0:T(4,128)(2,1)S(1)} %all_to_all.35.received, f32[640,384]{1,0:T(8,128)S(1)} %copy-done, f32[8,384]{1,0:T(8,128)S(1)} %copy-done.4, f32[24,128]{1,0:T(8,128)S(1)} %copy-done.5, bf16[128,384]{1,0:T(8,128)(2,1)S(1)} %get-tuple-element.27.d_outpre, ...), custom_call_target="tpu_custom_call" | custom-call | tf_op jit(solution)/shard_map/input_kernel/pallas_call | solution.py:334
Async XLA Ops:
  3.9 70.6 %copy-start = (f32[640,384]{1,0:T(8,128)S(1)}, f32[640,384]{1,0:T(8,128)}, u32[]{:S(2)}) copy-start(f32[640,384]{1,0:T(8,128)} %get-tuple-element.19.projected) | copy-start | bytes 2949124
  59.0 15.5 %copy-start.3 = (bf16[24,12,128]{2,0,1:T(8,128)(2,1)S(1)}, bf16[24,12,128]{2,0,1:T(8,128)(2,1)}, u32[]{:S(2)}) copy-start(bf16[24,12,128]{2,0,1:T(8,128)(2,1)} %param.17) | copy-start | bytes 221188
  59.0 15.5 %copy-start.4 = (f32[8,384]{1,0:T(8,128)S(1)}, f32[8,384]{1,0:T(8,128)}, u32[]{:S(2)}) copy-start(f32[8,384]{1,0:T(8,128)} %get-tuple-element.20.inside) | copy-start | bytes 36868
  59.0 15.5 %copy-start.5 = (f32[24,128]{1,0:T(8,128)S(1)}, f32[24,128]{1,0:T(8,128)}, u32[]{:S(2)}) copy-start(f32[24,128]{1,0:T(8,128)} %get-tuple-element.21.vectors) | copy-start | bytes 36868
  59.0 15.5 %copy-start.6 = (bf16[128,128]{1,0:T(8,128)(2,1)S(1)}, bf16[128,128]{1,0:T(8,128)(2,1)}, u32[]{:S(2)}) copy-start(bf16[128,128]{1,0:T(8,128)(2,1)} %weights.2) | copy-start | bytes 98308
  113.9 15.2 %copy-start.1 = (bf16[128,640]{1,0:T(8,128)(2,1)S(1)}, bf16[128,640]{1,0:T(8,128)(2,1)}, u32[]{:S(2)}) copy-start(bf16[128,640]{1,0:T(8,128)(2,1)} %weights.3) | copy-start | bytes 491524
  113.9 15.2 %copy-start.2 = (bf16[24,12,128]{2,0,1:T(8,128)(2,1)S(1)}, bf16[24,12,128]{2,0,1:T(8,128)(2,1)}, u32[]{:S(2)}) copy-start(bf16[24,12,128]{2,0,1:T(8,128)(2,1)} %param.9) | copy-start | bytes 221188

commit v3 on v2

--- a/solution.py
+++ b/solution.py
@@ -125,18 +125,29 @@
 
 
 def project_kernel(
-    crop, pair_hbm, gain_hbm, bias_hbm, weights_hbm, out_gain_hbm, out_bias_hbm,
-    send, projected, inside, vectors,
-    padded, slots, pair, weights, gain, bias, out_gain, out_bias, arrived,
+    crop_hbm, pair_hbm, gain_hbm, bias_hbm, weights_hbm, out_gain_hbm, out_bias_hbm,
+    send, projected_hbm, inside, vectors,
+    padded, slots, projected, crop, pair, gain, bias, weights, out_gain, out_bias, arrived,
 ):
-    sources = (pair_hbm, gain_hbm, bias_hbm, weights_hbm, out_gain_hbm, out_bias_hbm)
-    targets = (pair, gain, bias, weights, out_gain, out_bias)
+    sources = (crop_hbm, pair_hbm, gain_hbm, bias_hbm, weights_hbm, out_gain_hbm, out_bias_hbm)
+    targets = (crop, pair, gain, bias, weights, out_gain, out_bias)
     loads = [
         pltpu.make_async_copy(source, target, arrived.at[n])
         for n, (source, target) in enumerate(zip(sources, targets))
     ]
     for load in loads:
         load.start()
+    loads[1].wait()
+    hat, _ = norm_rows(padded_rows(pair[...], padded))
+    loads[2].wait()
+    loads[3].wait()
+    normed = (hat * gain[...] + bias[...]).astype(bf16)
+    loads[4].wait()
+    projected[...] = dot(weights[...].T, normed, ((1,), (1,)))
+    keep = pltpu.make_async_copy(projected, projected_hbm, arrived.at[7])
+    keep.start()
+
+    loads[0].wait()
     row_pos = lax.axis_index(ROWS)
     col_pos = lax.axis_index(COLS)
     lane = lax.broadcasted_iota(jnp.int32, (8, LANES), 1)
@@ -149,67 +160,50 @@
     same = (crop_rows == crop_cols).astype(f32)
     inside[...] = same
     mask = same[:1, :]
-
-    for load in loads[:3]:
-        load.wait()
-    hat, _ = norm_rows(padded_rows(pair[...], padded))
-    normed = (hat * gain[...] + bias[...]).astype(bf16)
-    for load in loads[3:]:
-        load.wait()
-    vectors[...] = jnp.concatenate(
-        [jnp.broadcast_to(v[...], (8, C)) for v in (gain, out_gain, out_bias)], axis=0
-    )
-    proj = dot(weights[...].T, normed, ((1,), (1,)))
-    projected[...] = proj
-    left = mask * jax.nn.sigmoid(proj[2 * C : 3 * C]) * proj[:C]
-    right = mask * jax.nn.sigmoid(proj[3 * C : 4 * C]) * proj[C : 2 * C]
+    left = mask * jax.nn.sigmoid(projected[2 * C : 3 * C]) * projected[:C]
+    right = mask * jax.nn.sigmoid(projected[3 * C : 4 * C]) * projected[C : 2 * C]
     put_rows(slots, pl.ds(0, C, stride=2), left)
     put_rows(slots, pl.ds(1, C, stride=2), right)
     send[...] = message_rows(slots)
-
-
-def collect_kernel(received, left, right, slots):
+    loads[5].wait()
+    loads[6].wait()
+    vectors[...] = jnp.concatenate(
+        [jnp.broadcast_to(v[...], (8, C)) for v in (gain, out_gain, out_bias)], axis=0
+    )
+    keep.wait()
+
+
+def collect_kernel(received, both, right, slots):
     own_rows(slots, received)
     parts = parts_of(slots)
     parts = swap_blocks(parts)
-    for side, out in enumerate((left, right)):
+    for side in range(2):
         pieces = []
         for t in range(3):
             for k in range(8):
                 at = (3 * side + t) * R
                 pieces.append(parts[k][at : at + RF] + parts[k][at + RF : at + R])
         whole = jnp.concatenate(pieces, axis=0)
-        if side:
-            out[...] = whole.astype(bf16)
-        else:
-            packed = pack_rows(whole).astype(bf16)
-            for q in range(Q):
-                out[q] = packed
-
-
-def reorder(transposed):
-    shape = (N, Q * WIDTH) if transposed else (Q * WIDTH, N)
-    wide = lax.broadcasted_iota(jnp.int32, shape, 1 if transposed else 0)
-    target = lax.broadcasted_iota(jnp.int32, shape, 0 if transposed else 1)
-    within = (wide // PAD % 2) * TI + wide % PAD
-    position = wide // (2 * PAD)
-    hit = (target == within * R + position) & (wide % PAD < TI)
-    return hit.astype(f32).astype(bf16)
-
-
-def triangle_kernel(left_packed, right, left_all, send, slots):
-    for q in range(Q):
-        left_all[q] = unpack_rows(left_packed[q].astype(f32)).astype(bf16)
-    rows = []
+        both[PACK * side : PACK * (side + 1)] = pack_rows(whole).astype(bf16)
+    right[...] = whole.astype(bf16)
+
+
+def residue_rows(column):
+    return pl.ds(column % 2 * TI * R + column // 2, TI, stride=R)
+
+
+def triangle_kernel(both, right, left_all, send, slots, ordered):
     block = own_block((WIDTH, 128))
     for q in range(Q):
-        product = dot(left_all[q], right[...], ((0,), (0,)))
+        left = unpack_rows(both[q, :PACK].astype(f32)).astype(bf16)
+        left_all[q] = left
+        product = dot(left, right[...], ((0,), (0,)))
         own = product[:WIDTH]
         for held in range(1, HELD):
             own = jnp.where(block == held, product[WIDTH * held : WIDTH * (held + 1)], own)
-        rows.append(own)
-    tri = jnp.concatenate(rows, axis=0).astype(bf16)
-    tri = dot(reorder(True), tri, ((1,), (0,)))
+        for e in range(E):
+            ordered[residue_rows(E * q + e), :] = own[PAD * e : PAD * e + TI]
+    tri = ordered[...]
     parts = [
         jnp.concatenate([tri[(8 * t + i) * R : (8 * t + i + 1) * R] for t in range(3)], axis=0)
         for i in range(8)
@@ -225,7 +219,8 @@
 
 
 def output_kernel(
-    received, projected, inside, vectors, cotangent, weights, update, d_outpre, send, padded, slots
+    received, projected, inside, vectors, cotangent, weights, update_hbm, d_outpre, send,
+    padded, slots, update, written,
 ):
     mask = inside[:1, :]
     own_rows(slots, received)
@@ -238,6 +233,8 @@
     gated_value = dot(weights[...].T, normed_out, ((1,), (0,)))
     gate = jax.nn.sigmoid(projected[4 * C :])
     update[...] = unpadded_rows((gate * gated_value).T, padded)
+    write = pltpu.make_async_copy(update, update_hbm, written)
+    write.start()
     upstream = padded_rows(cotangent[...], padded).T
     d_value = (upstream * gate).astype(bf16)
     d_outpre[...] = (upstream * gated_value * gate * (1.0 - gate)).astype(bf16)
@@ -247,35 +244,43 @@
     d_tri = inv_out * (grad - first_mean - tri_hat * second_mean)
     put_rows(slots, slice(None), jnp.where(mask > 0, d_tri, 0.0))
     send[...] = message_rows(slots)
-
-
-def back_kernel(received, left_all, right, d_right, send, slots):
+    write.wait()
+
+
+def padded_columns(rows):
+    spare = jnp.zeros((PAD - TI, 128), f32)
+    pieces = []
+    for e in range(E):
+        pieces += [rows[TI * e : TI * (e + 1)], spare]
+    block = jnp.concatenate(pieces, axis=0)
+    own = own_block((WIDTH, 128))
+    return jnp.concatenate(
+        [jnp.where(own == held, block, 0.0) for held in range(HELD)], axis=0
+    ).astype(bf16)
+
+
+def back_kernel(received, left_all, d_right, send, slots, ordered):
     own_rows(slots, received)
-    parts = parts_of(slots)
-    parts = swap_blocks(parts)
-    d_tri = jnp.concatenate(
-        [parts[i][t * R : (t + 1) * R] for t in range(3) for i in range(8)], axis=0
-    ).astype(bf16)
-    d_tri = dot(reorder(False), d_tri, ((1,), (0,))).astype(bf16)
+    parts = swap_blocks(parts_of(slots))
+    for t in range(3):
+        for i in range(8):
+            ordered[pl.ds((8 * t + i) * R, R), :] = parts[i][t * R : (t + 1) * R]
     total = jnp.zeros((FOLD, 128), f32)
-    own = own_block((WIDTH, 128))
     for q in range(Q):
-        block = d_tri[WIDTH * q : WIDTH * (q + 1)]
-        if HELD > 1:
-            block = jnp.concatenate(
-                [jnp.where(own == held, block, jnp.zeros_like(block)) for held in range(HELD)],
-                axis=0,
-            )
-        total = total + dot(left_all[q], block, ((1,), (0,)))
-        send[q] = pack_rows(dot(right[...], block, ((1,), (1,)))).astype(bf16)
+        rows = jnp.concatenate(
+            [ordered[residue_rows(E * q + e), :] for e in range(E)], axis=0
+        )
+        send[q] = rows.astype(bf16)
+        total = total + dot(left_all[q], padded_columns(rows), ((1,), (0,)))
     d_right[...] = total
 
 
-def spread_kernel(received, d_right, send, slots):
-    d_left = received[0].astype(f32)
-    for q in range(1, Q):
-        d_left = d_left + received[q].astype(f32)
-    d_left = unpack_rows(d_left)
+def spread_kernel(received, both, d_right, send, slots):
+    d_left = jnp.zeros((FOLD, 128), f32)
+    for q in range(Q):
+        right = unpack_rows(both[q, PACK:].astype(f32)).astype(bf16)
+        rows = padded_columns(received[q].astype(f32))
+        d_left = d_left + dot(right, rows, ((1,), (1,)))
     sides = (d_left, d_right[...])
     parts = [
         jnp.concatenate(
@@ -329,13 +334,16 @@
     pair_grad[...] = unpadded_rows(inv_in * (grad - first_mean - hat * second_mean), padded)
 
 
-def call(kernel, outs, scratch, *operands, spaces=None, vmem=40):
-    spaces = spaces or [pltpu.VMEM] * len(operands)
+def call(kernel, outs, scratch, *operands, inputs=None, written=(), vmem=40):
+    inputs = inputs or [pltpu.VMEM] * len(operands)
     return pl.pallas_call(
         kernel,
         out_shape=[jax.ShapeDtypeStruct(shape, dtype) for shape, dtype in outs],
-        in_specs=[pl.BlockSpec(memory_space=space) for space in spaces],
-        out_specs=[pl.BlockSpec(memory_space=pltpu.VMEM)] * len(outs),
+        in_specs=[pl.BlockSpec(memory_space=space) for space in inputs],
+        out_specs=[
+            pl.BlockSpec(memory_space=pl.ANY if n in written else pltpu.VMEM)
+            for n in range(len(outs))
+        ],
         scratch_shapes=[
             pltpu.VMEM(shape, f32) if isinstance(shape, tuple) else shape for shape in scratch
         ],
@@ -360,41 +368,44 @@
         project_kernel,
         [(BOTH, bf16), ((5 * C, LANES), f32), ((8, LANES), f32), ((24, C), f32)],
         [
-            padded, (3, 2 * C, 128), pltpu.VMEM((TI, TK, C), bf16), pltpu.VMEM((C, 5 * C), bf16),
-            (1, C), (1, C), (1, C), (1, C), pltpu.SemaphoreType.DMA((6,)),
+            padded, (3, 2 * C, 128), (5 * C, LANES), pltpu.SMEM((N,), jnp.int32),
+            pltpu.VMEM((TI, TK, C), bf16), (1, C), (1, C), pltpu.VMEM((C, 5 * C), bf16),
+            (1, C), (1, C), pltpu.SemaphoreType.DMA((8,)),
         ],
         crop, pair, in_gain, in_bias, in_weights, out_gain, out_bias,
-        spaces=[pltpu.SMEM] + [pl.ANY] * 6,
+        inputs=[pl.ANY] * 7,
+        written=(1,),
         vmem=58,
     )
-    left, right = call(
+    both, right = call(
         collect_kernel,
-        [((Q, PACK, 128), bf16), ((FOLD, 128), bf16)],
+        [((2 * PACK, 128), bf16), ((FOLD, 128), bf16)],
         [(3, 2 * C, 128)],
         exchange(send),
     )
-    left = lax.all_to_all(left, "zhi", 0, 0, tiled=True)
+    both = lax.all_gather(both, "zhi", axis=0)
     left_all, send = call(
         triangle_kernel,
         [((Q, FOLD, 128), bf16), (ONE, bf16)],
-        [(3, C, 128)],
-        left, right,
+        [(3, C, 128), (N, 128)],
+        both, right,
     )
     update, d_outpre, send = call(
         output_kernel,
         [tile, ((C, LANES), bf16), (ONE, bf16)],
-        [padded, (3, C, 128)],
+        [padded, (3, C, 128), pltpu.VMEM((TI, TK, C), bf16), pltpu.SemaphoreType.DMA(())],
         exchange(send), projected, inside, vectors, cotangent, out_weights,
+        written=(0,),
     )
     d_right, send = call(
         back_kernel,
-        [((FOLD, 128), f32), ((Q, PACK, 128), bf16)],
-        [(3, C, 128)],
-        exchange(send), left_all, right,
-    )
-    partial = lax.all_to_all(send, "zhi", 0, 0, tiled=True)
+        [((FOLD, 128), f32), ((Q, E * TI, 128), bf16)],
+        [(3, C, 128), (N, 128)],
+        exchange(send), left_all,
+    )
+    rows = lax.all_to_all(send, "zhi", 0, 0, tiled=True)
     (send,) = call(
-        spread_kernel, [(BOTH, bf16)], [(3, 2 * C, 128)], partial, d_right
+        spread_kernel, [(BOTH, bf16)], [(3, 2 * C, 128)], rows, both, d_right
     )
     (pair_grad,) = call(
         input_kernel,

time: 131 us -> 126 us (0.962)
  blocking collectives: 121 us -> 117 us
    all_to_all x2 -> x1, blocking collectives: 57.8 us -> 19 us  [body(): rows = lax.all_to_all(send, 'zhi', 0, 0, tiled=True)]
    all_gather x0 -> x1, blocking collectives: none -> 31.3 us  [body(): both = lax.all_gather(both, 'zhi', axis=0)]
    all_to_all x4, blocking collectives: 63.2 us -> 66.4 us  [exchange(): return lax.all_to_all(messages, OWNERS, 0, 0, tiled=True)]
where the time goes in v3:
time: 126 us
  blocking collectives  117 us (93%)
  Pallas kernels  8.41 us (7%)
    all_to_all x4, blocking collectives, exchange(): return lax.all_to_all(messages, OWNERS, 0, 0, tiled=True)  66.4 us
    all_gather x1, blocking collectives, body(): both = lax.all_gather(both, 'zhi', axis=0)  31.3 us
    all_to_all x1, blocking collectives, body(): rows = lax.all_to_all(send, 'zhi', 0, 0, tiled=True)  19 us
    pallas_call x7, Pallas kernels, call(): pl.pallas_call(kernel, out_shape=[jax.ShapeDtypeStruct(shape, dtype) for...  8.41 us

profile of v3, /device:TPU:1, one launch (start us, length us, event | category | flops | bytes accessed | tf_op | source)
XLA Modules:
  0.0 125.9 jit_solution(7547447301338407115)
XLA Ops:
  0.6 3.2 %project_kernel.1 = (bf16[64,4,384]{2,1,0:T(4,128)(2,1)}, f32[640,384]{1,0:T(8,128)}, f32[8,384]{1,0:T(8,128)}, f32[24,128]{1,0:T(8,128)}) custom-call(s32[384]{0:T(512)} %crop_hbm.1, bf16[12,24,128]{2,1,0:T(8,128)(2,1)} %bitcast.11, f32[1,128]{1,0:T(1,128)} %bitcast.15, f32[1,128]{1,0:T(1,128)} %bitcast.16, bf16[128,640]{1,0:T(8,128)(2,1)} %weights.3, ...), custom_call_target="tpu_custom_call" | custom-call | tf_op jit(solution)/shard_map/project_kernel/pallas_call | solution.py:339
  3.8 0.0 copy-start
  3.8 20.3 %all_to_all.25.received = bf16[64,4,384]{2,1,0:T(4,128)(2,1)S(1)} all-to-all(bf16[64,4,384]{2,1,0:T(4,128)(2,1)} %get-tuple-element.15), channel_id=1, replica_groups=mesh['xlo'=2,'y'=4,'core'=2,'zhi'=8,'zlo'=2,'xhi'=2] {'zlo','xhi','xlo',..., dimensions={0} | all-to-all | bytes 393216 | tf_op jit(solution)/shard_map/all_to_all | solution.py:356
  24.2 0.4 collect_kernel.1
  24.6 31.3 %all-gather = bf16[2304,128]{1,0:T(8,128)(2,1)S(1)} all-gather(bf16[288,128]{1,0:T(8,128)(2,1)S(1)} %get-tuple-element.16), channel_id=2, replica_groups=mesh['xlo'=2,'y'=4,'core'=2,'zhi'=8,'zlo'=2,'xhi'=2] {'zhi'}, dimensions={0}, use_global_device_ids=true | all-gather | bytes 663552 | tf_op jit(solution)/shard_map/all_gather | solution.py:386
  55.9 1.0 triangle_kernel.1
  56.9 0.0 copy-start.3
  56.9 0.0 copy-start.4
  56.9 0.0 copy-start.5
  56.9 0.0 copy-start.6
  56.9 17.5 %all_to_all.26.received = bf16[64,2,384]{2,1,0:T(2,128)(2,1)S(1)} all-to-all(bf16[64,2,384]{2,1,0:T(2,128)(2,1)S(1)} %get-tuple-element.18), channel_id=1, replica_groups=mesh['xlo'=2,'y'=4,'core'=2,'zhi'=8,'zlo'=2,'xhi'=2] {'zlo','xhi','xlo',..., dimensions={0} | all-to-all | bytes 196608 | tf_op jit(solution)/shard_map/all_to_all | solution.py:356
  74.5 0.0 copy-done
  74.5 0.0 copy-done.3
  74.5 0.0 copy-done.4
  74.5 0.0 copy-done.5
  74.5 0.0 copy-done.6
  74.5 1.2 output_kernel.1
  75.7 12.3 %all_to_all.27.received = bf16[64,2,384]{2,1,0:T(2,128)(2,1)S(1)} all-to-all(bf16[64,2,384]{2,1,0:T(2,128)(2,1)S(1)} %get-tuple-element.23), channel_id=1, replica_groups=mesh['xlo'=2,'y'=4,'core'=2,'zhi'=8,'zlo'=2,'xhi'=2] {'zlo','xhi','xlo',..., dimensions={0} | all-to-all | bytes 196608 | tf_op jit(solution)/shard_map/all_to_all | solution.py:356
  88.0 0.6 back_kernel.1
  88.6 19.0 %all_to_all.28.received = bf16[8,48,128]{2,1,0:T(8,128)(2,1)S(1)} all-to-all(bf16[8,48,128]{2,1,0:T(8,128)(2,1)S(1)} %get-tuple-element.25), channel_id=1, replica_groups=mesh['xlo'=2,'y'=4,'core'=2,'zhi'=8,'zlo'=2,'xhi'=2] {'zhi'}, dimensions={0} | all-to-all | bytes 196608 | tf_op jit(solution)/shard_map/all_to_all | solution.py:406
  107.6 0.6 spread_kernel.1
  108.3 0.0 copy-start.1
  108.3 0.0 copy-start.2
  108.3 16.3 %all_to_all.29.received = bf16[64,4,384]{2,1,0:T(4,128)(2,1)S(1)} all-to-all(bf16[64,4,384]{2,1,0:T(4,128)(2,1)S(1)} %spread_kernel.1), channel_id=1, replica_groups=mesh['xlo'=2,'y'=4,'core'=2,'zhi'=8,'zlo'=2,'xhi'=2] {'zlo','xhi','xlo',..., dimensions={0} | all-to-all | bytes 393216 | tf_op jit(solution)/shard_map/all_to_all | solution.py:356
  124.5 0.0 copy-done.1
  124.5 0.0 copy-done.2
  124.5 1.4 %input_kernel.1 = bf16[12,24,128]{2,1,0:T(8,128)(2,1)} custom-call(bf16[64,4,384]{2,1,0:T(4,128)(2,1)S(1)} %all_to_all.29.received, f32[640,384]{1,0:T(8,128)S(1)} %copy-done, f32[8,384]{1,0:T(8,128)S(1)} %copy-done.4, f32[24,128]{1,0:T(8,128)S(1)} %copy-done.5, bf16[128,384]{1,0:T(8,128)(2,1)S(1)} %get-tuple-element.27.d_outpre, ...), custom_call_target="tpu_custom_call" | custom-call | tf_op jit(solution)/shard_map/input_kernel/pallas_call | solution.py:339
Async XLA Ops:
  3.8 70.6 %copy-start = (f32[640,384]{1,0:T(8,128)S(1)}, f32[640,384]{1,0:T(8,128)}, u32[]{:S(2)}) copy-start(f32[640,384]{1,0:T(8,128)} %get-tuple-element.19.projected) | copy-start | bytes 2949124
  56.9 17.6 %copy-start.3 = (bf16[24,12,128]{2,0,1:T(8,128)(2,1)S(1)}, bf16[24,12,128]{2,0,1:T(8,128)(2,1)}, u32[]{:S(2)}) copy-start(bf16[24,12,128]{2,0,1:T(8,128)(2,1)} %param.17) | copy-start | bytes 221188
  56.9 17.6 %copy-start.4 = (f32[8,384]{1,0:T(8,128)S(1)}, f32[8,384]{1,0:T(8,128)}, u32[]{:S(2)}) copy-start(f32[8,384]{1,0:T(8,128)} %get-tuple-element.20.inside) | copy-start | bytes 36868
  56.9 17.6 %copy-start.5 = (f32[24,128]{1,0:T(8,128)S(1)}, f32[24,128]{1,0:T(8,128)}, u32[]{:S(2)}) copy-start(f32[24,128]{1,0:T(8,128)} %get-tuple-element.21.vectors) | copy-start | bytes 36868
  56.9 17.6 %copy-start.6 = (bf16[128,128]{1,0:T(8,128)(2,1)S(1)}, bf16[128,128]{1,0:T(8,128)(2,1)}, u32[]{:S(2)}) copy-start(bf16[128,128]{1,0:T(8,128)(2,1)} %weights.2) | copy-start | bytes 98308
  108.3 16.3 %copy-start.1 = (bf16[128,640]{1,0:T(8,128)(2,1)S(1)}, bf16[128,640]{1,0:T(8,128)(2,1)}, u32[]{:S(2)}) copy-start(bf16[128,640]{1,0:T(8,128)(2,1)} %weights.3) | copy-start | bytes 491524
  108.3 16.3 %copy-start.2 = (bf16[24,12,128]{2,0,1:T(8,128)(2,1)S(1)}, bf16[24,12,128]{2,0,1:T(8,128)(2,1)}, u32[]{:S(2)}) copy-start(bf16[24,12,128]{2,0,1:T(8,128)(2,1)} %param.9) | copy-start | bytes 221188

commit v4 on v3

v4 whole, which is shorter than its diff:
```python
import jax
import jax.numpy as jnp
from jax import lax
from jax.experimental import pallas as pl
from jax.experimental.pallas import tpu as pltpu
from jax.sharding import Mesh, PartitionSpec as P

norm_eps = 1e-05
f32 = jnp.float32
bf16 = jnp.bfloat16
ROWS = ("xlo", "y", "core")
COLS = ("zhi", "zlo", "xhi")
OWNERS = ("zlo", "xhi", "xlo", "y", "core")
TK, TI, PAD = 24, 12, 16
LANES = TK * PAD
E, R, Q = 4, 16, 8
HELD = 8 // E
WIDTH = 128 // HELD
C = 128
N = 384
FOLD = N // 2
PACK = FOLD * TI // PAD
GROUP = FOLD - PACK
RF = R // 2


def dot(first_op, second_op, dims):
    return lax.dot_general(first_op, second_op, (dims, ((), ())), preferred_element_type=f32)


def swap_blocks(parts):
    parts = list(parts)
    block = lax.broadcasted_iota(jnp.int32, parts[0].shape, 1) // PAD
    for step in (4, 2, 1):
        upper = (block & step) != 0
        for a in range(8):
            if a & step:
                continue
            b = a | step
            low, high = parts[a], parts[b]
            parts[a] = jnp.where(upper, pltpu.roll(high, step * PAD, 1), low)
            parts[b] = jnp.where(upper, high, pltpu.roll(low, 128 - step * PAD, 1))
    return parts


def as_column(row):
    return jnp.broadcast_to(row, (C, C)).T[:, :1]


def padded_rows(tile, scratch):
    tile = tile.astype(f32)
    for i in range(PAD):
        part = tile[i] if i < TI else jnp.zeros((TK, C), f32)
        scratch[pl.ds(i, TK, stride=PAD), :] = part
    return scratch[...]


def unpadded_rows(values, scratch):
    scratch[...] = values
    return jnp.stack([scratch[pl.ds(i, TK, stride=PAD), :] for i in range(TI)]).astype(bf16)


def parts_of(slots):
    return [
        jnp.concatenate([slots[n, from_owner(held, e), :] for n in range(slots.shape[0])], axis=0)
        for held in range(HELD)
        for e in range(E)
    ]


def pack_rows(values):
    spare = lax.broadcasted_iota(jnp.int32, (PACK, 128), 1) % PAD >= TI
    last = values[PACK:]
    moved = [pltpu.roll(last, TI - (PAD - TI) * g, 1) for g in range(3)]
    return jnp.where(spare, jnp.concatenate(moved, axis=0), values[:PACK])


def unpack_rows(packed):
    lane = lax.broadcasted_iota(jnp.int32, (GROUP, 128), 1) % PAD
    last = jnp.zeros((GROUP, 128), f32)
    for g in range(3):
        back = pltpu.roll(packed[GROUP * g : GROUP * (g + 1)], 128 - TI + (PAD - TI) * g, 1)
        last = jnp.where(lane // (PAD - TI) == g, back, last)
    spare = lax.broadcasted_iota(jnp.int32, (PACK, 128), 1) % PAD >= TI
    return jnp.concatenate([jnp.where(spare, 0.0, packed), last], axis=0)


def own_block(shape):
    return lax.broadcasted_iota(jnp.int32, shape, 1) // WIDTH


def norm_rows(values):
    centered = values - jnp.mean(values, axis=1, keepdims=True)
    inv_std = lax.rsqrt(jnp.mean(centered * centered, axis=1, keepdims=True) + norm_eps)
    return centered * inv_std, inv_std


def put_kind(slots, kind, values):
    for t in range(3):
        slots[3 * kind + t, :, :] = values[:, 128 * t : 128 * (t + 1)]


def get_kind(slots, kind):
    return jnp.concatenate([slots[3 * kind + t, :, :] for t in range(3)], axis=1)


def as_messages(slots):
    rows = jnp.concatenate([slots[n, :, :] for n in range(slots.shape[0])], axis=1)
    return rows.reshape(C // HELD, HELD, -1).astype(bf16)


def from_messages(slots, received):
    rows = received[...].astype(f32).reshape(C, -1)
    for n in range(slots.shape[0]):
        slots[n, :, :] = rows[:, 128 * n : 128 * (n + 1)]


def from_owner(held, e):
    return pl.ds(HELD * R * e + held, R, stride=HELD)


def project_kernel(
    crop_hbm, pair_hbm, gain_hbm, bias_hbm, weights_hbm, out_gain_hbm, out_bias_hbm,
    cotangent_hbm, out_weights_hbm, send, projected_hbm, inside, vectors, grad,
    padded, slots, projected, crop, pair, gain, bias, weights, out_gain, out_bias,
    cotangent, out_weights, arrived,
):
    sources = (
        crop_hbm, pair_hbm, gain_hbm, bias_hbm, weights_hbm, out_gain_hbm, out_bias_hbm,
        cotangent_hbm, out_weights_hbm,
    )
    targets = (crop, pair, gain, bias, weights, out_gain, out_bias, cotangent, out_weights)
    loads = [
        pltpu.make_async_copy(source, target, arrived.at[n])
        for n, (source, target) in enumerate(zip(sources, targets))
    ]
    for load in loads:
        load.start()
    loads[1].wait()
    hat, _ = norm_rows(padded_rows(pair[...], padded))
    loads[2].wait()
    loads[3].wait()
    normed = (hat * gain[...] + bias[...]).astype(bf16)
    loads[4].wait()
    projected[...] = dot(weights[...].T, normed, ((1,), (1,)))
    keep = pltpu.make_async_copy(projected, projected_hbm, arrived.at[9])
    keep.start()

    loads[0].wait()
    row_pos = lax.axis_index(ROWS)
    col_pos = lax.axis_index(COLS)
    lane = lax.broadcasted_iota(jnp.int32, (8, LANES), 1)
    crop_rows = jnp.zeros((8, LANES), jnp.int32)
    crop_cols = jnp.full((8, LANES), -1, jnp.int32)
    for k in range(TK):
        crop_rows = jnp.where(lane // PAD == k, crop[row_pos * TK + k], crop_rows)
    for i in range(TI):
        crop_cols = jnp.where(lane % PAD == i, crop[col_pos * TI + i], crop_cols)
    same = (crop_rows == crop_cols).astype(f32)
    inside[...] = same
    mask = same[:1, :]
    put_kind(slots, 0, mask * jax.nn.sigmoid(projected[2 * C : 3 * C]) * projected[:C])
    put_kind(slots, 1, mask * jax.nn.sigmoid(projected[3 * C : 4 * C]) * projected[C : 2 * C])
    for load in loads[5:]:
        load.wait()
    upstream = padded_rows(cotangent[...], padded).T
    d_value = (upstream * jax.nn.sigmoid(projected[4 * C :])).astype(bf16)
    value_grad = dot(out_weights[...], d_value, ((1,), (0,))) * as_column(out_gain[...])
    grad[...] = value_grad
    put_kind(slots, 2, jnp.where(mask > 0, value_grad, 0.0))
    send[...] = as_messages(slots)
    vectors[...] = jnp.concatenate(
        [jnp.broadcast_to(v[...], (8, C)) for v in (gain, out_gain, out_bias)], axis=0
    )
    keep.wait()


def collect_kernel(received, gathered, left, right, slots):
    from_messages(slots, received)
    parts = swap_blocks(parts_of(slots))
    for kind in range(3):
        pieces = []
        for t in range(3):
            for k in range(8):
                at = (3 * kind + t) * R
                pieces.append(parts[k][at : at + RF] + parts[k][at + RF : at + R])
        whole = jnp.concatenate(pieces, axis=0)
        gathered[PACK * kind : PACK * (kind + 1)] = pack_rows(whole).astype(bf16)
        if kind < 2:
            (left, right)[kind][...] = whole.astype(bf16)


def residue_rows(column):
    return pl.ds(column % 2 * TI * R + column // 2, TI, stride=R)


def own_rows(block):
    lanes = own_block((WIDTH, 128))
    own = block[:WIDTH]
    for held in range(1, HELD):
        own = jnp.where(lanes == held, block[WIDTH * held : WIDTH * (held + 1)], own)
    return own


def triangle_kernel(gathered, left, right, left_all, right_all, send, slots, ordered, folded):
    place = 2 * (lax.axis_index("zhi") % (Q // 2))
    spare = jnp.zeros((PAD - TI, 128), f32)
    for q in range(Q):
        left_q = unpack_rows(gathered[q, :PACK].astype(f32)).astype(bf16)
        right_q = unpack_rows(gathered[q, PACK : 2 * PACK].astype(f32)).astype(bf16)
        left_all[q] = left_q
        right_all[q] = right_q
        folded[...] = unpack_rows(gathered[q, 2 * PACK :].astype(f32))
        own_i = [folded[pl.ds(place + half, TK, stride=RF), :] for half in range(2)]
        pieces = []
        for e in range(E):
            pieces += [own_i[e // 2][e % 2 * TI : (e % 2 + 1) * TI], spare]
        blocks = (
            dot(left_q, right[...], ((0,), (0,))),
            dot(right_q, left[...], ((0,), (0,))),
            jnp.concatenate(pieces * HELD, axis=0).T,
        )
        for kind, block in enumerate(blocks):
            own = own_rows(block)
            for e in range(E):
                ordered[kind, residue_rows(E * q + e), :] = own[PAD * e : PAD * e + TI]
    parts = swap_blocks(
        [
            jnp.concatenate(
                [ordered[kind, (8 * t + i) * R : (8 * t + i + 1) * R] for kind in range(3) for t in range(3)],
                axis=0,
            )
            for i in range(8)
        ]
    )
    for held in range(HELD):
        for e in range(E):
            part = parts[held * E + e]
            for n in range(9):
                slots[n, from_owner(held, e), :] = part[n * R : (n + 1) * R]
    send[...] = as_messages(slots)


def norm_tri(slots, kind, mask):
    tri = jnp.where(mask, get_kind(slots, kind), 0.0)
    centered = tri - jnp.mean(tri, axis=0, keepdims=True)
    inv_out = lax.rsqrt(jnp.mean(centered * centered, axis=0, keepdims=True) + norm_eps)
    return centered * inv_out, inv_out


def norm_back(grad, tri_hat, inv_out, mask):
    first_mean = jnp.mean(grad, axis=0, keepdims=True)
    second_mean = jnp.mean(grad * tri_hat, axis=0, keepdims=True)
    return jnp.where(mask, inv_out * (grad - first_mean - tri_hat * second_mean), 0.0)


def output_kernel(
    received, projected, inside, vectors, grad, cotangent, weights, update_hbm, d_outpre, send,
    padded, slots, slots_back, update, written,
):
    mask = inside[:1, :] > 0
    from_messages(slots, received)
    tri_hat, inv_out = norm_tri(slots, 0, mask)
    normed_out = (tri_hat * as_column(vectors[8:9]) + as_column(vectors[16:17])).astype(bf16)
    gated_value = dot(weights[...].T, normed_out, ((1,), (0,)))
    gate = jax.nn.sigmoid(projected[4 * C :])
    update[...] = unpadded_rows((gate * gated_value).T, padded)
    write = pltpu.make_async_copy(update, update_hbm, written)
    write.start()
    put_kind(slots_back, 0, norm_back(grad[...], tri_hat, inv_out, mask))
    mirror_hat, mirror_inv = norm_tri(slots, 1, mask)
    mirror_grad = jnp.where(mask, get_kind(slots, 2), 0.0)
    put_kind(slots_back, 1, norm_back(mirror_grad, mirror_hat, mirror_inv, mask))
    send[...] = as_messages(slots_back)
    upstream = padded_rows(cotangent[...], padded).T
    d_outpre[...] = (upstream * gated_value * gate * (1.0 - gate)).astype(bf16)
    write.wait()


def padded_columns(rows):
    spare = jnp.zeros((PAD - TI, 128), f32)
    pieces = []
    for e in range(E):
        pieces += [rows[TI * e : TI * (e + 1)], spare]
    block = jnp.concatenate(pieces, axis=0)
    own = own_block((WIDTH, 128))
    return jnp.concatenate(
        [jnp.where(own == held, block, 0.0) for held in range(HELD)], axis=0
    ).astype(bf16)


def back_kernel(received, left_all, right_all, send, slots, ordered):
    from_messages(slots, received)
    parts = swap_blocks(parts_of(slots))
    for kind in range(2):
        for t in range(3):
            for i in range(8):
                n = 3 * kind + t
                ordered[kind, pl.ds((8 * t + i) * R, R), :] = parts[i][n * R : (n + 1) * R]
    d_left = jnp.zeros((FOLD, 128), f32)
    d_right = jnp.zeros((FOLD, 128), f32)
    for q in range(Q):
        by_i, by_j = (
            padded_columns(
                jnp.concatenate([ordered[kind, residue_rows(E * q + e), :] for e in range(E)], axis=0)
            )
            for kind in range(2)
        )
        d_right = d_right + dot(left_all[q], by_i, ((1,), (0,)))
        d_left = d_left + dot(right_all[q], by_j, ((1,), (0,)))
    sides = (d_left, d_right)
    parts = swap_blocks(
        [
            jnp.concatenate(
                [
                    sides[side][(8 * t + k) * RF : (8 * t + k + 1) * RF]
                    for side in range(2)
                    for t in range(3)
                ],
                axis=0,
            )
            for k in range(8)
        ]
    )
    for held in range(HELD):
        for e in range(E):
            part = parts[held * E + e]
            for n in range(6):
                piece = part[n * RF : (n + 1) * RF]
                for half in range(2):
                    start = HELD * (R * e + RF * half) + held
                    slots[n, pl.ds(start, RF, stride=HELD), :] = piece
    send[...] = as_messages(slots)


def input_kernel(
    received, projected, inside, vectors, d_outpre, pair, weights, pair_grad, padded, slots
):
    from_messages(slots, received)
    mask = inside[:1, :]
    d_left = get_kind(slots, 0) * mask
    d_right = get_kind(slots, 1) * mask
    left_val, right_val = projected[:C], projected[C : 2 * C]
    left_sig = jax.nn.sigmoid(projected[2 * C : 3 * C])
    right_sig = jax.nn.sigmoid(projected[3 * C : 4 * C])
    d_proj = jnp.concatenate(
        [
            (d_left * left_sig).astype(bf16),
            (d_right * right_sig).astype(bf16),
            (d_left * left_val * left_sig * (1.0 - left_sig)).astype(bf16),
            (d_right * right_val * right_sig * (1.0 - right_sig)).astype(bf16),
            d_outpre[...],
        ],
        axis=0,
    )
    grad = dot(weights[...], d_proj, ((1,), (0,))).T * vectors[:1]
    hat, inv_in = norm_rows(padded_rows(pair[...], padded))
    first_mean = jnp.mean(grad, axis=1, keepdims=True)
    second_mean = jnp.mean(grad * hat, axis=1, keepdims=True)
    pair_grad[...] = unpadded_rows(inv_in * (grad - first_mean - hat * second_mean), padded)


def call(kernel, outs, scratch, *operands, inputs=None, written=(), vmem=40):
    inputs = inputs or [pltpu.VMEM] * len(operands)
    return pl.pallas_call(
        kernel,
        out_shape=[jax.ShapeDtypeStruct(shape, dtype) for shape, dtype in outs],
        in_specs=[pl.BlockSpec(memory_space=space) for space in inputs],
        out_specs=[
            pl.BlockSpec(memory_space=pl.ANY if n in written else pltpu.VMEM)
            for n in range(len(outs))
        ],
        scratch_shapes=[
            pltpu.VMEM(shape, f32) if isinstance(shape, tuple) else shape for shape in scratch
        ],
        compiler_params=pltpu.CompilerParams(vmem_limit_bytes=vmem * 1024 * 1024),
        name=kernel.__name__,
    )(*operands)


def exchange(messages):
    return lax.all_to_all(messages, OWNERS, 0, 0, tiled=True)


def body(pair, crop, in_gain, in_bias, in_weights, out_gain, out_bias, out_weights, cotangent):
    padded = (LANES, C)
    tile = ((TI, TK, C), bf16)
    pair = pair.transpose(1, 0, 2)
    cotangent = cotangent.transpose(1, 0, 2)
    in_gain, in_bias, out_gain, out_bias = (
        v.reshape(1, C) for v in (in_gain, in_bias, out_gain, out_bias)
    )
    def messages(kinds):
        return ((C // HELD, HELD, kinds * LANES), bf16)

    def slots(kinds):
        return (3 * kinds, C, 128)

    every_block = ((Q, FOLD, 128), bf16)
    own = ((FOLD, 128), bf16)
    send, projected, inside, vectors, grad = call(
        project_kernel,
        [messages(3), ((5 * C, LANES), f32), ((8, LANES), f32), ((24, C), f32), ((C, LANES), f32)],
        [
            padded, slots(3), (5 * C, LANES), pltpu.SMEM((N,), jnp.int32),
            pltpu.VMEM((TI, TK, C), bf16), (1, C), (1, C), pltpu.VMEM((C, 5 * C), bf16),
            (1, C), (1, C), pltpu.VMEM((TI, TK, C), bf16), pltpu.VMEM((C, C), bf16),
            pltpu.SemaphoreType.DMA((10,)),
        ],
        crop, pair, in_gain, in_bias, in_weights, out_gain, out_bias, cotangent, out_weights,
        inputs=[pl.ANY] * 9,
        written=(1,),
        vmem=58,
    )
    gathered, left, right = call(
        collect_kernel,
        [((3 * PACK, 128), bf16), own, own],
        [slots(3)],
        exchange(send),
    )
    left_all, right_all, send = call(
        triangle_kernel,
        [every_block, every_block, messages(3)],
        [slots(3), (3, N, 128), (FOLD, 128)],
        lax.all_gather(gathered, "zhi", axis=0), left, right,
    )
    update, d_outpre, send = call(
        output_kernel,
        [tile, ((C, LANES), bf16), messages(2)],
        [
            padded, slots(3), slots(2), pltpu.VMEM((TI, TK, C), bf16), pltpu.SemaphoreType.DMA(()),
        ],
        exchange(send), projected, inside, vectors, grad, cotangent, out_weights,
        written=(0,),
    )
    (send,) = call(
        back_kernel,
        [messages(2)],
        [slots(2), (2, N, 128)],
        exchange(send), left_all, right_all,
    )
    (pair_grad,) = call(
        input_kernel,
        [tile],
        [padded, slots(2)],
        exchange(send), projected, inside, vectors, d_outpre, pair, in_weights,
    )
    return update.transpose(1, 0, 2), pair_grad.transpose(1, 0, 2)


def solution(mesh):
    split = Mesh(mesh.devices.reshape(2, 4, 2, Q, 16 // Q, 2), ROWS + COLS)
    tiles = P(ROWS, COLS, None)
    in_specs = (tiles, P(), P(), P(), P(), P(), P(), P(), tiles)
    return jax.shard_map(
        body, mesh=split, in_specs=in_specs, out_specs=(tiles, tiles), check_vma=False
    )
```

time: 126 us -> 112 us (0.89)
  blocking collectives: 117 us -> 101 us
  Pallas kernels: 8.41 us -> 10.3 us
    all_to_all x1 -> x0, blocking collectives: 19 us -> none  [body(): rows = lax.all_to_all(send, 'zhi', 0, 0, tiled=True)]
    all_gather x1, blocking collectives: 31.3 us -> 33.7 us  [body(): lax.all_gather(gathered, 'zhi', axis=0)]
    pallas_call x7 -> x6, Pallas kernels: 8.41 us -> 10.3 us  [call(): pl.pallas_call(kernel, out_shape=[jax.ShapeDtypeStruct(shape, dtype) for...]
where the time goes in v4:
time: 112 us
  blocking collectives  101 us (90%)
  Pallas kernels  10.3 us (9%)
    all_to_all x4, blocking collectives, exchange(): return lax.all_to_all(messages, OWNERS, 0, 0, tiled=True)  67.1 us
    all_gather x1, blocking collectives, body(): lax.all_gather(gathered, 'zhi', axis=0)  33.7 us
    pallas_call x6, Pallas kernels, call(): pl.pallas_call(kernel, out_shape=[jax.ShapeDtypeStruct(shape, dtype) for...  10.3 us

profile of v4, /device:TPU:1, one launch (start us, length us, event | category | flops | bytes accessed | tf_op | source)
XLA Modules:
  0.0 111.9 jit_solution(258601975391231880)
XLA Ops:
  0.6 3.3 %project_kernel.1 = (bf16[64,2,1152]{2,1,0:T(2,128)(2,1)}, f32[640,384]{1,0:T(8,128)}, f32[8,384]{1,0:T(8,128)}, f32[24,128]{1,0:T(8,128)}, f32[128,384]{1,0:T(8,128)}) custom-call(s32[384]{0:T(512)} %crop_hbm.1, bf16[12,24,128]{2,1,0:T(8,128)(2,1)} %bitcast.12, f32[1,128]{1,0:T(1,128)} %bitcast.15, f32[1,128]{1,0:T(1,128)} %bitcast.16, ...), custom_call_target="tpu_custom_call" | custom-call | tf_op jit(solution)/shard_map/project_kernel/pallas_call | solution.py:365
  4.0 21.2 %all_to_all.20.received = bf16[64,2,1152]{2,1,0:T(2,128)(2,1)S(1)} all-to-all(bf16[64,2,1152]{2,1,0:T(2,128)(2,1)} %get-tuple-element.16), channel_id=1, replica_groups=mesh['xlo'=2,'y'=4,'core'=2,'zhi'=8,'zlo'=2,'xhi'=2] {'zlo','xhi','xlo',..., dimensions={0} | all-to-all | bytes 589824 | tf_op jit(solution)/shard_map/all_to_all | solution.py:382
  25.1 0.7 collect_kernel.1
  25.8 33.7 %all-gather = bf16[3456,128]{1,0:T(8,128)(2,1)S(1)} all-gather(bf16[432,128]{1,0:T(8,128)(2,1)S(1)} %get-tuple-element.17), channel_id=2, replica_groups=mesh['xlo'=2,'y'=4,'core'=2,'zhi'=8,'zlo'=2,'xhi'=2] {'zhi'}, dimensions={0}, use_global_device_ids=true | all-gather | bytes 995328 | tf_op jit(solution)/shard_map/all_gather | solution.py:425
  59.5 0.0 copy-start
  59.5 1.9 %triangle_kernel.1 = (bf16[8,192,128]{2,1,0:T(8,128)(2,1)S(1)}, bf16[8,192,128]{2,1,0:T(8,128)(2,1)S(1)}, bf16[64,2,1152]{2,1,0:T(2,128)(2,1)S(1)}) custom-call(bf16[8,432,128]{2,1,0:T(8,128)(2,1)S(1)} %bitcast.9, bf16[192,128]{1,0:T(8,128)(2,1)S(1)} %get-tuple-element.18.left, bf16[192,128]{1,0:T(8,128)(2,1)S(1)} %get-tuple-element.19.right), custom_call_target="tpu_custom_call" | custom-call | tf_op jit(solution)/shard_map/triangle_kernel/pallas_call | solution.py:365
  61.4 0.0 copy-start.2
  61.4 0.0 copy-start.4
  61.4 0.0 copy-start.5
  61.4 0.0 copy-start.6
  61.4 0.0 copy-start.7
  61.4 19.5 %all_to_all.21.received = bf16[64,2,1152]{2,1,0:T(2,128)(2,1)S(1)} all-to-all(bf16[64,2,1152]{2,1,0:T(2,128)(2,1)S(1)} %get-tuple-element.20), channel_id=1, replica_groups=mesh['xlo'=2,'y'=4,'core'=2,'zhi'=8,'zlo'=2,'xhi'=2] {'zlo','xhi','xlo',..., dimensions={0} | all-to-all | bytes 589824 | tf_op jit(solution)/shard_map/all_to_all | solution.py:382
  80.9 0.0 copy-done
  80.9 0.0 copy-done.2
  80.9 0.0 copy-done.4
  80.9 0.0 copy-done.5
  81.0 0.0 copy-done.6
  81.0 0.0 copy-done.7
  81.0 1.7 %output_kernel.1 = (bf16[12,24,128]{2,1,0:T(8,128)(2,1)}, bf16[128,384]{1,0:T(8,128)(2,1)S(1)}, bf16[64,2,768]{2,1,0:T(2,128)(2,1)S(1)}) custom-call(bf16[64,2,1152]{2,1,0:T(2,128)(2,1)S(1)} %all_to_all.21.received, f32[640,384]{1,0:T(8,128)S(1)} %copy-done, f32[8,384]{1,0:T(8,128)S(1)} %copy-done.6, f32[24,128]{1,0:T(8,128)S(1)} %copy-done.7, ...), custom_call_target="tpu_custom_call" | custom-call | tf_op jit(solution)/shard_map/output_kernel/pallas_call | solution.py:365
  82.6 13.1 %all_to_all.22.received = bf16[64,2,768]{2,1,0:T(2,128)(2,1)S(1)} all-to-all(bf16[64,2,768]{2,1,0:T(2,128)(2,1)S(1)} %get-tuple-element.26), channel_id=1, replica_groups=mesh['xlo'=2,'y'=4,'core'=2,'zhi'=8,'zlo'=2,'xhi'=2] {'zlo','xhi','xlo',..., dimensions={0} | all-to-all | bytes 393216 | tf_op jit(solution)/shard_map/all_to_all | solution.py:382
  95.8 1.3 %back_kernel.1 = bf16[64,2,768]{2,1,0:T(2,128)(2,1)S(1)} custom-call(bf16[64,2,768]{2,1,0:T(2,128)(2,1)S(1)} %all_to_all.22.received, bf16[8,192,128]{2,1,0:T(8,128)(2,1)S(1)} %get-tuple-element.27.left_all, bf16[8,192,128]{2,1,0:T(8,128)(2,1)S(1)} %get-tuple-element.28.right_all), custom_call_target="tpu_custom_call" | custom-call | tf_op jit(solution)/shard_map/back_kernel/pallas_call | solution.py:365
  97.1 0.0 copy-start.1
  97.1 0.0 copy-start.3
  97.1 13.3 %all_to_all.23.received = bf16[64,2,768]{2,1,0:T(2,128)(2,1)S(1)} all-to-all(bf16[64,2,768]{2,1,0:T(2,128)(2,1)S(1)} %back_kernel.1), channel_id=1, replica_groups=mesh['xlo'=2,'y'=4,'core'=2,'zhi'=8,'zlo'=2,'xhi'=2] {'zlo','xhi','xlo',..., dimensions={0} | all-to-all | bytes 393216 | tf_op jit(solution)/shard_map/all_to_all | solution.py:382
  110.4 0.0 copy-done.1
  110.4 0.0 copy-done.3
  110.4 1.4 %input_kernel.1 = bf16[12,24,128]{2,1,0:T(8,128)(2,1)} custom-call(bf16[64,2,768]{2,1,0:T(2,128)(2,1)S(1)} %all_to_all.23.received, f32[640,384]{1,0:T(8,128)S(1)} %copy-done, f32[8,384]{1,0:T(8,128)S(1)} %copy-done.6, f32[24,128]{1,0:T(8,128)S(1)} %copy-done.7, bf16[128,384]{1,0:T(8,128)(2,1)S(1)} %get-tuple-element.29.d_outpre, ...), custom_call_target="tpu_custom_call" | custom-call | tf_op jit(solution)/shard_map/input_kernel/pallas_call | solution.py:365
Async XLA Ops:
  59.5 21.4 %copy-start = (f32[640,384]{1,0:T(8,128)S(1)}, f32[640,384]{1,0:T(8,128)}, u32[]{:S(2)}) copy-start(f32[640,384]{1,0:T(8,128)} %get-tuple-element.21.projected) | copy-start | bytes 2949124
  61.4 19.5 %copy-start.2 = (bf16[24,12,128]{2,0,1:T(8,128)(2,1)S(1)}, bf16[24,12,128]{2,0,1:T(8,128)(2,1)}, u32[]{:S(2)}) copy-start(bf16[24,12,128]{2,0,1:T(8,128)(2,1)} %param.17) | copy-start | bytes 221188
  61.4 19.5 %copy-start.4 = (f32[128,384]{1,0:T(8,128)S(1)}, f32[128,384]{1,0:T(8,128)}, u32[]{:S(2)}) copy-start(f32[128,384]{1,0:T(8,128)} %get-tuple-element.24.grad) | copy-start | bytes 589828
  61.4 19.5 %copy-start.5 = (bf16[128,128]{1,0:T(8,128)(2,1)S(1)}, bf16[128,128]{1,0:T(8,128)(2,1)}, u32[]{:S(2)}) copy-start(bf16[128,128]{1,0:T(8,128)(2,1)} %weights.2) | copy-start | bytes 98308
  61.4 19.5 %copy-start.6 = (f32[8,384]{1,0:T(8,128)S(1)}, f32[8,384]{1,0:T(8,128)}, u32[]{:S(2)}) copy-start(f32[8,384]{1,0:T(8,128)} %get-tuple-element.22.inside) | copy-start | bytes 36868
  61.4 19.5 %copy-start.7 = (f32[24,128]{1,0:T(8,128)S(1)}, f32[24,128]{1,0:T(8,128)}, u32[]{:S(2)}) copy-start(f32[24,128]{1,0:T(8,128)} %get-tuple-element.23.vectors) | copy-start | bytes 36868
  97.1 13.3 %copy-start.1 = (bf16[128,640]{1,0:T(8,128)(2,1)S(1)}, bf16[128,640]{1,0:T(8,128)(2,1)}, u32[]{:S(2)}) copy-start(bf16[128,640]{1,0:T(8,128)(2,1)} %weights.3) | copy-start | bytes 491524
  97.1 13.3 %copy-start.3 = (bf16[24,12,128]{2,0,1:T(8,128)(2,1)S(1)}, bf16[24,12,128]{2,0,1:T(8,128)(2,1)}, u32[]{:S(2)}) copy-start(bf16[24,12,128]{2,0,1:T(8,128)(2,1)} %param.9) | copy-start | bytes 221188

commit v5 on v4

--- a/solution.py
+++ b/solution.py
@@ -60,12 +60,13 @@
     return jnp.stack([scratch[pl.ds(i, TK, stride=PAD), :] for i in range(TI)]).astype(bf16)
 
 
-def parts_of(slots):
-    return [
-        jnp.concatenate([slots[n, from_owner(held, e), :] for n in range(slots.shape[0])], axis=0)
-        for held in range(HELD)
-        for e in range(E)
-    ]
+def parts_of(slots, kinds):
+    parts = []
+    for held in range(HELD):
+        for e in range(E):
+            packed = [slots[n, from_owner(held, e), :] for n in range(slots.shape[0])]
+            parts.append(jnp.concatenate(unpack_slabs(packed, 3 * kinds), axis=0))
+    return parts
 
 
 def pack_rows(values):
@@ -95,24 +96,56 @@
     return centered * inv_std, inv_std
 
 
-def put_kind(slots, kind, values):
-    for t in range(3):
-        slots[3 * kind + t, :, :] = values[:, 128 * t : 128 * (t + 1)]
-
-
-def get_kind(slots, kind):
-    return jnp.concatenate([slots[3 * kind + t, :, :] for t in range(3)], axis=1)
-
-
-def as_messages(slots):
-    rows = jnp.concatenate([slots[n, :, :] for n in range(slots.shape[0])], axis=1)
-    return rows.reshape(C // HELD, HELD, -1).astype(bf16)
-
-
-def from_messages(slots, received):
+def slabs_of(values):
+    return [values[:, 128 * t : 128 * (t + 1)] for t in range(3)]
+
+
+def get_kind(slabs, kind):
+    return jnp.concatenate(slabs[3 * kind : 3 * kind + 3], axis=1)
+
+
+def pack_slabs(slabs):
+    rest, packed = list(slabs), []
+    lane = lax.broadcasted_iota(jnp.int32, rest[0].shape, 1) % PAD
+    while len(rest) >= 4:
+        for g in range(3):
+            moved = pltpu.roll(rest[3], TI - (PAD - TI) * g, 1)
+            packed.append(jnp.where(lane >= TI, moved, rest[g]))
+        rest = rest[4:]
+    return packed + rest
+
+
+def unpack_slabs(packed, count):
+    rest, slabs = list(packed), []
+    lane = lax.broadcasted_iota(jnp.int32, rest[0].shape, 1) % PAD
+    while count - len(slabs) >= 4:
+        back = [pltpu.roll(rest[g], 128 - TI + (PAD - TI) * g, 1) for g in range(3)]
+        last = jnp.where(lane < 4, back[0], jnp.where(lane < 8, back[1], back[2]))
+        slabs += rest[:3] + [last]
+        rest = rest[3:]
+    return slabs + rest
+
+
+def packed_count(kinds):
+    return 3 * kinds - 3 * kinds // 4
+
+
+def as_messages(packed):
+    return jnp.concatenate(packed, axis=1).reshape(C // HELD, HELD, -1).astype(bf16)
+
+
+def from_messages(received):
     rows = received[...].astype(f32).reshape(C, -1)
-    for n in range(slots.shape[0]):
-        slots[n, :, :] = rows[:, 128 * n : 128 * (n + 1)]
+    return [rows[:, n : n + 128] for n in range(0, rows.shape[1], 128)]
+
+
+def fill_slots(slots, received):
+    for n, slab in enumerate(from_messages(received)):
+        slots[n, :, :] = slab
+
+
+def all_slots(slots):
+    return [slots[n, :, :] for n in range(slots.shape[0])]
 
 
 def from_owner(held, e):
@@ -122,7 +155,7 @@
 def project_kernel(
     crop_hbm, pair_hbm, gain_hbm, bias_hbm, weights_hbm, out_gain_hbm, out_bias_hbm,
     cotangent_hbm, out_weights_hbm, send, projected_hbm, inside, vectors, grad,
-    padded, slots, projected, crop, pair, gain, bias, weights, out_gain, out_bias,
+    padded, projected, crop, pair, gain, bias, weights, out_gain, out_bias,
     cotangent, out_weights, arrived,
 ):
     sources = (
@@ -159,16 +192,18 @@
     same = (crop_rows == crop_cols).astype(f32)
     inside[...] = same
     mask = same[:1, :]
-    put_kind(slots, 0, mask * jax.nn.sigmoid(projected[2 * C : 3 * C]) * projected[:C])
-    put_kind(slots, 1, mask * jax.nn.sigmoid(projected[3 * C : 4 * C]) * projected[C : 2 * C])
+    left = mask * jax.nn.sigmoid(projected[2 * C : 3 * C]) * projected[:C]
+    right = mask * jax.nn.sigmoid(projected[3 * C : 4 * C]) * projected[C : 2 * C]
     for load in loads[5:]:
         load.wait()
     upstream = padded_rows(cotangent[...], padded).T
     d_value = (upstream * jax.nn.sigmoid(projected[4 * C :])).astype(bf16)
     value_grad = dot(out_weights[...], d_value, ((1,), (0,))) * as_column(out_gain[...])
     grad[...] = value_grad
-    put_kind(slots, 2, jnp.where(mask > 0, value_grad, 0.0))
-    send[...] = as_messages(slots)
+    masked_grad = jnp.where(mask > 0, value_grad, 0.0)
+    send[...] = as_messages(
+        pack_slabs(slabs_of(left) + slabs_of(right) + slabs_of(masked_grad))
+    )
     vectors[...] = jnp.concatenate(
         [jnp.broadcast_to(v[...], (8, C)) for v in (gain, out_gain, out_bias)], axis=0
     )
@@ -176,8 +211,8 @@
 
 
 def collect_kernel(received, gathered, left, right, slots):
-    from_messages(slots, received)
-    parts = swap_blocks(parts_of(slots))
+    fill_slots(slots, received)
+    parts = swap_blocks(parts_of(slots, 3))
     for kind in range(3):
         pieces = []
         for t in range(3):
@@ -236,13 +271,13 @@
     for held in range(HELD):
         for e in range(E):
             part = parts[held * E + e]
-            for n in range(9):
-                slots[n, from_owner(held, e), :] = part[n * R : (n + 1) * R]
-    send[...] = as_messages(slots)
-
-
-def norm_tri(slots, kind, mask):
-    tri = jnp.where(mask, get_kind(slots, kind), 0.0)
+            for n, slab in enumerate(pack_slabs([part[n * R : (n + 1) * R] for n in range(9)])):
+                slots[n, from_owner(held, e), :] = slab
+    send[...] = as_messages(all_slots(slots))
+
+
+def norm_tri(slabs, kind, mask):
+    tri = jnp.where(mask, get_kind(slabs, kind), 0.0)
     centered = tri - jnp.mean(tri, axis=0, keepdims=True)
     inv_out = lax.rsqrt(jnp.mean(centered * centered, axis=0, keepdims=True) + norm_eps)
     return centered * inv_out, inv_out
@@ -256,22 +291,22 @@
 
 def output_kernel(
     received, projected, inside, vectors, grad, cotangent, weights, update_hbm, d_outpre, send,
-    padded, slots, slots_back, update, written,
+    padded, update, written,
 ):
     mask = inside[:1, :] > 0
-    from_messages(slots, received)
-    tri_hat, inv_out = norm_tri(slots, 0, mask)
+    slabs = unpack_slabs(from_messages(received), 9)
+    tri_hat, inv_out = norm_tri(slabs, 0, mask)
     normed_out = (tri_hat * as_column(vectors[8:9]) + as_column(vectors[16:17])).astype(bf16)
     gated_value = dot(weights[...].T, normed_out, ((1,), (0,)))
     gate = jax.nn.sigmoid(projected[4 * C :])
     update[...] = unpadded_rows((gate * gated_value).T, padded)
     write = pltpu.make_async_copy(update, update_hbm, written)
     write.start()
-    put_kind(slots_back, 0, norm_back(grad[...], tri_hat, inv_out, mask))
-    mirror_hat, mirror_inv = norm_tri(slots, 1, mask)
-    mirror_grad = jnp.where(mask, get_kind(slots, 2), 0.0)
-    put_kind(slots_back, 1, norm_back(mirror_grad, mirror_hat, mirror_inv, mask))
-    send[...] = as_messages(slots_back)
+    d_tri = norm_back(grad[...], tri_hat, inv_out, mask)
+    mirror_hat, mirror_inv = norm_tri(slabs, 1, mask)
+    mirror_grad = jnp.where(mask, get_kind(slabs, 2), 0.0)
+    d_mirror = norm_back(mirror_grad, mirror_hat, mirror_inv, mask)
+    send[...] = as_messages(pack_slabs(slabs_of(d_tri) + slabs_of(d_mirror)))
     upstream = padded_rows(cotangent[...], padded).T
     d_outpre[...] = (upstream * gated_value * gate * (1.0 - gate)).astype(bf16)
     write.wait()
@@ -290,8 +325,8 @@
 
 
 def back_kernel(received, left_all, right_all, send, slots, ordered):
-    from_messages(slots, received)
-    parts = swap_blocks(parts_of(slots))
+    fill_slots(slots, received)
+    parts = swap_blocks(parts_of(slots, 2))
     for kind in range(2):
         for t in range(3):
             for i in range(8):
@@ -325,21 +360,20 @@
     for held in range(HELD):
         for e in range(E):
             part = parts[held * E + e]
-            for n in range(6):
-                piece = part[n * RF : (n + 1) * RF]
+            for n, slab in enumerate(pack_slabs([part[n * RF : (n + 1) * RF] for n in range(6)])):
                 for half in range(2):
                     start = HELD * (R * e + RF * half) + held
-                    slots[n, pl.ds(start, RF, stride=HELD), :] = piece
-    send[...] = as_messages(slots)
+                    slots[n, pl.ds(start, RF, stride=HELD), :] = slab
+    send[...] = as_messages(all_slots(slots))
 
 
 def input_kernel(
-    received, projected, inside, vectors, d_outpre, pair, weights, pair_grad, padded, slots
+    received, projected, inside, vectors, d_outpre, pair, weights, pair_grad, padded
 ):
-    from_messages(slots, received)
+    slabs = unpack_slabs(from_messages(received), 6)
     mask = inside[:1, :]
-    d_left = get_kind(slots, 0) * mask
-    d_right = get_kind(slots, 1) * mask
+    d_left = get_kind(slabs, 0) * mask
+    d_right = get_kind(slabs, 1) * mask
     left_val, right_val = projected[:C], projected[C : 2 * C]
     left_sig = jax.nn.sigmoid(projected[2 * C : 3 * C])
     right_sig = jax.nn.sigmoid(projected[3 * C : 4 * C])
@@ -391,10 +425,10 @@
         v.reshape(1, C) for v in (in_gain, in_bias, out_gain, out_bias)
     )
     def messages(kinds):
-        return ((C // HELD, HELD, kinds * LANES), bf16)
+        return ((C // HELD, HELD, 128 * packed_count(kinds)), bf16)
 
     def slots(kinds):
-        return (3 * kinds, C, 128)
+        return (packed_count(kinds), C, 128)
 
     every_block = ((Q, FOLD, 128), bf16)
     own = ((FOLD, 128), bf16)
@@ -402,7 +436,7 @@
         project_kernel,
         [messages(3), ((5 * C, LANES), f32), ((8, LANES), f32), ((24, C), f32), ((C, LANES), f32)],
         [
-            padded, slots(3), (5 * C, LANES), pltpu.SMEM((N,), jnp.int32),
+            padded, (5 * C, LANES), pltpu.SMEM((N,), jnp.int32),
             pltpu.VMEM((TI, TK, C), bf16), (1, C), (1, C), pltpu.VMEM((C, 5 * C), bf16),
             (1, C), (1, C), pltpu.VMEM((TI, TK, C), bf16), pltpu.VMEM((C, C), bf16),
             pltpu.SemaphoreType.DMA((10,)),
@@ -428,7 +462,7 @@
         output_kernel,
         [tile, ((C, LANES), bf16), messages(2)],
         [
-            padded, slots(3), slots(2), pltpu.VMEM((TI, TK, C), bf16), pltpu.SemaphoreType.DMA(()),
+            padded, pltpu.VMEM((TI, TK, C), bf16), pltpu.SemaphoreType.DMA(()),
         ],
         exchange(send), projected, inside, vectors, grad, cotangent, out_weights,
         written=(0,),
@@ -442,7 +476,7 @@
     (pair_grad,) = call(
         input_kernel,
         [tile],
-        [padded, slots(2)],
+        [padded],
         exchange(send), projected, inside, vectors, d_outpre, pair, in_weights,
     )
     return update.transpose(1, 0, 2), pair_grad.transpose(1, 0, 2)

time: 112 us -> 110 us (0.982)
  blocking collectives: 101 us -> 98.7 us
    all_to_all x4, blocking collectives: 67.1 us -> 65 us  [exchange(): return lax.all_to_all(messages, OWNERS, 0, 0, tiled=True)]
where the time goes in v5:
time: 110 us
  blocking collectives  98.7 us (90%)
  Pallas kernels  10 us (9%)
    all_to_all x4, blocking collectives, exchange(): return lax.all_to_all(messages, OWNERS, 0, 0, tiled=True)  65 us
    all_gather x1, blocking collectives, body(): lax.all_gather(gathered, 'zhi', axis=0)  33.7 us
    pallas_call x6, Pallas kernels, call(): pl.pallas_call(kernel, out_shape=[jax.ShapeDtypeStruct(shape, dtype) for...  10 us

profile of v5, /device:TPU:1, one launch (start us, length us, event | category | flops | bytes accessed | tf_op | source)
XLA Modules:
  0.0 109.5 jit_solution(16365909364088095615)
XLA Ops:
  0.6 3.3 %project_kernel.1 = (bf16[64,2,896]{2,1,0:T(2,128)(2,1)}, f32[640,384]{1,0:T(8,128)}, f32[8,384]{1,0:T(8,128)}, f32[24,128]{1,0:T(8,128)}, f32[128,384]{1,0:T(8,128)}) custom-call(s32[384]{0:T(512)} %crop_hbm.1, bf16[12,24,128]{2,1,0:T(8,128)(2,1)} %bitcast.12, f32[1,128]{1,0:T(1,128)} %bitcast.15, f32[1,128]{1,0:T(1,128)} %bitcast.16, ...), custom_call_target="tpu_custom_call" | custom-call | tf_op jit(solution)/shard_map/project_kernel/pallas_call | solution.py:399
  4.0 20.5 %all_to_all.20.received = bf16[64,2,896]{2,1,0:T(2,128)(2,1)S(1)} all-to-all(bf16[64,2,896]{2,1,0:T(2,128)(2,1)} %get-tuple-element.16), channel_id=1, replica_groups=mesh['xlo'=2,'y'=4,'core'=2,'zhi'=8,'zlo'=2,'xhi'=2] {'zlo','xhi','xlo',..., dimensions={0} | all-to-all | bytes 458752 | tf_op jit(solution)/shard_map/all_to_all | solution.py:416
  24.5 0.8 collect_kernel.1
  25.3 0.0 copy-start
  25.4 33.7 %all-gather = bf16[3456,128]{1,0:T(8,128)(2,1)S(1)} all-gather(bf16[432,128]{1,0:T(8,128)(2,1)S(1)} %get-tuple-element.17), channel_id=2, replica_groups=mesh['xlo'=2,'y'=4,'core'=2,'zhi'=8,'zlo'=2,'xhi'=2] {'zhi'}, dimensions={0}, use_global_device_ids=true | all-gather | bytes 995328 | tf_op jit(solution)/shard_map/all_gather | solution.py:459
  59.1 1.9 %triangle_kernel.1 = (bf16[8,192,128]{2,1,0:T(8,128)(2,1)S(1)}, bf16[8,192,128]{2,1,0:T(8,128)(2,1)S(1)}, bf16[64,2,896]{2,1,0:T(2,128)(2,1)S(1)}) custom-call(bf16[8,432,128]{2,1,0:T(8,128)(2,1)S(1)} %bitcast.9, bf16[192,128]{1,0:T(8,128)(2,1)S(1)} %get-tuple-element.18.left, bf16[192,128]{1,0:T(8,128)(2,1)S(1)} %get-tuple-element.19.right), custom_call_target="tpu_custom_call" | custom-call | tf_op jit(solution)/shard_map/triangle_kernel/pallas_call | solution.py:399
  61.0 0.0 copy-start.2
  61.0 0.0 copy-start.4
  61.0 0.0 copy-start.5
  61.0 0.0 copy-start.6
  61.1 0.0 copy-start.7
  61.1 18.6 %all_to_all.21.received = bf16[64,2,896]{2,1,0:T(2,128)(2,1)S(1)} all-to-all(bf16[64,2,896]{2,1,0:T(2,128)(2,1)S(1)} %get-tuple-element.20), channel_id=1, replica_groups=mesh['xlo'=2,'y'=4,'core'=2,'zhi'=8,'zlo'=2,'xhi'=2] {'zlo','xhi','xlo',..., dimensions={0} | all-to-all | bytes 458752 | tf_op jit(solution)/shard_map/all_to_all | solution.py:416
  79.6 0.0 copy-done
  79.6 0.0 copy-done.2
  79.6 0.0 copy-done.4
  79.6 0.0 copy-done.5
  79.7 0.0 copy-done.6
  79.7 0.0 copy-done.7
  79.7 1.3 %output_kernel.1 = (bf16[12,24,128]{2,1,0:T(8,128)(2,1)}, bf16[128,384]{1,0:T(8,128)(2,1)S(1)}, bf16[64,2,640]{2,1,0:T(2,128)(2,1)S(1)}) custom-call(bf16[64,2,896]{2,1,0:T(2,128)(2,1)S(1)} %all_to_all.21.received, f32[640,384]{1,0:T(8,128)S(1)} %copy-done, f32[8,384]{1,0:T(8,128)S(1)} %copy-done.6, f32[24,128]{1,0:T(8,128)S(1)} %copy-done.7, ...), custom_call_target="tpu_custom_call" | custom-call | tf_op jit(solution)/shard_map/output_kernel/pallas_call | solution.py:399
  81.0 12.9 %all_to_all.22.received = bf16[64,2,640]{2,1,0:T(2,128)(2,1)S(1)} all-to-all(bf16[64,2,640]{2,1,0:T(2,128)(2,1)S(1)} %get-tuple-element.26), channel_id=1, replica_groups=mesh['xlo'=2,'y'=4,'core'=2,'zhi'=8,'zlo'=2,'xhi'=2] {'zlo','xhi','xlo',..., dimensions={0} | all-to-all | bytes 327680 | tf_op jit(solution)/shard_map/all_to_all | solution.py:416
  93.8 1.3 %back_kernel.1 = bf16[64,2,640]{2,1,0:T(2,128)(2,1)S(1)} custom-call(bf16[64,2,640]{2,1,0:T(2,128)(2,1)S(1)} %all_to_all.22.received, bf16[8,192,128]{2,1,0:T(8,128)(2,1)S(1)} %get-tuple-element.27.left_all, bf16[8,192,128]{2,1,0:T(8,128)(2,1)S(1)} %get-tuple-element.28.right_all), custom_call_target="tpu_custom_call" | custom-call | tf_op jit(solution)/shard_map/back_kernel/pallas_call | solution.py:399
  95.1 0.0 copy-start.1
  95.2 0.0 copy-start.3
  95.2 13.0 %all_to_all.23.received = bf16[64,2,640]{2,1,0:T(2,128)(2,1)S(1)} all-to-all(bf16[64,2,640]{2,1,0:T(2,128)(2,1)S(1)} %back_kernel.1), channel_id=1, replica_groups=mesh['xlo'=2,'y'=4,'core'=2,'zhi'=8,'zlo'=2,'xhi'=2] {'zlo','xhi','xlo',..., dimensions={0} | all-to-all | bytes 327680 | tf_op jit(solution)/shard_map/all_to_all | solution.py:416
  108.2 0.0 copy-done.1
  108.2 0.0 copy-done.3
  108.2 1.3 %input_kernel.1 = bf16[12,24,128]{2,1,0:T(8,128)(2,1)} custom-call(bf16[64,2,640]{2,1,0:T(2,128)(2,1)S(1)} %all_to_all.23.received, f32[640,384]{1,0:T(8,128)S(1)} %copy-done, f32[8,384]{1,0:T(8,128)S(1)} %copy-done.6, f32[24,128]{1,0:T(8,128)S(1)} %copy-done.7, bf16[128,384]{1,0:T(8,128)(2,1)S(1)} %get-tuple-element.29.d_outpre, ...), custom_call_target="tpu_custom_call" | custom-call | tf_op jit(solution)/shard_map/input_kernel/pallas_call | solution.py:399
Async XLA Ops:
  25.3 54.3 %copy-start = (f32[640,384]{1,0:T(8,128)S(1)}, f32[640,384]{1,0:T(8,128)}, u32[]{:S(2)}) copy-start(f32[640,384]{1,0:T(8,128)} %get-tuple-element.21.projected) | copy-start | bytes 2949124
  61.0 18.6 %copy-start.2 = (bf16[24,12,128]{2,0,1:T(8,128)(2,1)S(1)}, bf16[24,12,128]{2,0,1:T(8,128)(2,1)}, u32[]{:S(2)}) copy-start(bf16[24,12,128]{2,0,1:T(8,128)(2,1)} %param.17) | copy-start | bytes 221188
  61.0 18.6 %copy-start.4 = (f32[128,384]{1,0:T(8,128)S(1)}, f32[128,384]{1,0:T(8,128)}, u32[]{:S(2)}) copy-start(f32[128,384]{1,0:T(8,128)} %get-tuple-element.24.grad) | copy-start | bytes 589828
  61.0 18.6 %copy-start.5 = (bf16[128,128]{1,0:T(8,128)(2,1)S(1)}, bf16[128,128]{1,0:T(8,128)(2,1)}, u32[]{:S(2)}) copy-start(bf16[128,128]{1,0:T(8,128)(2,1)} %weights.2) | copy-start | bytes 98308
  61.0 18.6 %copy-start.6 = (f32[8,384]{1,0:T(8,128)S(1)}, f32[8,384]{1,0:T(8,128)}, u32[]{:S(2)}) copy-start(f32[8,384]{1,0:T(8,128)} %get-tuple-element.22.inside) | copy-start | bytes 36868
  61.1 18.6 %copy-start.7 = (f32[24,128]{1,0:T(8,128)S(1)}, f32[24,128]{1,0:T(8,128)}, u32[]{:S(2)}) copy-start(f32[24,128]{1,0:T(8,128)} %get-tuple-element.23.vectors) | copy-start | bytes 36868
  95.1 13.0 %copy-start.1 = (bf16[128,640]{1,0:T(8,128)(2,1)S(1)}, bf16[128,640]{1,0:T(8,128)(2,1)}, u32[]{:S(2)}) copy-start(bf16[128,640]{1,0:T(8,128)(2,1)} %weights.3) | copy-start | bytes 491524
  95.2 13.0 %copy-start.3 = (bf16[24,12,128]{2,0,1:T(8,128)(2,1)S(1)}, bf16[24,12,128]{2,0,1:T(8,128)(2,1)}, u32[]{:S(2)}) copy-start(bf16[24,12,128]{2,0,1:T(8,128)(2,1)} %param.9) | copy-start | bytes 221188

commit v6 on v5

--- a/solution.py
+++ b/solution.py
@@ -60,13 +60,17 @@
     return jnp.stack([scratch[pl.ds(i, TK, stride=PAD), :] for i in range(TI)]).astype(bf16)
 
 
-def parts_of(slots, kinds):
-    parts = []
-    for held in range(HELD):
-        for e in range(E):
-            packed = [slots[n, from_owner(held, e), :] for n in range(slots.shape[0])]
-            parts.append(jnp.concatenate(unpack_slabs(packed, 3 * kinds), axis=0))
-    return parts
+def parts_of(slots):
+    return [
+        jnp.concatenate([slots[n, from_owner(held, e), :] for n in range(slots.shape[0])], axis=0)
+        for held in range(HELD)
+        for e in range(E)
+    ]
+
+
+def unpacked_rows(rows, kinds):
+    slabs = [rows[n : n + R] for n in range(0, rows.shape[0], R)]
+    return unpack_slabs(slabs, 3 * kinds)
 
 
 def pack_rows(values):
@@ -154,8 +158,8 @@
 
 def project_kernel(
     crop_hbm, pair_hbm, gain_hbm, bias_hbm, weights_hbm, out_gain_hbm, out_bias_hbm,
-    cotangent_hbm, out_weights_hbm, send, projected_hbm, inside, vectors, grad,
-    padded, projected, crop, pair, gain, bias, weights, out_gain, out_bias,
+    cotangent_hbm, out_weights_hbm, send, projected, inside, vectors, grad,
+    padded, crop, pair, gain, bias, weights, out_gain, out_bias,
     cotangent, out_weights, arrived,
 ):
     sources = (
@@ -176,8 +180,6 @@
     normed = (hat * gain[...] + bias[...]).astype(bf16)
     loads[4].wait()
     projected[...] = dot(weights[...].T, normed, ((1,), (1,)))
-    keep = pltpu.make_async_copy(projected, projected_hbm, arrived.at[9])
-    keep.start()
 
     loads[0].wait()
     row_pos = lax.axis_index(ROWS)
@@ -207,18 +209,17 @@
     vectors[...] = jnp.concatenate(
         [jnp.broadcast_to(v[...], (8, C)) for v in (gain, out_gain, out_bias)], axis=0
     )
-    keep.wait()
 
 
 def collect_kernel(received, gathered, left, right, slots):
     fill_slots(slots, received)
-    parts = swap_blocks(parts_of(slots, 3))
+    parts = [unpacked_rows(part, 3) for part in swap_blocks(parts_of(slots))]
     for kind in range(3):
         pieces = []
         for t in range(3):
             for k in range(8):
-                at = (3 * kind + t) * R
-                pieces.append(parts[k][at : at + RF] + parts[k][at + RF : at + R])
+                slab = parts[k][3 * kind + t]
+                pieces.append(slab[:RF] + slab[RF:])
         whole = jnp.concatenate(pieces, axis=0)
         gathered[PACK * kind : PACK * (kind + 1)] = pack_rows(whole).astype(bf16)
         if kind < 2:
@@ -262,7 +263,13 @@
     parts = swap_blocks(
         [
             jnp.concatenate(
-                [ordered[kind, (8 * t + i) * R : (8 * t + i + 1) * R] for kind in range(3) for t in range(3)],
+                pack_slabs(
+                    [
+                        ordered[kind, (8 * t + i) * R : (8 * t + i + 1) * R]
+                        for kind in range(3)
+                        for t in range(3)
+                    ]
+                ),
                 axis=0,
             )
             for i in range(8)
@@ -271,8 +278,8 @@
     for held in range(HELD):
         for e in range(E):
             part = parts[held * E + e]
-            for n, slab in enumerate(pack_slabs([part[n * R : (n + 1) * R] for n in range(9)])):
-                slots[n, from_owner(held, e), :] = slab
+            for n in range(slots.shape[0]):
+                slots[n, from_owner(held, e), :] = part[n * R : (n + 1) * R]
     send[...] = as_messages(all_slots(slots))
 
 
@@ -326,12 +333,11 @@
 
 def back_kernel(received, left_all, right_all, send, slots, ordered):
     fill_slots(slots, received)
-    parts = swap_blocks(parts_of(slots, 2))
+    parts = [unpacked_rows(part, 2) for part in swap_blocks(parts_of(slots))]
     for kind in range(2):
         for t in range(3):
             for i in range(8):
-                n = 3 * kind + t
-                ordered[kind, pl.ds((8 * t + i) * R, R), :] = parts[i][n * R : (n + 1) * R]
+                ordered[kind, pl.ds((8 * t + i) * R, R), :] = parts[i][3 * kind + t]
     d_left = jnp.zeros((FOLD, 128), f32)
     d_right = jnp.zeros((FOLD, 128), f32)
     for q in range(Q):
@@ -347,11 +353,13 @@
     parts = swap_blocks(
         [
             jnp.concatenate(
-                [
-                    sides[side][(8 * t + k) * RF : (8 * t + k + 1) * RF]
-                    for side in range(2)
-                    for t in range(3)
-                ],
+                pack_slabs(
+                    [
+                        sides[side][(8 * t + k) * RF : (8 * t + k + 1) * RF]
+                        for side in range(2)
+                        for t in range(3)
+                    ]
+                ),
                 axis=0,
             )
             for k in range(8)
@@ -360,10 +368,10 @@
     for held in range(HELD):
         for e in range(E):
             part = parts[held * E + e]
-            for n, slab in enumerate(pack_slabs([part[n * RF : (n + 1) * RF] for n in range(6)])):
+            for n in range(slots.shape[0]):
                 for half in range(2):
                     start = HELD * (R * e + RF * half) + held
-                    slots[n, pl.ds(start, RF, stride=HELD), :] = slab
+                    slots[n, pl.ds(start, RF, stride=HELD), :] = part[n * RF : (n + 1) * RF]
     send[...] = as_messages(all_slots(slots))
 
 
@@ -394,7 +402,7 @@
     pair_grad[...] = unpadded_rows(inv_in * (grad - first_mean - hat * second_mean), padded)
 
 
-def call(kernel, outs, scratch, *operands, inputs=None, written=(), vmem=40):
+def call(kernel, outs, scratch, *operands, inputs=None, written=()):
     inputs = inputs or [pltpu.VMEM] * len(operands)
     return pl.pallas_call(
         kernel,
@@ -407,7 +415,7 @@
         scratch_shapes=[
             pltpu.VMEM(shape, f32) if isinstance(shape, tuple) else shape for shape in scratch
         ],
-        compiler_params=pltpu.CompilerParams(vmem_limit_bytes=vmem * 1024 * 1024),
+        compiler_params=pltpu.CompilerParams(vmem_limit_bytes=40 * 1024 * 1024),
         name=kernel.__name__,
     )(*operands)
 
@@ -436,15 +444,18 @@
         project_kernel,
         [messages(3), ((5 * C, LANES), f32), ((8, LANES), f32), ((24, C), f32), ((C, LANES), f32)],
         [
-            padded, (5 * C, LANES), pltpu.SMEM((N,), jnp.int32),
+            padded, pltpu.SMEM((N,), jnp.int32),
             pltpu.VMEM((TI, TK, C), bf16), (1, C), (1, C), pltpu.VMEM((C, 5 * C), bf16),
             (1, C), (1, C), pltpu.VMEM((TI, TK, C), bf16), pltpu.VMEM((C, C), bf16),
-            pltpu.SemaphoreType.DMA((10,)),
+            pltpu.SemaphoreType.DMA((9,)),
         ],
-        crop, pair, in_gain, in_bias, in_weights, out_gain, out_bias, cotangent, out_weights,
+        *(
+            pltpu.with_memory_space_constraint(v, pltpu.HBM)
+            for v in (
+                crop, pair, in_gain, in_bias, in_weights, out_gain, out_bias, cotangent, out_weights
+            )
+        ),
         inputs=[pl.ANY] * 9,
-        written=(1,),
-        vmem=58,
     )
     gathered, left, right = call(
         collect_kernel,

time: 110 us -> 108 us (0.982)
  Pallas kernels: 10 us -> 8.63 us
    all_to_all x4, blocking collectives: 65 us -> 63 us  [exchange(): return lax.all_to_all(messages, OWNERS, 0, 0, tiled=True)]
    all_gather x1, blocking collectives: 33.7 us -> 35.3 us  [body(): lax.all_gather(gathered, 'zhi', axis=0)]
    pallas_call x6, Pallas kernels: 10 us -> 8.63 us  [call(): pl.pallas_call(kernel, out_shape=[jax.ShapeDtypeStruct(shape, dtype) for...]
where the time goes in v6:
time: 108 us
  blocking collectives  98.3 us (91%)
  Pallas kernels  8.63 us (8%)
    all_to_all x4, blocking collectives, exchange(): return lax.all_to_all(messages, OWNERS, 0, 0, tiled=True)  63 us
    all_gather x1, blocking collectives, body(): lax.all_gather(gathered, 'zhi', axis=0)  35.3 us
    pallas_call x6, Pallas kernels, call(): pl.pallas_call(kernel, out_shape=[jax.ShapeDtypeStruct(shape, dtype) for...  8.63 us

profile of v6, /device:TPU:1, one launch (start us, length us, event | category | flops | bytes accessed | tf_op | source)
XLA Modules:
  0.0 107.7 jit_solution(5610155434791821659)
XLA Ops:
  0.6 2.3 %project_kernel.1 = (bf16[64,2,896]{2,1,0:T(2,128)(2,1)S(1)}, f32[640,384]{1,0:T(8,128)S(1)}, f32[8,384]{1,0:T(8,128)S(1)}, f32[24,128]{1,0:T(8,128)S(1)}, f32[128,384]{1,0:T(8,128)S(1)}) custom-call(s32[384]{0:T(512)} %crop_hbm.1, bf16[12,24,128]{2,1,0:T(8,128)(2,1)} %bitcast.12, f32[1,128]{1,0:T(1,128)} %bitcast.15, f32[1,128]{1,0:T(1,128)} %bitcast.16, ...), custom_call_target="tpu_custom_call" | custom-call | tf_op jit(solution)/shard_map/project_kernel/pallas_call | solution.py:407
  2.9 19.6 %all_to_all.20.received = bf16[64,2,896]{2,1,0:T(2,128)(2,1)S(1)} all-to-all(bf16[64,2,896]{2,1,0:T(2,128)(2,1)S(1)} %get-tuple-element.16), channel_id=1, replica_groups=mesh['xlo'=2,'y'=4,'core'=2,'zhi'=8,'zlo'=2,'xhi'=2] {'zlo','xhi','xlo',..., dimensions={0} | all-to-all | bytes 458752 | tf_op jit(solution)/shard_map/all_to_all | solution.py:424
  22.6 0.6 collect_kernel.1
  23.2 35.3 %all-gather = bf16[3456,128]{1,0:T(8,128)(2,1)S(1)} all-gather(bf16[432,128]{1,0:T(8,128)(2,1)S(1)} %get-tuple-element.17), channel_id=2, replica_groups=mesh['xlo'=2,'y'=4,'core'=2,'zhi'=8,'zlo'=2,'xhi'=2] {'zhi'}, dimensions={0}, use_global_device_ids=true | all-gather | bytes 995328 | tf_op jit(solution)/shard_map/all_gather | solution.py:470
  58.6 1.8 %triangle_kernel.1 = (bf16[8,192,128]{2,1,0:T(8,128)(2,1)S(1)}, bf16[8,192,128]{2,1,0:T(8,128)(2,1)S(1)}, bf16[64,2,896]{2,1,0:T(2,128)(2,1)S(1)}) custom-call(bf16[8,432,128]{2,1,0:T(8,128)(2,1)S(1)} %bitcast.9, bf16[192,128]{1,0:T(8,128)(2,1)S(1)} %get-tuple-element.18.left, bf16[192,128]{1,0:T(8,128)(2,1)S(1)} %get-tuple-element.19.right), custom_call_target="tpu_custom_call" | custom-call | tf_op jit(solution)/shard_map/triangle_kernel/pallas_call | solution.py:407
  60.4 0.0 copy-start.1
  60.4 0.0 copy-start.3
  60.4 17.5 %all_to_all.21.received = bf16[64,2,896]{2,1,0:T(2,128)(2,1)S(1)} all-to-all(bf16[64,2,896]{2,1,0:T(2,128)(2,1)S(1)} %get-tuple-element.20), channel_id=1, replica_groups=mesh['xlo'=2,'y'=4,'core'=2,'zhi'=8,'zlo'=2,'xhi'=2] {'zlo','xhi','xlo',..., dimensions={0} | all-to-all | bytes 458752 | tf_op jit(solution)/shard_map/all_to_all | solution.py:424
  78.0 0.0 copy-done.1
  78.0 0.0 copy-done.3
  78.0 1.3 %output_kernel.1 = (bf16[12,24,128]{2,1,0:T(8,128)(2,1)}, bf16[128,384]{1,0:T(8,128)(2,1)S(1)}, bf16[64,2,640]{2,1,0:T(2,128)(2,1)S(1)}) custom-call(bf16[64,2,896]{2,1,0:T(2,128)(2,1)S(1)} %all_to_all.21.received, f32[640,384]{1,0:T(8,128)S(1)} %get-tuple-element.21.projected, f32[8,384]{1,0:T(8,128)S(1)} %get-tuple-element.22.inside, ...), custom_call_target="tpu_custom_call" | custom-call | tf_op jit(solution)/shard_map/output_kernel/pallas_call | solution.py:407
  79.3 12.9 %all_to_all.22.received = bf16[64,2,640]{2,1,0:T(2,128)(2,1)S(1)} all-to-all(bf16[64,2,640]{2,1,0:T(2,128)(2,1)S(1)} %get-tuple-element.26), channel_id=1, replica_groups=mesh['xlo'=2,'y'=4,'core'=2,'zhi'=8,'zlo'=2,'xhi'=2] {'zlo','xhi','xlo',..., dimensions={0} | all-to-all | bytes 327680 | tf_op jit(solution)/shard_map/all_to_all | solution.py:424
  92.1 1.2 %back_kernel.1 = bf16[64,2,640]{2,1,0:T(2,128)(2,1)S(1)} custom-call(bf16[64,2,640]{2,1,0:T(2,128)(2,1)S(1)} %all_to_all.22.received, bf16[8,192,128]{2,1,0:T(8,128)(2,1)S(1)} %get-tuple-element.27.left_all, bf16[8,192,128]{2,1,0:T(8,128)(2,1)S(1)} %get-tuple-element.28.right_all), custom_call_target="tpu_custom_call" | custom-call | tf_op jit(solution)/shard_map/back_kernel/pallas_call | solution.py:407
  93.3 0.0 copy-start
  93.3 0.0 copy-start.2
  93.4 13.0 %all_to_all.23.received = bf16[64,2,640]{2,1,0:T(2,128)(2,1)S(1)} all-to-all(bf16[64,2,640]{2,1,0:T(2,128)(2,1)S(1)} %back_kernel.1), channel_id=1, replica_groups=mesh['xlo'=2,'y'=4,'core'=2,'zhi'=8,'zlo'=2,'xhi'=2] {'zlo','xhi','xlo',..., dimensions={0} | all-to-all | bytes 327680 | tf_op jit(solution)/shard_map/all_to_all | solution.py:424
  106.4 0.0 copy-done
  106.4 0.0 copy-done.2
  106.4 1.3 %input_kernel.1 = bf16[12,24,128]{2,1,0:T(8,128)(2,1)} custom-call(bf16[64,2,640]{2,1,0:T(2,128)(2,1)S(1)} %all_to_all.23.received, f32[640,384]{1,0:T(8,128)S(1)} %get-tuple-element.21.projected, f32[8,384]{1,0:T(8,128)S(1)} %get-tuple-element.22.inside, f32[24,128]{1,0:T(8,128)S(1)} %get-tuple-element.23.vectors, ...), custom_call_target="tpu_custom_call" | custom-call | tf_op jit(solution)/shard_map/input_kernel/pallas_call | solution.py:407
Async XLA Ops:
  60.4 17.5 %copy-start.1 = (bf16[24,12,128]{2,0,1:T(8,128)(2,1)S(1)}, bf16[24,12,128]{2,0,1:T(8,128)(2,1)}, u32[]{:S(2)}) copy-start(bf16[24,12,128]{2,0,1:T(8,128)(2,1)} %param.17) | copy-start | bytes 221188
  60.4 17.5 %copy-start.3 = (bf16[128,128]{1,0:T(8,128)(2,1)S(1)}, bf16[128,128]{1,0:T(8,128)(2,1)}, u32[]{:S(2)}) copy-start(bf16[128,128]{1,0:T(8,128)(2,1)} %weights.2) | copy-start | bytes 98308
  93.3 13.0 %copy-start = (bf16[128,640]{1,0:T(8,128)(2,1)S(1)}, bf16[128,640]{1,0:T(8,128)(2,1)}, u32[]{:S(2)}) copy-start(bf16[128,640]{1,0:T(8,128)(2,1)} %weights.3) | copy-start | bytes 491524
  93.3 13.0 %copy-start.2 = (bf16[24,12,128]{2,0,1:T(8,128)(2,1)S(1)}, bf16[24,12,128]{2,0,1:T(8,128)(2,1)}, u32[]{:S(2)}) copy-start(bf16[24,12,128]{2,0,1:T(8,128)(2,1)} %param.9) | copy-start | bytes 221188

commit v7 on v6

--- a/solution.py
+++ b/solution.py
@@ -158,7 +158,7 @@
 
 def project_kernel(
     crop_hbm, pair_hbm, gain_hbm, bias_hbm, weights_hbm, out_gain_hbm, out_bias_hbm,
-    cotangent_hbm, out_weights_hbm, send, projected, inside, vectors, grad,
+    cotangent_hbm, out_weights_hbm, send, projected, inside, vectors, grad, hat, inv_in, upstream,
     padded, crop, pair, gain, bias, weights, out_gain, out_bias,
     cotangent, out_weights, arrived,
 ):
@@ -174,12 +174,17 @@
     for load in loads:
         load.start()
     loads[1].wait()
-    hat, _ = norm_rows(padded_rows(pair[...], padded))
+    pair_hat, scale = norm_rows(padded_rows(pair[...], padded))
+    hat[...] = pair_hat
+    inv_in[...] = jnp.broadcast_to(scale, (LANES, C))
     loads[2].wait()
     loads[3].wait()
-    normed = (hat * gain[...] + bias[...]).astype(bf16)
+    normed = (pair_hat * gain[...] + bias[...]).astype(bf16)
     loads[4].wait()
-    projected[...] = dot(weights[...].T, normed, ((1,), (1,)))
+    proj = dot(weights[...].T, normed, ((1,), (1,)))
+    opened = jax.nn.sigmoid(proj[2 * C :])
+    projected[: 2 * C] = proj[: 2 * C]
+    projected[2 * C :] = opened
 
     loads[0].wait()
     row_pos = lax.axis_index(ROWS)
@@ -194,12 +199,13 @@
     same = (crop_rows == crop_cols).astype(f32)
     inside[...] = same
     mask = same[:1, :]
-    left = mask * jax.nn.sigmoid(projected[2 * C : 3 * C]) * projected[:C]
-    right = mask * jax.nn.sigmoid(projected[3 * C : 4 * C]) * projected[C : 2 * C]
+    left = mask * opened[:C] * proj[:C]
+    right = mask * opened[C : 2 * C] * proj[C : 2 * C]
     for load in loads[5:]:
         load.wait()
-    upstream = padded_rows(cotangent[...], padded).T
-    d_value = (upstream * jax.nn.sigmoid(projected[4 * C :])).astype(bf16)
+    turned = padded_rows(cotangent[...], padded).T
+    upstream[...] = turned
+    d_value = (turned * opened[2 * C :]).astype(bf16)
     value_grad = dot(out_weights[...], d_value, ((1,), (0,))) * as_column(out_gain[...])
     grad[...] = value_grad
     masked_grad = jnp.where(mask > 0, value_grad, 0.0)
@@ -242,18 +248,20 @@
     place = 2 * (lax.axis_index("zhi") % (Q // 2))
     spare = jnp.zeros((PAD - TI, 128), f32)
     for q in range(Q):
-        left_q = unpack_rows(gathered[q, :PACK].astype(f32)).astype(bf16)
-        right_q = unpack_rows(gathered[q, PACK : 2 * PACK].astype(f32)).astype(bf16)
-        left_all[q] = left_q
-        right_all[q] = right_q
+        lanes = slice(128 * q, 128 * (q + 1))
+        left_all[:, lanes] = unpack_rows(gathered[q, :PACK].astype(f32)).astype(bf16)
+        right_all[:, lanes] = unpack_rows(gathered[q, PACK : 2 * PACK].astype(f32)).astype(bf16)
+    tri = dot(left_all[...], right[...], ((0,), (0,)))
+    mirror = dot(right_all[...], left[...], ((0,), (0,)))
+    for q in range(Q):
         folded[...] = unpack_rows(gathered[q, 2 * PACK :].astype(f32))
         own_i = [folded[pl.ds(place + half, TK, stride=RF), :] for half in range(2)]
         pieces = []
         for e in range(E):
             pieces += [own_i[e // 2][e % 2 * TI : (e % 2 + 1) * TI], spare]
         blocks = (
-            dot(left_q, right[...], ((0,), (0,))),
-            dot(right_q, left[...], ((0,), (0,))),
+            tri[128 * q : 128 * (q + 1)],
+            mirror[128 * q : 128 * (q + 1)],
             jnp.concatenate(pieces * HELD, axis=0).T,
         )
         for kind, block in enumerate(blocks):
@@ -297,7 +305,7 @@
 
 
 def output_kernel(
-    received, projected, inside, vectors, grad, cotangent, weights, update_hbm, d_outpre, send,
+    received, projected, inside, vectors, grad, upstream, weights, update_hbm, d_outpre, send,
     padded, update, written,
 ):
     mask = inside[:1, :] > 0
@@ -305,7 +313,7 @@
     tri_hat, inv_out = norm_tri(slabs, 0, mask)
     normed_out = (tri_hat * as_column(vectors[8:9]) + as_column(vectors[16:17])).astype(bf16)
     gated_value = dot(weights[...].T, normed_out, ((1,), (0,)))
-    gate = jax.nn.sigmoid(projected[4 * C :])
+    gate = projected[4 * C :]
     update[...] = unpadded_rows((gate * gated_value).T, padded)
     write = pltpu.make_async_copy(update, update_hbm, written)
     write.start()
@@ -314,8 +322,7 @@
     mirror_grad = jnp.where(mask, get_kind(slabs, 2), 0.0)
     d_mirror = norm_back(mirror_grad, mirror_hat, mirror_inv, mask)
     send[...] = as_messages(pack_slabs(slabs_of(d_tri) + slabs_of(d_mirror)))
-    upstream = padded_rows(cotangent[...], padded).T
-    d_outpre[...] = (upstream * gated_value * gate * (1.0 - gate)).astype(bf16)
+    d_outpre[...] = (upstream[...] * gated_value * gate * (1.0 - gate)).astype(bf16)
     write.wait()
 
 
@@ -338,17 +345,20 @@
         for t in range(3):
             for i in range(8):
                 ordered[kind, pl.ds((8 * t + i) * R, R), :] = parts[i][3 * kind + t]
-    d_left = jnp.zeros((FOLD, 128), f32)
-    d_right = jnp.zeros((FOLD, 128), f32)
-    for q in range(Q):
-        by_i, by_j = (
-            padded_columns(
-                jnp.concatenate([ordered[kind, residue_rows(E * q + e), :] for e in range(E)], axis=0)
-            )
-            for kind in range(2)
+    by_i, by_j = (
+        jnp.concatenate(
+            [
+                padded_columns(
+                    jnp.concatenate([ordered[kind, residue_rows(E * q + e), :] for e in range(E)], axis=0)
+                )
+                for q in range(Q)
+            ],
+            axis=0,
         )
-        d_right = d_right + dot(left_all[q], by_i, ((1,), (0,)))
-        d_left = d_left + dot(right_all[q], by_j, ((1,), (0,)))
+        for kind in range(2)
+    )
+    d_right = dot(left_all[...], by_i, ((1,), (0,)))
+    d_left = dot(right_all[...], by_j, ((1,), (0,)))
     sides = (d_left, d_right)
     parts = swap_blocks(
         [
@@ -376,15 +386,14 @@
 
 
 def input_kernel(
-    received, projected, inside, vectors, d_outpre, pair, weights, pair_grad, padded
+    received, projected, inside, vectors, d_outpre, hat, inv_in, weights, pair_grad, padded
 ):
     slabs = unpack_slabs(from_messages(received), 6)
     mask = inside[:1, :]
     d_left = get_kind(slabs, 0) * mask
     d_right = get_kind(slabs, 1) * mask
     left_val, right_val = projected[:C], projected[C : 2 * C]
-    left_sig = jax.nn.sigmoid(projected[2 * C : 3 * C])
-    right_sig = jax.nn.sigmoid(projected[3 * C : 4 * C])
+    left_sig, right_sig = projected[2 * C : 3 * C], projected[3 * C : 4 * C]
     d_proj = jnp.concatenate(
         [
             (d_left * left_sig).astype(bf16),
@@ -396,10 +405,11 @@
         axis=0,
     )
     grad = dot(weights[...], d_proj, ((1,), (0,))).T * vectors[:1]
-    hat, inv_in = norm_rows(padded_rows(pair[...], padded))
     first_mean = jnp.mean(grad, axis=1, keepdims=True)
-    second_mean = jnp.mean(grad * hat, axis=1, keepdims=True)
-    pair_grad[...] = unpadded_rows(inv_in * (grad - first_mean - hat * second_mean), padded)
+    second_mean = jnp.mean(grad * hat[...], axis=1, keepdims=True)
+    pair_grad[...] = unpadded_rows(
+        inv_in[...] * (grad - first_mean - hat[...] * second_mean), padded
+    )
 
 
 def call(kernel, outs, scratch, *operands, inputs=None, written=()):
@@ -438,11 +448,14 @@
     def slots(kinds):
         return (packed_count(kinds), C, 128)
 
-    every_block = ((Q, FOLD, 128), bf16)
+    every_block = ((FOLD, Q * 128), bf16)
     own = ((FOLD, 128), bf16)
-    send, projected, inside, vectors, grad = call(
+    send, projected, inside, vectors, grad, hat, inv_in, upstream = call(
         project_kernel,
-        [messages(3), ((5 * C, LANES), f32), ((8, LANES), f32), ((24, C), f32), ((C, LANES), f32)],
+        [
+            messages(3), ((5 * C, LANES), f32), ((8, LANES), f32), ((24, C), f32), ((C, LANES), f32),
+            (padded, f32), (padded, f32), ((C, LANES), f32),
+        ],
         [
             padded, pltpu.SMEM((N,), jnp.int32),
             pltpu.VMEM((TI, TK, C), bf16), (1, C), (1, C), pltpu.VMEM((C, 5 * C), bf16),
@@ -475,7 +488,7 @@
         [
             padded, pltpu.VMEM((TI, TK, C), bf16), pltpu.SemaphoreType.DMA(()),
         ],
-        exchange(send), projected, inside, vectors, grad, cotangent, out_weights,
+        exchange(send), projected, inside, vectors, grad, upstream, out_weights,
         written=(0,),
     )
     (send,) = call(
@@ -488,7 +501,7 @@
         input_kernel,
         [tile],
         [padded],
-        exchange(send), projected, inside, vectors, d_outpre, pair, in_weights,
+        exchange(send), projected, inside, vectors, d_outpre, hat, inv_in, in_weights,
     )
     return update.transpose(1, 0, 2), pair_grad.transpose(1, 0, 2)
 

time: 108 us -> 108 us (level)
  no operation moved by 1% of the time
where the time goes in v7:
time: 108 us; the launch traced here: 107 us
  blocking collectives  98.2 us (91%)
  Pallas kernels  8.48 us (8%)
    all_to_all x4, blocking collectives, exchange(): return lax.all_to_all(messages, OWNERS, 0, 0, tiled=True)  63.6 us
    all_gather x1, blocking collectives, body(): lax.all_gather(gathered, 'zhi', axis=0)  34.6 us
    pallas_call x6, Pallas kernels, call(): pl.pallas_call(kernel, out_shape=[jax.ShapeDtypeStruct(shape, dtype) for...  8.48 us

profile of v7, /device:TPU:1, one launch (start us, length us, event | category | flops | bytes accessed | tf_op | source)
XLA Modules:
  0.0 107.4 jit_solution(2308987343898699376)
XLA Ops:
  0.6 2.3 %project_kernel.1 = (bf16[64,2,896]{2,1,0:T(2,128)(2,1)S(1)}, f32[640,384]{1,0:T(8,128)S(1)}, f32[8,384]{1,0:T(8,128)S(1)}, f32[24,128]{1,0:T(8,128)S(1)}, f32[1...) custom-call(s32[384]{0:T(512)} %crop_hbm.1, ...), custom_call_target="tpu_custom_call" | custom-call | tf_op jit(solution)/shard_map/project_kernel/pallas_call | solution.py:417
  2.9 19.6 %all_to_all.20.received = bf16[64,2,896]{2,1,0:T(2,128)(2,1)S(1)} all-to-all(bf16[64,2,896]{2,1,0:T(2,128)(2,1)S(1)} %get-tuple-element.19), channel_id=1, replica_groups=mesh['xlo'=2,'y'=4,'core'=2,'zhi'=8,'zlo'=2,'xhi'=2] {'zlo','xhi','xlo',..., dimensions={0} | all-to-all | bytes 458752 | tf_op jit(solution)/shard_map/all_to_all | solution.py:434
  22.6 0.6 collect_kernel.1
  23.2 34.6 %all-gather = bf16[3456,128]{1,0:T(8,128)(2,1)S(1)} all-gather(bf16[432,128]{1,0:T(8,128)(2,1)S(1)} %get-tuple-element.20), channel_id=2, replica_groups=mesh['xlo'=2,'y'=4,'core'=2,'zhi'=8,'zlo'=2,'xhi'=2] {'zhi'}, dimensions={0}, use_global_device_ids=true | all-gather | bytes 995328 | tf_op jit(solution)/shard_map/all_gather | solution.py:483
  57.9 1.8 %triangle_kernel.1 = (bf16[192,1024]{1,0:T(8,128)(2,1)S(1)}, bf16[192,1024]{1,0:T(8,128)(2,1)S(1)}, bf16[64,2,896]{2,1,0:T(2,128)(2,1)S(1)}) custom-call(bf16[8,432,128]{2,1,0:T(8,128)(2,1)S(1)} %bitcast.9, bf16[192,128]{1,0:T(8,128)(2,1)S(1)} %get-tuple-element.21.left, bf16[192,128]{1,0:T(8,128)(2,1)S(1)} %get-tuple-element.22.right), custom_call_target="tpu_custom_call" | custom-call | tf_op jit(solution)/shard_map/triangle_kernel/pallas_call | solution.py:417
  59.7 0.0 copy-start.1
  59.7 18.1 %all_to_all.21.received = bf16[64,2,896]{2,1,0:T(2,128)(2,1)S(1)} all-to-all(bf16[64,2,896]{2,1,0:T(2,128)(2,1)S(1)} %get-tuple-element.23), channel_id=1, replica_groups=mesh['xlo'=2,'y'=4,'core'=2,'zhi'=8,'zlo'=2,'xhi'=2] {'zlo','xhi','xlo',..., dimensions={0} | all-to-all | bytes 458752 | tf_op jit(solution)/shard_map/all_to_all | solution.py:434
  77.8 0.0 copy-done.1
  77.8 1.2 %output_kernel.1 = (bf16[12,24,128]{2,1,0:T(8,128)(2,1)}, bf16[128,384]{1,0:T(8,128)(2,1)S(1)}, bf16[64,2,640]{2,1,0:T(2,128)(2,1)S(1)}) custom-call(bf16[64,2,896]{2,1,0:T(2,128)(2,1)S(1)} %all_to_all.21.received, f32[640,384]{1,0:T(8,128)S(1)} %get-tuple-element.24.projected, f32[8,384]{1,0:T(8,128)S(1)} %get-tuple-element.25.inside, ...), custom_call_target="tpu_custom_call" | custom-call | tf_op jit(solution)/shard_map/output_kernel/pallas_call | solution.py:417
  79.0 12.9 %all_to_all.22.received = bf16[64,2,640]{2,1,0:T(2,128)(2,1)S(1)} all-to-all(bf16[64,2,640]{2,1,0:T(2,128)(2,1)S(1)} %get-tuple-element.30), channel_id=1, replica_groups=mesh['xlo'=2,'y'=4,'core'=2,'zhi'=8,'zlo'=2,'xhi'=2] {'zlo','xhi','xlo',..., dimensions={0} | all-to-all | bytes 327680 | tf_op jit(solution)/shard_map/all_to_all | solution.py:434
  91.9 1.2 %back_kernel.1 = bf16[64,2,640]{2,1,0:T(2,128)(2,1)S(1)} custom-call(bf16[64,2,640]{2,1,0:T(2,128)(2,1)S(1)} %all_to_all.22.received, bf16[192,1024]{1,0:T(8,128)(2,1)S(1)} %get-tuple-element.31.left_all, bf16[192,1024]{1,0:T(8,128)(2,1)S(1)} %get-tuple-element.32.right_all), custom_call_target="tpu_custom_call" | custom-call | tf_op jit(solution)/shard_map/back_kernel/pallas_call | solution.py:417
  93.1 0.0 copy-start
  93.1 13.0 %all_to_all.23.received = bf16[64,2,640]{2,1,0:T(2,128)(2,1)S(1)} all-to-all(bf16[64,2,640]{2,1,0:T(2,128)(2,1)S(1)} %back_kernel.1), channel_id=1, replica_groups=mesh['xlo'=2,'y'=4,'core'=2,'zhi'=8,'zlo'=2,'xhi'=2] {'zlo','xhi','xlo',..., dimensions={0} | all-to-all | bytes 327680 | tf_op jit(solution)/shard_map/all_to_all | solution.py:434
  106.1 0.0 copy-done
  106.1 1.3 %input_kernel.1 = bf16[12,24,128]{2,1,0:T(8,128)(2,1)} custom-call(bf16[64,2,640]{2,1,0:T(2,128)(2,1)S(1)} %all_to_all.23.received, f32[640,384]{1,0:T(8,128)S(1)} %get-tuple-element.24.projected, f32[8,384]{1,0:T(8,128)S(1)} %get-tuple-element.25.inside, f32[24,128]{1,0:T(8,128)S(1)} %get-tuple-element.26.vectors, ...), custom_call_target="tpu_custom_call" | custom-call | tf_op jit(solution)/shard_map/input_kernel/pallas_call | solution.py:417
Async XLA Ops:
  59.7 18.1 %copy-start.1 = (bf16[128,128]{1,0:T(8,128)(2,1)S(1)}, bf16[128,128]{1,0:T(8,128)(2,1)}, u32[]{:S(2)}) copy-start(bf16[128,128]{1,0:T(8,128)(2,1)} %weights.2) | copy-start | bytes 98308
  93.1 13.0 %copy-start = (bf16[128,640]{1,0:T(8,128)(2,1)S(1)}, bf16[128,640]{1,0:T(8,128)(2,1)}, u32[]{:S(2)}) copy-start(bf16[128,640]{1,0:T(8,128)(2,1)} %weights.3) | copy-start | bytes 491524

commit v8 on v7

--- a/solution.py
+++ b/solution.py
@@ -19,6 +19,7 @@
 C = 128
 N = 384
 FOLD = N // 2
+SPAN = N + 4 * 16
 PACK = FOLD * TI // PAD
 GROUP = FOLD - PACK
 RF = R // 2
@@ -479,7 +480,7 @@
     left_all, right_all, send = call(
         triangle_kernel,
         [every_block, every_block, messages(3)],
-        [slots(3), (3, N, 128), (FOLD, 128)],
+        [slots(3), (3, SPAN, 128), (FOLD, 128)],
         lax.all_gather(gathered, "zhi", axis=0), left, right,
     )
     update, d_outpre, send = call(
@@ -494,7 +495,7 @@
     (send,) = call(
         back_kernel,
         [messages(2)],
-        [slots(2), (2, N, 128)],
+        [slots(2), (2, SPAN, 128)],
         exchange(send), left_all, right_all,
     )
     (pair_grad,) = call(

time: 108 us -> 108 us (level)
  no operation moved by 1% of the time
where the time goes in v8:
time: 108 us; the launch traced here: 107 us
  blocking collectives  98.2 us (91%)
  Pallas kernels  8.48 us (8%)
    all_to_all x4, blocking collectives, exchange(): return lax.all_to_all(messages, OWNERS, 0, 0, tiled=True)  63.6 us
    all_gather x1, blocking collectives, body(): lax.all_gather(gathered, 'zhi', axis=0)  34.6 us
    pallas_call x6, Pallas kernels, call(): pl.pallas_call(kernel, out_shape=[jax.ShapeDtypeStruct(shape, dtype) for...  8.48 us

profile of v8, /device:TPU:1, one launch (start us, length us, event | category | flops | bytes accessed | tf_op | source)
XLA Modules:
  0.0 107.4 jit_solution(17944416414128945645)
XLA Ops:
  0.6 2.3 %project_kernel.1 = (bf16[64,2,896]{2,1,0:T(2,128)(2,1)S(1)}, f32[640,384]{1,0:T(8,128)S(1)}, f32[8,384]{1,0:T(8,128)S(1)}, f32[24,128]{1,0:T(8,128)S(1)}, f32[1...) custom-call(s32[384]{0:T(512)} %crop_hbm.1, ...), custom_call_target="tpu_custom_call" | custom-call | tf_op jit(solution)/shard_map/project_kernel/pallas_call | solution.py:418
  2.9 19.6 %all_to_all.20.received = bf16[64,2,896]{2,1,0:T(2,128)(2,1)S(1)} all-to-all(bf16[64,2,896]{2,1,0:T(2,128)(2,1)S(1)} %get-tuple-element.19), channel_id=1, replica_groups=mesh['xlo'=2,'y'=4,'core'=2,'zhi'=8,'zlo'=2,'xhi'=2] {'zlo','xhi','xlo',..., dimensions={0} | all-to-all | bytes 458752 | tf_op jit(solution)/shard_map/all_to_all | solution.py:435
  22.6 0.6 collect_kernel.1
  23.2 34.6 %all-gather = bf16[3456,128]{1,0:T(8,128)(2,1)S(1)} all-gather(bf16[432,128]{1,0:T(8,128)(2,1)S(1)} %get-tuple-element.20), channel_id=2, replica_groups=mesh['xlo'=2,'y'=4,'core'=2,'zhi'=8,'zlo'=2,'xhi'=2] {'zhi'}, dimensions={0}, use_global_device_ids=true | all-gather | bytes 995328 | tf_op jit(solution)/shard_map/all_gather | solution.py:484
  57.9 1.8 %triangle_kernel.1 = (bf16[192,1024]{1,0:T(8,128)(2,1)S(1)}, bf16[192,1024]{1,0:T(8,128)(2,1)S(1)}, bf16[64,2,896]{2,1,0:T(2,128)(2,1)S(1)}) custom-call(bf16[8,432,128]{2,1,0:T(8,128)(2,1)S(1)} %bitcast.9, bf16[192,128]{1,0:T(8,128)(2,1)S(1)} %get-tuple-element.21.left, bf16[192,128]{1,0:T(8,128)(2,1)S(1)} %get-tuple-element.22.right), custom_call_target="tpu_custom_call" | custom-call | tf_op jit(solution)/shard_map/triangle_kernel/pallas_call | solution.py:418
  59.7 0.0 copy-start.1
  59.7 18.1 %all_to_all.21.received = bf16[64,2,896]{2,1,0:T(2,128)(2,1)S(1)} all-to-all(bf16[64,2,896]{2,1,0:T(2,128)(2,1)S(1)} %get-tuple-element.23), channel_id=1, replica_groups=mesh['xlo'=2,'y'=4,'core'=2,'zhi'=8,'zlo'=2,'xhi'=2] {'zlo','xhi','xlo',..., dimensions={0} | all-to-all | bytes 458752 | tf_op jit(solution)/shard_map/all_to_all | solution.py:435
  77.8 0.0 copy-done.1
  77.8 1.2 %output_kernel.1 = (bf16[12,24,128]{2,1,0:T(8,128)(2,1)}, bf16[128,384]{1,0:T(8,128)(2,1)S(1)}, bf16[64,2,640]{2,1,0:T(2,128)(2,1)S(1)}) custom-call(bf16[64,2,896]{2,1,0:T(2,128)(2,1)S(1)} %all_to_all.21.received, f32[640,384]{1,0:T(8,128)S(1)} %get-tuple-element.24.projected, f32[8,384]{1,0:T(8,128)S(1)} %get-tuple-element.25.inside, ...), custom_call_target="tpu_custom_call" | custom-call | tf_op jit(solution)/shard_map/output_kernel/pallas_call | solution.py:418
  79.0 12.9 %all_to_all.22.received = bf16[64,2,640]{2,1,0:T(2,128)(2,1)S(1)} all-to-all(bf16[64,2,640]{2,1,0:T(2,128)(2,1)S(1)} %get-tuple-element.30), channel_id=1, replica_groups=mesh['xlo'=2,'y'=4,'core'=2,'zhi'=8,'zlo'=2,'xhi'=2] {'zlo','xhi','xlo',..., dimensions={0} | all-to-all | bytes 327680 | tf_op jit(solution)/shard_map/all_to_all | solution.py:435
  91.9 1.2 %back_kernel.1 = bf16[64,2,640]{2,1,0:T(2,128)(2,1)S(1)} custom-call(bf16[64,2,640]{2,1,0:T(2,128)(2,1)S(1)} %all_to_all.22.received, bf16[192,1024]{1,0:T(8,128)(2,1)S(1)} %get-tuple-element.31.left_all, bf16[192,1024]{1,0:T(8,128)(2,1)S(1)} %get-tuple-element.32.right_all), custom_call_target="tpu_custom_call" | custom-call | tf_op jit(solution)/shard_map/back_kernel/pallas_call | solution.py:418
  93.1 0.0 copy-start
  93.1 13.0 %all_to_all.23.received = bf16[64,2,640]{2,1,0:T(2,128)(2,1)S(1)} all-to-all(bf16[64,2,640]{2,1,0:T(2,128)(2,1)S(1)} %back_kernel.1), channel_id=1, replica_groups=mesh['xlo'=2,'y'=4,'core'=2,'zhi'=8,'zlo'=2,'xhi'=2] {'zlo','xhi','xlo',..., dimensions={0} | all-to-all | bytes 327680 | tf_op jit(solution)/shard_map/all_to_all | solution.py:435
  106.1 0.0 copy-done
  106.1 1.3 %input_kernel.1 = bf16[12,24,128]{2,1,0:T(8,128)(2,1)} custom-call(bf16[64,2,640]{2,1,0:T(2,128)(2,1)S(1)} %all_to_all.23.received, f32[640,384]{1,0:T(8,128)S(1)} %get-tuple-element.24.projected, f32[8,384]{1,0:T(8,128)S(1)} %get-tuple-element.25.inside, f32[24,128]{1,0:T(8,128)S(1)} %get-tuple-element.26.vectors, ...), custom_call_target="tpu_custom_call" | custom-call | tf_op jit(solution)/shard_map/input_kernel/pallas_call | solution.py:418
Async XLA Ops:
  59.7 18.1 %copy-start.1 = (bf16[128,128]{1,0:T(8,128)(2,1)S(1)}, bf16[128,128]{1,0:T(8,128)(2,1)}, u32[]{:S(2)}) copy-start(bf16[128,128]{1,0:T(8,128)(2,1)} %weights.2) | copy-start | bytes 98308
  93.1 13.0 %copy-start = (bf16[128,640]{1,0:T(8,128)(2,1)S(1)}, bf16[128,640]{1,0:T(8,128)(2,1)}, u32[]{:S(2)}) copy-start(bf16[128,640]{1,0:T(8,128)(2,1)} %weights.3) | copy-start | bytes 491524

commit v9 on v8

--- a/solution.py
+++ b/solution.py
@@ -39,6 +39,11 @@
                 continue
             b = a | step
             low, high = parts[a], parts[b]
+            if step == 4:
+                turned = pltpu.roll(jnp.where(upper, low, high), 64, 1)
+                parts[a] = jnp.where(upper, turned, low)
+                parts[b] = jnp.where(upper, high, turned)
+                continue
             parts[a] = jnp.where(upper, pltpu.roll(high, step * PAD, 1), low)
             parts[b] = jnp.where(upper, high, pltpu.roll(low, 128 - step * PAD, 1))
     return parts
@@ -136,11 +141,11 @@
 
 
 def as_messages(packed):
-    return jnp.concatenate(packed, axis=1).reshape(C // HELD, HELD, -1).astype(bf16)
+    return jnp.concatenate(packed, axis=1).astype(bf16).reshape(C // HELD, HELD, -1)
 
 
 def from_messages(received):
-    rows = received[...].astype(f32).reshape(C, -1)
+    rows = received[...].reshape(C, -1).astype(f32)
     return [rows[:, n : n + 128] for n in range(0, rows.shape[1], 128)]
 
 

time: 108 us -> 107 us (level)
  no operation moved by 1% of the time
where the time goes in v9:
time: 107 us
  blocking collectives  98.2 us (92%)
  Pallas kernels  8.14 us (8%)
    all_to_all x4, blocking collectives, exchange(): return lax.all_to_all(messages, OWNERS, 0, 0, tiled=True)  63.6 us
    all_gather x1, blocking collectives, body(): lax.all_gather(gathered, 'zhi', axis=0)  34.6 us
    pallas_call x6, Pallas kernels, call(): pl.pallas_call(kernel, out_shape=[jax.ShapeDtypeStruct(shape, dtype) for...  8.14 us

profile of v9, /device:TPU:1, one launch (start us, length us, event | category | flops | bytes accessed | tf_op | source)
XLA Modules:
  0.0 107.1 jit_solution(9846792371817525805)
XLA Ops:
  0.6 2.1 %project_kernel.1 = (bf16[64,2,896]{2,1,0:T(2,128)(2,1)S(1)}, f32[640,384]{1,0:T(8,128)S(1)}, f32[8,384]{1,0:T(8,128)S(1)}, f32[24,128]{1,0:T(8,128)S(1)}, f32[1...) custom-call(s32[384]{0:T(512)} %crop_hbm.1, ...), custom_call_target="tpu_custom_call" | custom-call | tf_op jit(solution)/shard_map/project_kernel/pallas_call | solution.py:423
  2.8 19.6 %all_to_all.20.received = bf16[64,2,896]{2,1,0:T(2,128)(2,1)S(1)} all-to-all(bf16[64,2,896]{2,1,0:T(2,128)(2,1)S(1)} %get-tuple-element.19), channel_id=1, replica_groups=mesh['xlo'=2,'y'=4,'core'=2,'zhi'=8,'zlo'=2,'xhi'=2] {'zlo','xhi','xlo',..., dimensions={0} | all-to-all | bytes 458752 | tf_op jit(solution)/shard_map/all_to_all | solution.py:440
  22.4 0.7 collect_kernel.1
  23.1 34.6 %all-gather = bf16[3456,128]{1,0:T(8,128)(2,1)S(1)} all-gather(bf16[432,128]{1,0:T(8,128)(2,1)S(1)} %get-tuple-element.20), channel_id=2, replica_groups=mesh['xlo'=2,'y'=4,'core'=2,'zhi'=8,'zlo'=2,'xhi'=2] {'zhi'}, dimensions={0}, use_global_device_ids=true | all-gather | bytes 995328 | tf_op jit(solution)/shard_map/all_gather | solution.py:489
  57.7 1.7 %triangle_kernel.1 = (bf16[192,1024]{1,0:T(8,128)(2,1)S(1)}, bf16[192,1024]{1,0:T(8,128)(2,1)S(1)}, bf16[64,2,896]{2,1,0:T(2,128)(2,1)S(1)}) custom-call(bf16[8,432,128]{2,1,0:T(8,128)(2,1)S(1)} %bitcast.9, bf16[192,128]{1,0:T(8,128)(2,1)S(1)} %get-tuple-element.21.left, bf16[192,128]{1,0:T(8,128)(2,1)S(1)} %get-tuple-element.22.right), custom_call_target="tpu_custom_call" | custom-call | tf_op jit(solution)/shard_map/triangle_kernel/pallas_call | solution.py:423
  59.4 0.0 copy-start.1
  59.4 18.1 %all_to_all.21.received = bf16[64,2,896]{2,1,0:T(2,128)(2,1)S(1)} all-to-all(bf16[64,2,896]{2,1,0:T(2,128)(2,1)S(1)} %get-tuple-element.23), channel_id=1, replica_groups=mesh['xlo'=2,'y'=4,'core'=2,'zhi'=8,'zlo'=2,'xhi'=2] {'zlo','xhi','xlo',..., dimensions={0} | all-to-all | bytes 458752 | tf_op jit(solution)/shard_map/all_to_all | solution.py:440
  77.5 0.0 copy-done.1
  77.5 1.2 %output_kernel.1 = (bf16[12,24,128]{2,1,0:T(8,128)(2,1)}, bf16[128,384]{1,0:T(8,128)(2,1)S(1)}, bf16[64,2,640]{2,1,0:T(2,128)(2,1)S(1)}) custom-call(bf16[64,2,896]{2,1,0:T(2,128)(2,1)S(1)} %all_to_all.21.received, f32[640,384]{1,0:T(8,128)S(1)} %get-tuple-element.24.projected, f32[8,384]{1,0:T(8,128)S(1)} %get-tuple-element.25.inside, ...), custom_call_target="tpu_custom_call" | custom-call | tf_op jit(solution)/shard_map/output_kernel/pallas_call | solution.py:423
  78.7 12.9 %all_to_all.22.received = bf16[64,2,640]{2,1,0:T(2,128)(2,1)S(1)} all-to-all(bf16[64,2,640]{2,1,0:T(2,128)(2,1)S(1)} %get-tuple-element.30), channel_id=1, replica_groups=mesh['xlo'=2,'y'=4,'core'=2,'zhi'=8,'zlo'=2,'xhi'=2] {'zlo','xhi','xlo',..., dimensions={0} | all-to-all | bytes 327680 | tf_op jit(solution)/shard_map/all_to_all | solution.py:440
  91.6 1.2 %back_kernel.1 = bf16[64,2,640]{2,1,0:T(2,128)(2,1)S(1)} custom-call(bf16[64,2,640]{2,1,0:T(2,128)(2,1)S(1)} %all_to_all.22.received, bf16[192,1024]{1,0:T(8,128)(2,1)S(1)} %get-tuple-element.31.left_all, bf16[192,1024]{1,0:T(8,128)(2,1)S(1)} %get-tuple-element.32.right_all), custom_call_target="tpu_custom_call" | custom-call | tf_op jit(solution)/shard_map/back_kernel/pallas_call | solution.py:423
  92.8 0.0 copy-start
  92.8 13.0 %all_to_all.23.received = bf16[64,2,640]{2,1,0:T(2,128)(2,1)S(1)} all-to-all(bf16[64,2,640]{2,1,0:T(2,128)(2,1)S(1)} %back_kernel.1), channel_id=1, replica_groups=mesh['xlo'=2,'y'=4,'core'=2,'zhi'=8,'zlo'=2,'xhi'=2] {'zlo','xhi','xlo',..., dimensions={0} | all-to-all | bytes 327680 | tf_op jit(solution)/shard_map/all_to_all | solution.py:440
  105.8 0.0 copy-done
  105.8 1.3 %input_kernel.1 = bf16[12,24,128]{2,1,0:T(8,128)(2,1)} custom-call(bf16[64,2,640]{2,1,0:T(2,128)(2,1)S(1)} %all_to_all.23.received, f32[640,384]{1,0:T(8,128)S(1)} %get-tuple-element.24.projected, f32[8,384]{1,0:T(8,128)S(1)} %get-tuple-element.25.inside, f32[24,128]{1,0:T(8,128)S(1)} %get-tuple-element.26.vectors, ...), custom_call_target="tpu_custom_call" | custom-call | tf_op jit(solution)/shard_map/input_kernel/pallas_call | solution.py:423
Async XLA Ops:
  59.4 18.1 %copy-start.1 = (bf16[128,128]{1,0:T(8,128)(2,1)S(1)}, bf16[128,128]{1,0:T(8,128)(2,1)}, u32[]{:S(2)}) copy-start(bf16[128,128]{1,0:T(8,128)(2,1)} %weights.2) | copy-start | bytes 98308
  92.8 13.0 %copy-start = (bf16[128,640]{1,0:T(8,128)(2,1)S(1)}, bf16[128,640]{1,0:T(8,128)(2,1)}, u32[]{:S(2)}) copy-start(bf16[128,640]{1,0:T(8,128)(2,1)} %weights.3) | copy-start | bytes 491524

commit v10 on v9

--- a/solution.py
+++ b/solution.py
@@ -250,6 +250,13 @@
     return own
 
 
+def unpack_own(rows):
+    lane = lax.broadcasted_iota(jnp.int32, (6, 128), 1) % PAD
+    back = [pltpu.roll(rows[6 * g : 6 * g + 6], 128 - TI + (PAD - TI) * g, 1) for g in range(3)]
+    last = jnp.where(lane < 4, back[0], jnp.where(lane < 8, back[1], back[2]))
+    return jnp.concatenate([rows[:18], last], axis=0)
+
+
 def triangle_kernel(gathered, left, right, left_all, right_all, send, slots, ordered, folded):
     place = 2 * (lax.axis_index("zhi") % (Q // 2))
     spare = jnp.zeros((PAD - TI, 128), f32)
@@ -260,8 +267,8 @@
     tri = dot(left_all[...], right[...], ((0,), (0,)))
     mirror = dot(right_all[...], left[...], ((0,), (0,)))
     for q in range(Q):
-        folded[...] = unpack_rows(gathered[q, 2 * PACK :].astype(f32))
-        own_i = [folded[pl.ds(place + half, TK, stride=RF), :] for half in range(2)]
+        folded[:PACK, :] = gathered[q, 2 * PACK :].astype(f32)
+        own_i = [unpack_own(folded[pl.ds(place + half, TK, stride=RF), :]) for half in range(2)]
         pieces = []
         for e in range(E):
             pieces += [own_i[e // 2][e % 2 * TI : (e % 2 + 1) * TI], spare]

time: 107 us -> 107 us (level)
  no operation moved by 1% of the time
where the time goes in v10:
time: 107 us
  blocking collectives  98.2 us (92%)
  Pallas kernels  8.06 us (8%)
    all_to_all x4, blocking collectives, exchange(): return lax.all_to_all(messages, OWNERS, 0, 0, tiled=True)  63.6 us
    all_gather x1, blocking collectives, body(): lax.all_gather(gathered, 'zhi', axis=0)  34.6 us
    pallas_call x6, Pallas kernels, call(): pl.pallas_call(kernel, out_shape=[jax.ShapeDtypeStruct(shape, dtype) for...  8.06 us

profile of v10, /device:TPU:1, one launch (start us, length us, event | category | flops | bytes accessed | tf_op | source)
XLA Modules:
  0.0 107.0 jit_solution(11554517405408839245)
XLA Ops:
  0.6 2.1 %project_kernel.1 = (bf16[64,2,896]{2,1,0:T(2,128)(2,1)S(1)}, f32[640,384]{1,0:T(8,128)S(1)}, f32[8,384]{1,0:T(8,128)S(1)}, f32[24,128]{1,0:T(8,128)S(1)}, f32[1...) custom-call(s32[384]{0:T(512)} %crop_hbm.1, ...), custom_call_target="tpu_custom_call" | custom-call | tf_op jit(solution)/shard_map/project_kernel/pallas_call | solution.py:430
  2.8 19.6 %all_to_all.20.received = bf16[64,2,896]{2,1,0:T(2,128)(2,1)S(1)} all-to-all(bf16[64,2,896]{2,1,0:T(2,128)(2,1)S(1)} %get-tuple-element.19), channel_id=1, replica_groups=mesh['xlo'=2,'y'=4,'core'=2,'zhi'=8,'zlo'=2,'xhi'=2] {'zlo','xhi','xlo',..., dimensions={0} | all-to-all | bytes 458752 | tf_op jit(solution)/shard_map/all_to_all | solution.py:447
  22.4 0.7 collect_kernel.1
  23.1 34.6 %all-gather = bf16[3456,128]{1,0:T(8,128)(2,1)S(1)} all-gather(bf16[432,128]{1,0:T(8,128)(2,1)S(1)} %get-tuple-element.20), channel_id=2, replica_groups=mesh['xlo'=2,'y'=4,'core'=2,'zhi'=8,'zlo'=2,'xhi'=2] {'zhi'}, dimensions={0}, use_global_device_ids=true | all-gather | bytes 995328 | tf_op jit(solution)/shard_map/all_gather | solution.py:496
  57.7 1.6 %triangle_kernel.1 = (bf16[192,1024]{1,0:T(8,128)(2,1)S(1)}, bf16[192,1024]{1,0:T(8,128)(2,1)S(1)}, bf16[64,2,896]{2,1,0:T(2,128)(2,1)S(1)}) custom-call(bf16[8,432,128]{2,1,0:T(8,128)(2,1)S(1)} %bitcast.9, bf16[192,128]{1,0:T(8,128)(2,1)S(1)} %get-tuple-element.21.left, bf16[192,128]{1,0:T(8,128)(2,1)S(1)} %get-tuple-element.22.right), custom_call_target="tpu_custom_call" | custom-call | tf_op jit(solution)/shard_map/triangle_kernel/pallas_call | solution.py:430
  59.3 0.0 copy-start.1
  59.3 18.1 %all_to_all.21.received = bf16[64,2,896]{2,1,0:T(2,128)(2,1)S(1)} all-to-all(bf16[64,2,896]{2,1,0:T(2,128)(2,1)S(1)} %get-tuple-element.23), channel_id=1, replica_groups=mesh['xlo'=2,'y'=4,'core'=2,'zhi'=8,'zlo'=2,'xhi'=2] {'zlo','xhi','xlo',..., dimensions={0} | all-to-all | bytes 458752 | tf_op jit(solution)/shard_map/all_to_all | solution.py:447
  77.4 0.0 copy-done.1
  77.4 1.2 %output_kernel.1 = (bf16[12,24,128]{2,1,0:T(8,128)(2,1)}, bf16[128,384]{1,0:T(8,128)(2,1)S(1)}, bf16[64,2,640]{2,1,0:T(2,128)(2,1)S(1)}) custom-call(bf16[64,2,896]{2,1,0:T(2,128)(2,1)S(1)} %all_to_all.21.received, f32[640,384]{1,0:T(8,128)S(1)} %get-tuple-element.24.projected, f32[8,384]{1,0:T(8,128)S(1)} %get-tuple-element.25.inside, ...), custom_call_target="tpu_custom_call" | custom-call | tf_op jit(solution)/shard_map/output_kernel/pallas_call | solution.py:430
  78.6 12.9 %all_to_all.22.received = bf16[64,2,640]{2,1,0:T(2,128)(2,1)S(1)} all-to-all(bf16[64,2,640]{2,1,0:T(2,128)(2,1)S(1)} %get-tuple-element.30), channel_id=1, replica_groups=mesh['xlo'=2,'y'=4,'core'=2,'zhi'=8,'zlo'=2,'xhi'=2] {'zlo','xhi','xlo',..., dimensions={0} | all-to-all | bytes 327680 | tf_op jit(solution)/shard_map/all_to_all | solution.py:447
  91.5 1.2 %back_kernel.1 = bf16[64,2,640]{2,1,0:T(2,128)(2,1)S(1)} custom-call(bf16[64,2,640]{2,1,0:T(2,128)(2,1)S(1)} %all_to_all.22.received, bf16[192,1024]{1,0:T(8,128)(2,1)S(1)} %get-tuple-element.31.left_all, bf16[192,1024]{1,0:T(8,128)(2,1)S(1)} %get-tuple-element.32.right_all), custom_call_target="tpu_custom_call" | custom-call | tf_op jit(solution)/shard_map/back_kernel/pallas_call | solution.py:430
  92.7 0.0 copy-start
  92.7 13.0 %all_to_all.23.received = bf16[64,2,640]{2,1,0:T(2,128)(2,1)S(1)} all-to-all(bf16[64,2,640]{2,1,0:T(2,128)(2,1)S(1)} %back_kernel.1), channel_id=1, replica_groups=mesh['xlo'=2,'y'=4,'core'=2,'zhi'=8,'zlo'=2,'xhi'=2] {'zlo','xhi','xlo',..., dimensions={0} | all-to-all | bytes 327680 | tf_op jit(solution)/shard_map/all_to_all | solution.py:447
  105.7 0.0 copy-done
  105.7 1.3 %input_kernel.1 = bf16[12,24,128]{2,1,0:T(8,128)(2,1)} custom-call(bf16[64,2,640]{2,1,0:T(2,128)(2,1)S(1)} %all_to_all.23.received, f32[640,384]{1,0:T(8,128)S(1)} %get-tuple-element.24.projected, f32[8,384]{1,0:T(8,128)S(1)} %get-tuple-element.25.inside, f32[24,128]{1,0:T(8,128)S(1)} %get-tuple-element.26.vectors, ...), custom_call_target="tpu_custom_call" | custom-call | tf_op jit(solution)/shard_map/input_kernel/pallas_call | solution.py:430
Async XLA Ops:
  59.3 18.1 %copy-start.1 = (bf16[128,128]{1,0:T(8,128)(2,1)S(1)}, bf16[128,128]{1,0:T(8,128)(2,1)}, u32[]{:S(2)}) copy-start(bf16[128,128]{1,0:T(8,128)(2,1)} %weights.2) | copy-start | bytes 98308
  92.7 13.0 %copy-start = (bf16[128,640]{1,0:T(8,128)(2,1)S(1)}, bf16[128,640]{1,0:T(8,128)(2,1)}, u32[]{:S(2)}) copy-start(bf16[128,640]{1,0:T(8,128)(2,1)} %weights.3) | copy-start | bytes 491524
